TPU v7x, 512 devices: a whole 4x4x16 slice. The times are simulated.
512 devices in a mesh: dp: 512 (over y, z, x, core).
Axes of the slice: x: 4, y: 4, z: 16, core: 2. Of those that a mesh axis runs over, the one named last changes fastest.
Arguments:
- img_feat: bfloat16 [131072, 1152], P('dp'), may hold values from -6 to 6
- head_weight: bfloat16 [1152, 640], replicated, may hold values from -0.1875 to 0.1875
- txt_emb: bfloat16 [131072, 640], P('dp'), may hold values from -6 to 6
- labels: int32 [131072], P('dp'), may hold values from 0 to 63
- log_logit_scale: float32 [1], replicated, may hold values from 0 to 1.5
- bias: float32 [1], replicated, may hold values from -3 to -1
Outputs:
- d_img_feat: bfloat16 [131072, 1152], P('dp')
- d_txt_emb: bfloat16 [131072, 640], P('dp')
- d_head: bfloat16 [1152, 640], replicated
All inputs are finite; a program needn't handle non-finite values.
Results may differ from a plain program's by a relative error of at most 0.0065.
Values may be sent and summed in bfloat16 or wider, within the bound.
No kernel may reach another device: no remote copies, remote signals or barrier semaphores. Data moves between devices by JAX's collectives and lax.ppermute only.
A program may use at most 64 MiB of HBM per device.

v0:
```python
import jax
import jax.numpy as jnp
from jax import lax
from jax.sharding import PartitionSpec as P


def partner(value, axis, bit):
    mask = 2**bit
    pairs = [(source, source ^ mask) for source in range(lax.axis_size(axis))]
    return lax.ppermute(value, axis, pairs)


def score_gradient(
    image_unit_rows, partner_captions, label_sign_value, logit_scale_value, logit_bias_value
):
    pair_logits = (
        logit_scale_value
        * lax.dot_general(
            image_unit_rows,
            partner_captions,
            (((1,), (1,)), ((), ())),
            preferred_element_type=jnp.float32,
        )
        + logit_bias_value
    )
    return (-label_sign_value * jax.nn.sigmoid(-label_sign_value * pair_logits)).astype(
        jnp.bfloat16
    )


def logit_block(
    image_unit_rows, partner_captions, label_sign_value, logit_scale_value, logit_bias_value
):
    block_gradient = score_gradient(
        image_unit_rows, partner_captions, label_sign_value, logit_scale_value, logit_bias_value
    )
    image_gradient = logit_scale_value * jnp.dot(
        block_gradient, partner_captions, preferred_element_type=jnp.float32
    )
    partner_gradient = logit_scale_value * lax.dot_general(
        block_gradient,
        image_unit_rows,
        (((0,), (0,)), ((), ())),
        preferred_element_type=jnp.float32,
    )
    return (image_gradient, partner_gradient)


def fetch_text(block, round_index):
    for bit_index in range(round_index + 1):
        block = partner(block, "dp", bit_index)
    return block


def return_grads(block, round_index):
    for bit_index in range(round_index + 1):
        block = partner(block, "dp", bit_index)
    return block


def per_device(img_feat, head_weight, txt_emb, labels, log_logit_scale, bias):
    proj = jnp.dot(img_feat, head_weight, preferred_element_type=jnp.float32)
    inv_img = lax.rsqrt(jnp.sum(proj * proj, axis=-1, keepdims=True) + 1e-06)
    unit_img = proj * inv_img
    image_unit_rows = unit_img.astype(jnp.bfloat16)
    txt_float = txt_emb.astype(jnp.float32)
    inv_txt = lax.rsqrt(jnp.sum(txt_float * txt_float, axis=-1, keepdims=True) + 1e-06)
    unit_txt = txt_float * inv_txt
    text_unit_rows = unit_txt.astype(jnp.bfloat16)
    logit_scale_value = jnp.exp(log_logit_scale[0])
    logit_bias_value = bias[0]
    local_sign = jnp.where(labels[:, None] == labels[None, :], 1.0, -1.0).astype(jnp.float32)
    partner_sign = -jnp.ones_like(local_sign)
    unit_image_gradient, unit_text_gradient = logit_block(
        image_unit_rows, text_unit_rows, local_sign, logit_scale_value, logit_bias_value
    )
    for round_index in range(4):
        partner_captions = fetch_text(text_unit_rows, round_index)
        image_gradient, partner_gradient = logit_block(
            image_unit_rows, partner_captions, partner_sign, logit_scale_value, logit_bias_value
        )
        unit_image_gradient = unit_image_gradient + image_gradient
        unit_text_gradient = unit_text_gradient + return_grads(partner_gradient, round_index)
    d_proj = (
        (
            unit_image_gradient
            - unit_img * jnp.sum(unit_img * unit_image_gradient, axis=-1, keepdims=True)
        )
        * inv_img
    ).astype(jnp.bfloat16)
    head_terms = lax.dot_general(
        img_feat, d_proj, (((0,), (0,)), ((), ())), preferred_element_type=jnp.float32
    )
    d_head = lax.psum(head_terms, "dp").astype(jnp.bfloat16)
    d_img_feat = lax.dot_general(
        d_proj, head_weight, (((1,), (1,)), ((), ())), preferred_element_type=jnp.float32
    ).astype(jnp.bfloat16)
    d_txt_emb = (
        (
            unit_text_gradient
            - unit_txt * jnp.sum(unit_txt * unit_text_gradient, axis=-1, keepdims=True)
        )
        * inv_txt
    ).astype(jnp.bfloat16)
    return (d_img_feat, d_txt_emb, d_head)


def solution(mesh):
    return jax.shard_map(
        per_device,
        mesh=mesh,
        in_specs=(P("dp", None), P(), P("dp", None), P("dp"), P(), P()),
        out_specs=(P("dp", None), P("dp", None), P()),
        check_vma=False,
    )
```

profile of v0, /device:TPU:1, one launch (start us, length us, event | category | flops | bytes accessed | tf_op | source)
XLA Modules:
  0.0 308.5 jit_solution(3868976381010972198)
XLA Ops:
  3.0 8.8 %collective-permute-start = (bf16[256,640]{1,0:T(8,128)(2,1)S(1)}, bf16[256,640]{1,0:T(8,128)(2,1)S(1)}, u32[]{:S(2)}, u32[]{:S(2)}) collective-permute-start(bf16[256,640]{1,0:T(8,128)(2,1)S(1)} %fusion.39), channel_id=1, source_target_pairs={{0,1},{1,0},{2,3},{3,2},{4,5},{5,4},{6,7},{7,6},{8,9},{9,8},{10,11... | collective-permute-start | bytes 983048 | tf_op jit(solution)/shard_map/ppermute | solution.py:10
  13.6 1.9 collective-permute-start.1
  17.4 7.5 %collective-permute-done.1 = bf16[256,640]{1,0:T(8,128)(2,1)S(1)} collective-permute-done((bf16[256,640]{1,0:T(8,128)(2,1)S(1)}, bf16[256,640]{1,0:T(8,128)(2,1)S(1)}, u32[]{:S(2)}, u32[]{:S(2)}) %collective-permute-start.1) | collective-permute-done | bytes 327712 | tf_op jit(solution)/shard_map/ppermute | solution.py:10
  24.9 1.9 collective-permute-start.2
  27.4 9.3 %collective-permute-done.2 = bf16[256,640]{1,0:T(8,128)(2,1)S(1)} collective-permute-done((bf16[256,640]{1,0:T(8,128)(2,1)S(1)}, bf16[256,640]{1,0:T(8,128)(2,1)S(1)}, u32[]{:S(2)}, u32[]{:S(2)}) %collective-permute-start.2) | collective-permute-done | bytes 327712 | tf_op jit(solution)/shard_map/ppermute | solution.py:10
  39.8 3.6 %collective-permute-start.4 = (f32[256,640]{1,0:T(8,128)}, f32[256,640]{1,0:T(8,128)}, u32[]{:S(2)}, u32[]{:S(2)}) collective-permute-start(f32[256,640]{1,0:T(8,128)} %convolution_multiply_fusion.3), channel_id=1, source_target_pairs={{0,1},{1,0},{2,3},{3,2},{4,5},{5,4},{6,7},{7,6},{8,9},{9,8},{10,11... | collective-permute-start | bytes 1966088 | tf_op jit(solution)/shard_map/ppermute | solution.py:10
  43.6 2.5 collective-permute-done.3
  46.7 4.5 %collective-permute-start.10 = (f32[256,640]{1,0:T(8,128)S(1)}, f32[256,640]{1,0:T(8,128)S(1)}, u32[]{:S(2)}, u32[]{:S(2)}) collective-permute-start(f32[256,640]{1,0:T(8,128)S(1)} %convolution_multiply_fusion), channel_id=1, source_target_pairs={{0,1},{1,0},{2,3},{3,2},{4,5},{5,4},{6,7},{7,6},{8,9},{9,8},{10,11... | collective-permute-start | bytes 1966088 | tf_op jit(solution)/shard_map/ppermute | solution.py:10
  52.2 1.9 collective-permute-start.7
  54.2 2.4 collective-permute-start.11
  56.8 2.7 collective-permute-start.5
  60.1 3.1 collective-permute-start.8
  63.2 8.7 %collective-permute-done.11 = f32[256,640]{1,0:T(8,128)S(1)} collective-permute-done((f32[256,640]{1,0:T(8,128)S(1)}, f32[256,640]{1,0:T(8,128)S(1)}, u32[]{:S(2)}, u32[]{:S(2)}) %collective-permute-start.11) | collective-permute-done | bytes 655392 | tf_op jit(solution)/shard_map/ppermute | solution.py:10
  71.8 2.2 collective-permute-start.12
  74.7 2.2 convolution_bitcast_fusion
  76.9 2.3 collective-permute-start.6
  79.3 6.7 %collective-permute-done.8 = f32[256,640]{1,0:T(8,128)} collective-permute-done((f32[256,640]{1,0:T(8,128)S(1)}, f32[256,640]{1,0:T(8,128)}, u32[]{:S(2)}, u32[]{:S(2)}) %collective-permute-start.8) | collective-permute-done | bytes 655392 | tf_op jit(solution)/shard_map/ppermute | solution.py:10
  86.0 2.2 collective-permute-start.9
  88.2 11.7 %collective-permute-done.12 = f32[256,640]{1,0:T(8,128)} collective-permute-done((f32[256,640]{1,0:T(8,128)S(1)}, f32[256,640]{1,0:T(8,128)}, u32[]{:S(2)}, u32[]{:S(2)}) %collective-permute-start.12) | collective-permute-done | bytes 655392 | tf_op jit(solution)/shard_map/ppermute | solution.py:10
  100.0 1.9 collective-permute-start.13
  101.9 198.9 %all-reduce.1 = bf16[1152,640]{0,1:T(8,128)(2,1)S(1)} all-reduce(f32[1152,640]{0,1:T(8,128)} %convolution_bitcast_fusion), channel_id=1, replica_groups=mesh['dp'=512] {'dp'}, use_global_device_ids=true, to_apply=%region_4.5 | all-reduce | flops 737280 | bytes 4423680 | tf_op jit(solution)/shard_map/psum | solution.py:94
  300.8 2.1 copy.9
  302.9 2.5 convolution_convert_fusion
  305.4 2.1 fusion.40
  (41 shorter events, 12.4 us)
Async XLA Ops:
  0.6 11.2 %copy-start = (bf16[1152,640]{1,0:T(8,128)(2,1)S(1)}, bf16[1152,640]{1,0:T(8,128)(2,1)}, u32[]{:S(2)}) copy-start(bf16[1152,640]{1,0:T(8,128)(2,1)} %param.7) | copy-start | bytes 4423684
  3.0 14.0 %copy-start.4 = (s32[256]{0:T(256)S(1)}, s32[256]{0:T(256)}, u32[]{:S(2)}) copy-start(s32[256]{0:T(256)} %param.9) | copy-start | bytes 3076
  3.0 10.6 %collective-permute-start = (bf16[256,640]{1,0:T(8,128)(2,1)S(1)}, bf16[256,640]{1,0:T(8,128)(2,1)S(1)}, u32[]{:S(2)}, u32[]{:S(2)}) collective-permute-start(bf16[256,640]{1,0:T(8,128)(2,1)S(1)} %fusion.39), channel_id=1, source_target_pairs={{0,1},{1,0},{2,3},{3,2},{4,5},{5,4},{6,7},{7,6},{8,9},{9,8},{10,11... | collective-permute-start | bytes 983048 | tf_op jit(solution)/shard_map/ppermute | solution.py:10
  13.6 11.2 %collective-permute-start.1 = (bf16[256,640]{1,0:T(8,128)(2,1)S(1)}, bf16[256,640]{1,0:T(8,128)(2,1)S(1)}, u32[]{:S(2)}, u32[]{:S(2)}) collective-permute-start(bf16[256,640]{1,0:T(8,128)(2,1)S(1)} %collective-permute-done), channel_id=1, source_target_pairs={{0,2},{1,3},{2,0},{3,1},{4,6},{5,7},{6,4},{7,5},{8,10},{9,11},{10,... | collective-permute-start | bytes 983048 | tf_op jit(solution)/shard_map/ppermute | solution.py:10
  24.9 11.8 %collective-permute-start.2 = (bf16[256,640]{1,0:T(8,128)(2,1)S(1)}, bf16[256,640]{1,0:T(8,128)(2,1)S(1)}, u32[]{:S(2)}, u32[]{:S(2)}) collective-permute-start(bf16[256,640]{1,0:T(8,128)(2,1)S(1)} %collective-permute-done.1), channel_id=1, source_target_pairs={{0,4},{1,5},{2,6},{3,7},{4,0},{5,1},{6,2},{7,3},{8,12},{9,13},{10,... | collective-permute-start | bytes 983048 | tf_op jit(solution)/shard_map/ppermute | solution.py:10
  36.7 9.4 %collective-permute-start.3 = (bf16[256,640]{1,0:T(8,128)(2,1)S(1)}, bf16[256,640]{1,0:T(8,128)(2,1)S(1)}, u32[]{:S(2)}, u32[]{:S(2)}) collective-permute-start(bf16[256,640]{1,0:T(8,128)(2,1)S(1)} %collective-permute-done.2), channel_id=1, source_target_pairs={{0,8},{1,9},{2,10},{3,11},{4,12},{5,13},{6,14},{7,15},{8,0},{9,1},... | collective-permute-start | bytes 983048 | tf_op jit(solution)/shard_map/ppermute | solution.py:10
  39.8 265.7 %collective-permute-start.4 = (f32[256,640]{1,0:T(8,128)}, f32[256,640]{1,0:T(8,128)}, u32[]{:S(2)}, u32[]{:S(2)}) collective-permute-start(f32[256,640]{1,0:T(8,128)} %convolution_multiply_fusion.3), channel_id=1, source_target_pairs={{0,1},{1,0},{2,3},{3,2},{4,5},{5,4},{6,7},{7,6},{8,9},{9,8},{10,11... | collective-permute-start | bytes 1966088 | tf_op jit(solution)/shard_map/ppermute | solution.py:10
  46.7 7.4 %collective-permute-start.10 = (f32[256,640]{1,0:T(8,128)S(1)}, f32[256,640]{1,0:T(8,128)S(1)}, u32[]{:S(2)}, u32[]{:S(2)}) collective-permute-start(f32[256,640]{1,0:T(8,128)S(1)} %convolution_multiply_fusion), channel_id=1, source_target_pairs={{0,1},{1,0},{2,3},{3,2},{4,5},{5,4},{6,7},{7,6},{8,9},{9,8},{10,11... | collective-permute-start | bytes 1966088 | tf_op jit(solution)/shard_map/ppermute | solution.py:10
  52.2 7.9 %collective-permute-start.7 = (f32[256,640]{1,0:T(8,128)S(1)}, f32[256,640]{1,0:T(8,128)S(1)}, u32[]{:S(2)}, u32[]{:S(2)}) collective-permute-start(f32[256,640]{1,0:T(8,128)S(1)} %convolution_multiply_fusion.1), channel_id=1, source_target_pairs={{0,1},{1,0},{2,3},{3,2},{4,5},{5,4},{6,7},{7,6},{8,9},{9,8},{10,11... | collective-permute-start | bytes 1966088 | tf_op jit(solution)/shard_map/ppermute | solution.py:10
  54.2 17.7 %collective-permute-start.11 = (f32[256,640]{1,0:T(8,128)S(1)}, f32[256,640]{1,0:T(8,128)S(1)}, u32[]{:S(2)}, u32[]{:S(2)}) collective-permute-start(f32[256,640]{1,0:T(8,128)S(1)} %collective-permute-done.10), channel_id=1, source_target_pairs={{0,2},{1,3},{2,0},{3,1},{4,6},{5,7},{6,4},{7,5},{8,10},{9,11},{10,... | collective-permute-start | bytes 1966088 | tf_op jit(solution)/shard_map/ppermute | solution.py:10
  56.8 20.1 %collective-permute-start.5 = (f32[256,640]{1,0:T(8,128)S(1)}, f32[256,640]{1,0:T(8,128)}, u32[]{:S(2)}, u32[]{:S(2)}) collective-permute-start(f32[256,640]{1,0:T(8,128)S(1)} %convolution_multiply_fusion.2), channel_id=1, source_target_pairs={{0,1},{1,0},{2,3},{3,2},{4,5},{5,4},{6,7},{7,6},{8,9},{9,8},{10,11... | collective-permute-start | bytes 1966088 | tf_op jit(solution)/shard_map/ppermute | solution.py:10
  60.1 14.6 %copy-start.3 = (bf16[256,1152]{1,0:T(8,128)(2,1)S(1)}, bf16[256,1152]{1,0:T(8,128)(2,1)}, u32[]{:S(2)}) copy-start(bf16[256,1152]{1,0:T(8,128)(2,1)} %param.6) | copy-start | bytes 1769476
  60.1 25.9 %collective-permute-start.8 = (f32[256,640]{1,0:T(8,128)S(1)}, f32[256,640]{1,0:T(8,128)}, u32[]{:S(2)}, u32[]{:S(2)}) collective-permute-start(f32[256,640]{1,0:T(8,128)S(1)} %collective-permute-done.7), channel_id=1, source_target_pairs={{0,2},{1,3},{2,0},{3,1},{4,6},{5,7},{6,4},{7,5},{8,10},{9,11},{10,... | collective-permute-start | bytes 1966088 | tf_op jit(solution)/shard_map/ppermute | solution.py:10
  71.8 28.1 %collective-permute-start.12 = (f32[256,640]{1,0:T(8,128)S(1)}, f32[256,640]{1,0:T(8,128)}, u32[]{:S(2)}, u32[]{:S(2)}) collective-permute-start(f32[256,640]{1,0:T(8,128)S(1)} %collective-permute-done.11), channel_id=1, source_target_pairs={{0,4},{1,5},{2,6},{3,7},{4,0},{5,1},{6,2},{7,3},{8,12},{9,13},{10,... | collective-permute-start | bytes 1966088 | tf_op jit(solution)/shard_map/ppermute | solution.py:10
  74.7 2.3 copy-start.2
  76.9 228.5 %collective-permute-start.6 = (f32[256,640]{1,0:T(8,128)}, f32[256,640]{1,0:T(8,128)}, u32[]{:S(2)}, u32[]{:S(2)}) collective-permute-start(f32[256,640]{1,0:T(8,128)} %collective-permute-done.5), channel_id=1, source_target_pairs={{0,2},{1,3},{2,0},{3,1},{4,6},{5,7},{6,4},{7,5},{8,10},{9,11},{10,... | collective-permute-start | bytes 1966088 | tf_op jit(solution)/shard_map/ppermute | solution.py:10
  86.0 219.4 %collective-permute-start.9 = (f32[256,640]{1,0:T(8,128)}, f32[256,640]{1,0:T(8,128)}, u32[]{:S(2)}, u32[]{:S(2)}) collective-permute-start(f32[256,640]{1,0:T(8,128)} %collective-permute-done.8), channel_id=1, source_target_pairs={{0,4},{1,5},{2,6},{3,7},{4,0},{5,1},{6,2},{7,3},{8,12},{9,13},{10,... | collective-permute-start | bytes 1966088 | tf_op jit(solution)/shard_map/ppermute | solution.py:10
  100.0 205.5 %collective-permute-start.13 = (f32[256,640]{1,0:T(8,128)}, f32[256,640]{1,0:T(8,128)}, u32[]{:S(2)}, u32[]{:S(2)}) collective-permute-start(f32[256,640]{1,0:T(8,128)} %collective-permute-done.12), channel_id=1, source_target_pairs={{0,8},{1,9},{2,10},{3,11},{4,12},{5,13},{6,14},{7,15},{8,0},{9,1},... | collective-permute-start | bytes 1966088 | tf_op jit(solution)/shard_map/ppermute | solution.py:10
  302.9 2.5 copy-start.1
where the time goes:
time: 310 us; the launch traced here: 309 us
  blocking collectives  199 us (64%)
  waiting for transfers between devices  46.4 us (15%)
  starting transfers between devices  41.4 us (13%)
  matrix products  13.8 us (4%)
  other arithmetic  3.55 us (1%)
    psum x1, blocking collectives, per_device(): d_head = lax.psum(head_terms, 'dp').astype(jnp.bfloat16)  199 us
    ppermute x14, waiting for transfers between devices, partner(): return lax.ppermute(value, axis, pairs)  46.4 us
    ppermute x14, starting transfers between devices, partner(): return lax.ppermute(value, axis, pairs)  41.4 us
  transfers between devices with their start and end apart: 14, of which 6 were waited for; matrix products, arithmetic and copies ran while one was open for 5% of the time, Pallas kernels for 0%

commit v1 on v0

v1 whole, which is shorter than its diff:
```python
import jax
import jax.numpy as jnp
from jax import lax
from jax.experimental import pallas as pl
from jax.experimental.pallas import tpu as pltpu
from jax.sharding import PartitionSpec as P

ROUNDS = (1, 3, 7, 15)
F32 = jnp.float32
BF16 = jnp.bfloat16


def swap(value, mask):
    pairs = [(source, source ^ mask) for source in range(lax.axis_size("dp"))]
    return lax.ppermute(value, "dp", pairs)


def after(value, *others):
    return lax.optimization_barrier((value,) + others)[0]


def rows_dot(left, right):
    return lax.dot_general(left, right, (((1,), (1,)), ((), ())), preferred_element_type=F32)


def part(value, start, size):
    return lax.dynamic_slice_in_dim(value, start, size, 0)


def head_kernel(label_ref, feat_ref, d_proj_ref, sent_ref, kept_ref):
    label = label_ref[0]
    for b in range(9):
        product = lax.dot_general(
            feat_ref[:, 128 * b : 128 * b + 128],
            d_proj_ref[...],
            (((0,), (0,)), ((), ())),
            preferred_element_type=F32,
        )
        for a in range(8):
            slab = product[16 * a : 16 * a + 16]
            chunk = label ^ a

            @pl.when(chunk >= 4)
            def _():
                sent_ref[chunk - 4, b] = slab.astype(BF16)

            @pl.when(chunk < 4)
            def _():
                kept_ref[chunk, b] = slab


def head_terms(label, feat, d_proj):
    return pl.pallas_call(
        head_kernel,
        out_shape=(
            jax.ShapeDtypeStruct((4, 9, 16, 640), BF16),
            jax.ShapeDtypeStruct((4, 9, 16, 640), F32),
        ),
        in_specs=[
            pl.BlockSpec(memory_space=pltpu.SMEM),
            pl.BlockSpec(memory_space=pltpu.VMEM),
            pl.BlockSpec(memory_space=pltpu.VMEM),
        ],
        out_specs=(
            pl.BlockSpec(memory_space=pltpu.VMEM),
            pl.BlockSpec(memory_space=pltpu.VMEM),
        ),
        compiler_params=pltpu.CompilerParams(vmem_limit_bytes=32 << 20),
        cost_estimate=pl.CostEstimate(flops=377487360, bytes_accessed=4000000, transcendentals=0),
    )(label, feat, d_proj)


def place_kernel(label_ref, mine_ref, other_ref, out_ref, sems):
    label = label_ref[0]
    copies = []
    for k in range(8):
        source = mine_ref.at[k] if k < 4 else other_ref.at[k - 4]
        copies.append(pltpu.make_async_copy(source, out_ref.at[:, label ^ k], sems.at[k]))
    for copy in copies:
        copy.start()
    for copy in copies:
        copy.wait()


def place(label, mine, other):
    return pl.pallas_call(
        place_kernel,
        out_shape=jax.ShapeDtypeStruct((9, 8, 16, 640), BF16),
        in_specs=[
            pl.BlockSpec(memory_space=pltpu.SMEM),
            pl.BlockSpec(memory_space=pl.ANY),
            pl.BlockSpec(memory_space=pl.ANY),
        ],
        out_specs=pl.BlockSpec(memory_space=pl.ANY),
        scratch_shapes=[pltpu.SemaphoreType.DMA((8,))],
        cost_estimate=pl.CostEstimate(flops=0, bytes_accessed=3000000, transcendentals=0),
    )(label, mine, other)


def halve(kept, sent, mask):
    total = kept + swap(sent, mask).astype(F32)
    half = total.shape[0] // 2
    return total[:half], total[half:].astype(BF16)


def join(mine, mask):
    return jnp.concatenate([mine, swap(mine, mask)], axis=0)


def join_in_order(mine, mask, bit, overlap=0):
    other = swap(mine, mask)
    low = jnp.concatenate([mine, other[overlap:]], axis=0)
    high = jnp.concatenate([other, mine[overlap:]], axis=0)
    return jnp.where(bit == 1, high, low)


def per_device(img_feat, head_weight, txt_emb, labels, log_logit_scale, bias):
    index = lax.axis_index("dp")
    bits = [(index >> k) & 1 for k in range(9)]

    txt_float = txt_emb.astype(F32)
    inv_txt = lax.rsqrt(jnp.sum(txt_float * txt_float, axis=-1, keepdims=True) + 1e-06)
    unit_txt = txt_float * inv_txt
    txt_rows = unit_txt.astype(BF16)
    captions = {c: swap(txt_rows, c) for c in reversed(ROUNDS)}

    proj = jnp.dot(img_feat, head_weight, preferred_element_type=F32)
    inv_img = lax.rsqrt(jnp.sum(proj * proj, axis=-1, keepdims=True) + 1e-06)
    unit_img = proj * inv_img
    img_rows = unit_img.astype(BF16)
    scale = jnp.exp(log_logit_scale[0])
    shift = bias[0]

    sign = jnp.where(labels[:, None] == labels[None, :], 1.0, -1.0).astype(F32)
    logits = scale * rows_dot(img_rows, txt_rows) + shift
    grad = (-sign * jax.nn.sigmoid(-sign * logits)).astype(BF16)
    d_unit_img = jnp.dot(grad, txt_rows, preferred_element_type=F32)
    for c in ROUNDS:
        logits = scale * rows_dot(img_rows, captions[c]) + shift
        grad_c = jax.nn.sigmoid(logits).astype(BF16)
        d_unit_img = d_unit_img + jnp.dot(grad_c, captions[c], preferred_element_type=F32)
    d_unit_img = scale * d_unit_img
    d_proj = (
        (d_unit_img - unit_img * jnp.sum(unit_img * d_unit_img, axis=-1, keepdims=True)) * inv_img
    ).astype(BF16)

    x_low, x_high = bits[1] ^ bits[2], bits[2]
    y_low, y_high = bits[7] ^ bits[8], bits[8]
    label = (bits[0] * 4 + x_low * 2 + x_high)[None]
    sent, kept = head_terms(label, img_feat, d_proj)
    kept, sent = halve(kept, sent, 1)
    kept, sent = halve(kept, sent, 2)
    total = (kept + swap(sent, 6).astype(F32)).reshape(144, 640)
    sent = part(total, (1 - y_low) * 72, 72).astype(BF16)
    total = part(total, y_low * 72, 72) + swap(sent, 128).astype(F32)
    img_late = after(img_rows, total)
    images = {c: swap(img_late, c) for c in ROUNDS}
    sent = part(total, (1 - y_high) * 32, 40).astype(BF16)
    total = part(total, y_high * 32, 40) + swap(sent, 384).astype(F32)
    for z in (1, 2, 4, 15):
        mine = total.astype(BF16)
        total = mine.astype(F32) + swap(mine, z * 8).astype(F32)
    piece = join_in_order(total.astype(BF16), 384, y_high, 8)
    piece = join_in_order(piece, 128, y_low).reshape(1, 9, 16, 640)
    piece = after(piece, *images.values())
    piece = join(piece, 6)
    piece = join(piece, 2)
    d_head = place(label, piece, swap(piece, 1)).reshape(1152, 640)

    d_img_feat = rows_dot(d_proj, head_weight).astype(BF16)

    d_unit_txt = lax.dot_general(grad, img_rows, (((0,), (0,)), ((), ())), preferred_element_type=F32)
    for c in ROUNDS:
        logits = scale * rows_dot(txt_rows, images[c]) + shift
        grad_c = jax.nn.sigmoid(logits).astype(BF16)
        d_unit_txt = d_unit_txt + jnp.dot(grad_c, images[c], preferred_element_type=F32)
    d_unit_txt = scale * d_unit_txt
    d_txt_emb = (
        (d_unit_txt - unit_txt * jnp.sum(unit_txt * d_unit_txt, axis=-1, keepdims=True)) * inv_txt
    ).astype(BF16)
    return (d_img_feat, d_txt_emb, d_head)


def solution(mesh):
    return jax.shard_map(
        per_device,
        mesh=mesh,
        in_specs=(P("dp", None), P(), P("dp", None), P("dp"), P(), P()),
        out_specs=(P("dp", None), P("dp", None), P()),
        check_vma=False,
    )
```

time: 310 us -> 224 us (0.72)
  blocking collectives: 199 us -> 0 us
  Pallas kernels: 0 us -> 48.6 us
  starting transfers between devices: 41.4 us -> 87.8 us
  matrix products: 13.8 us -> 27.1 us
    psum x1 -> x0, blocking collectives: 199 us -> none  [per_device(): d_head = lax.psum(head_terms, 'dp').astype(jnp.bfloat16)]
    pallas_call x0 -> x2, Pallas kernels: none -> 48.6 us  [the longest x1 45.8 us: place(): pl.pallas_call(place_kernel, out_shape=jax.ShapeDtypeStruct((9, 8, 16, 64...]
    ppermute x14 -> x22, starting transfers between devices: 41.4 us -> 87.8 us  [swap(): return lax.ppermute(value, 'dp', pairs)]
    dot_general x18 -> x13, matrix products: 13.8 us -> 27.1 us  [the longest x4 11 us: per_device(): jnp.dot(grad_c, captions[c], preferred_element_type=F32)]
    ppermute x14 -> x22, waiting for transfers between devices: 46.4 us -> 46.8 us  [swap(): return lax.ppermute(value, 'dp', pairs)]
  transfers between devices with their start and end apart: 14 -> 22, of which waited for: 6 -> 14; matrix products, arithmetic and copies ran while one was open for 5% -> 12% of each run, Pallas kernels for 0% -> 0%
where the time goes in v1:
time: 224 us; the launch traced here: 223 us
  starting transfers between devices  87.8 us (39%)
  Pallas kernels  48.6 us (22%)
  waiting for transfers between devices  46.8 us (21%)
  matrix products  27.1 us (12%)
  other arithmetic  6.11 us (3%)
  local copies, waits for them, and re-layouts  4.34 us (2%)
  between operations  2.47 us (1%)
    ppermute x22, starting transfers between devices, swap(): return lax.ppermute(value, 'dp', pairs)  87.8 us
    ppermute x22, waiting for transfers between devices, swap(): return lax.ppermute(value, 'dp', pairs)  46.8 us
    pallas_call x1, Pallas kernels, place(): pl.pallas_call(place_kernel, out_shape=jax.ShapeDtypeStruct((9, 8, 16, 64...  45.8 us
    dot_general x4, matrix products, per_device(): jnp.dot(grad_c, captions[c], preferred_element_type=F32)  11 us
    dot_general x4, matrix products, per_device(): jnp.dot(grad_c, images[c], preferred_element_type=F32)  9.99 us
  transfers between devices with their start and end apart: 22, of which 14 were waited for; matrix products, arithmetic and copies ran while one was open for 12% of the time, Pallas kernels for 0%

profile of v1, /device:TPU:1, one launch (start us, length us, event | category | flops | bytes accessed | tf_op | source)
XLA Modules:
  0.0 223.1 jit_solution(7784070164304483943)
XLA Ops:
  3.0 7.3 %collective-permute-start.3 = (bf16[256,640]{1,0:T(8,128)(2,1)S(1)}, bf16[256,640]{1,0:T(8,128)(2,1)}, u32[]{:S(2)}, u32[]{:S(2)}) collective-permute-start(bf16[256,640]{1,0:T(8,128)(2,1)S(1)} %fusion.68), channel_id=1, source_target_pairs={{0,15},{1,14},{2,13},{3,12},{4,11},{5,10},{6,9},{7,8},{8,7},{9,6},... | collective-permute-start | bytes 983048 | tf_op jit(solution)/shard_map/ppermute | solution.py:15
  12.2 3.6 %collective-permute-start = (bf16[256,640]{1,0:T(8,128)(2,1)S(1)}, bf16[256,640]{1,0:T(8,128)(2,1)}, u32[]{:S(2)}, u32[]{:S(2)}) collective-permute-start(bf16[256,640]{1,0:T(8,128)(2,1)S(1)} %fusion.68), channel_id=1, source_target_pairs={{0,1},{1,0},{2,3},{3,2},{4,5},{5,4},{6,7},{7,6},{8,9},{9,8},{10,11... | collective-permute-start | bytes 983048 | tf_op jit(solution)/shard_map/ppermute | solution.py:15
  29.8 2.8 %convolution_add_fusion.3 = f32[256,640]{1,0:T(8,128)} fusion(f32[256,640]{1,0:T(8,128)} %fusion.114, bf16[256,640]{1,0:T(8,128)(2,1)} %collective-permute-done, bf16[256,640]{1,0:T(8,128)(2,1)S(1)} %multiply_convert_fusion.1, f32[]{:T(128)} %bitcast.42, f32[]{:T(128)} %bitcast), kind=kOutput, calls=%fused_computation.11 | convolution fusion | flops 168329216 | bytes 1966088 | tf_op jit(solution)/shard_map/dot_general | solution.py:141
  32.6 3.0 %multiply_reduce_fusion = (f32[256]{0:T(256)S(1)}, f32[256,640]{1,0:T(8,128)}) fusion(f32[256,640]{1,0:T(8,128)S(1)} %get-tuple-element.12, f32[256]{0:T(256)S(1)} %add_rsqrt_fusion.1, f32[256,640]{1,0:T(8,128)} %fusion.64, f32[256,640]{1,0:T(8,128)} %fusion.65, f32[256,640]{1,0:T(8,128)} %convolution_add_fusion.3, ...), kind=kOutput, calls=%fused_computation.94 | convolution fusion | flops 169312000 | bytes 3934216 | tf_op jit(solution)/shard_map/dot_general | solution.py:141
  36.9 2.8 %shard_map.85 = (bf16[4,9,16,640]{3,2,1,0:T(8,128)(2,1)S(1)}, f32[4,9,16,640]{3,2,1,0:T(8,128)S(1)}) custom-call(s32[1]{0:T(128)} %bitcast.2.label_ref, bf16[256,1152]{1,0:T(8,128)(2,1)S(1)} %copy-done.1, bf16[256,640]{1,0:T(8,128)(2,1)S(1)} %multiply_convert_fusion.d_proj_ref), custom_call_target="tpu_custom_call" | custom-call | flops 377487360 | bytes 4000000 | tf_op jit(solution)/shard_map/pallas_call | solution.py:53
  46.1 9.7 %collective-permute-done.5 = bf16[2,9,16,640]{3,2,1,0:T(8,128)(2,1)S(1)} collective-permute-done((bf16[2,9,16,640]{3,2,1,0:T(8,128)(2,1)S(1)}, bf16[2,9,16,640]{3,2,1,0:T(8,128)(2,1)S(1)}, u32[]{:S(2)}, u32[]{:S(2)}) %collective-permute-start.5) | collective-permute-done | bytes 368672 | tf_op jit(solution)/shard_map/ppermute | solution.py:15
  56.6 3.8 %collective-permute-start.6 = (bf16[1,9,16,640]{3,2,1,0:T(8,128)(2,1)}, bf16[1,9,16,640]{3,2,1,0:T(8,128)(2,1)S(1)}, u32[]{:S(2)}, u32[]{:S(2)}) collective-permute-start(bf16[1,9,16,640]{3,2,1,0:T(8,128)(2,1)} %slice.37), channel_id=1, source_target_pairs={{0,6},{1,7},{2,4},{3,5},{4,2},{5,3},{6,0},{7,1},{8,14},{9,15},{10,... | collective-permute-start | bytes 552968 | tf_op jit(solution)/shard_map/ppermute | solution.py:15
  60.4 4.4 %collective-permute-done.6 = bf16[1,9,16,640]{3,2,1,0:T(8,128)(2,1)S(1)} collective-permute-done((bf16[1,9,16,640]{3,2,1,0:T(8,128)(2,1)}, bf16[1,9,16,640]{3,2,1,0:T(8,128)(2,1)S(1)}, u32[]{:S(2)}, u32[]{:S(2)}) %collective-permute-start.6) | collective-permute-done | bytes 184352 | tf_op jit(solution)/shard_map/ppermute | solution.py:15
  67.5 3.4 %collective-permute-done.7 = bf16[72,640]{1,0:T(8,128)(2,1)S(1)} collective-permute-done((bf16[72,640]{1,0:T(8,128)(2,1)S(1)}, bf16[72,640]{1,0:T(8,128)(2,1)S(1)}, u32[]{:S(2)}, u32[]{:S(2)}) %collective-permute-start.7) | collective-permute-done | bytes 92192 | tf_op jit(solution)/shard_map/ppermute | solution.py:15
  71.9 2.7 %collective-permute-start.12 = (bf16[40,640]{1,0:T(8,128)(2,1)S(1)}, bf16[40,640]{1,0:T(8,128)(2,1)S(1)}, u32[]{:S(2)}, u32[]{:S(2)}) collective-permute-start(bf16[40,640]{1,0:T(8,128)(2,1)S(1)} %dynamic-slice_convert_fusion.1), channel_id=1, source_target_pairs={{0,384},{1,385},{2,386},{3,387},{4,388},{5,389},{6,390},{7,391},{8... | collective-permute-start | bytes 153608 | tf_op jit(solution)/shard_map/ppermute | solution.py:15
  74.6 3.4 %collective-permute-done.12 = bf16[40,640]{1,0:T(8,128)(2,1)S(1)} collective-permute-done((bf16[40,640]{1,0:T(8,128)(2,1)S(1)}, bf16[40,640]{1,0:T(8,128)(2,1)S(1)}, u32[]{:S(2)}, u32[]{:S(2)}) %collective-permute-start.12) | collective-permute-done | bytes 51232 | tf_op jit(solution)/shard_map/ppermute | solution.py:15
  77.9 5.2 %collective-permute-start.13 = (bf16[40,640]{1,0:T(8,128)(2,1)S(1)}, bf16[40,640]{1,0:T(8,128)(2,1)S(1)}, u32[]{:S(2)}, u32[]{:S(2)}) collective-permute-start(bf16[40,640]{1,0:T(8,128)(2,1)S(1)} %add_convert_fusion.4), channel_id=1, source_target_pairs={{0,8},{1,9},{2,10},{3,11},{4,12},{5,13},{6,14},{7,15},{8,0},{9,1},... | collective-permute-start | bytes 153608 | tf_op jit(solution)/shard_map/ppermute | solution.py:15
  86.6 3.8 %collective-permute-done.14 = bf16[40,640]{1,0:T(8,128)(2,1)S(1)} collective-permute-done((bf16[40,640]{1,0:T(8,128)(2,1)S(1)}, bf16[40,640]{1,0:T(8,128)(2,1)S(1)}, u32[]{:S(2)}, u32[]{:S(2)}) %collective-permute-start.14) | collective-permute-done | bytes 51232 | tf_op jit(solution)/shard_map/ppermute | solution.py:15
  90.4 6.0 %collective-permute-start.15 = (bf16[40,640]{1,0:T(8,128)(2,1)S(1)}, bf16[40,640]{1,0:T(8,128)(2,1)S(1)}, u32[]{:S(2)}, u32[]{:S(2)}) collective-permute-start(bf16[40,640]{1,0:T(8,128)(2,1)S(1)} %add_convert_fusion.2), channel_id=1, source_target_pairs={{0,32},{1,33},{2,34},{3,35},{4,36},{5,37},{6,38},{7,39},{8,40},{9,... | collective-permute-start | bytes 153608 | tf_op jit(solution)/shard_map/ppermute | solution.py:15
  96.4 2.8 %collective-permute-done.15 = bf16[40,640]{1,0:T(8,128)(2,1)S(1)} collective-permute-done((bf16[40,640]{1,0:T(8,128)(2,1)S(1)}, bf16[40,640]{1,0:T(8,128)(2,1)S(1)}, u32[]{:S(2)}, u32[]{:S(2)}) %collective-permute-start.15) | collective-permute-done | bytes 51232 | tf_op jit(solution)/shard_map/ppermute | solution.py:15
  99.2 7.5 %collective-permute-start.16 = (bf16[40,640]{1,0:T(8,128)(2,1)S(1)}, bf16[40,640]{1,0:T(8,128)(2,1)S(1)}, u32[]{:S(2)}, u32[]{:S(2)}) collective-permute-start(bf16[40,640]{1,0:T(8,128)(2,1)S(1)} %add_convert_fusion.1), channel_id=1, source_target_pairs={{0,120},{1,121},{2,122},{3,123},{4,124},{5,125},{6,126},{7,127},{8... | collective-permute-start | bytes 153608 | tf_op jit(solution)/shard_map/ppermute | solution.py:15
  108.2 4.6 %collective-permute-start.17 = (bf16[40,640]{1,0:T(8,128)(2,1)S(1)}, bf16[40,640]{1,0:T(8,128)(2,1)S(1)}, u32[]{:S(2)}, u32[]{:S(2)}) collective-permute-start(bf16[40,640]{1,0:T(8,128)(2,1)S(1)} %add_convert_fusion), channel_id=1, source_target_pairs={{0,384},{1,385},{2,386},{3,387},{4,388},{5,389},{6,390},{7,391},{8... | collective-permute-start | bytes 153608 | tf_op jit(solution)/shard_map/ppermute | solution.py:15
  114.0 17.0 %collective-permute-start.11 = (bf16[256,640]{1,0:T(8,128)(2,1)S(1)}, bf16[256,640]{1,0:T(8,128)(2,1)S(1)}, u32[]{:S(2)}, u32[]{:S(2)}) collective-permute-start(bf16[256,640]{1,0:T(8,128)(2,1)S(1)} %multiply_convert_fusion.1), channel_id=1, source_target_pairs={{0,15},{1,14},{2,13},{3,12},{4,11},{5,10},{6,9},{7,8},{8,7},{9,6},... | collective-permute-start | bytes 983048 | tf_op jit(solution)/shard_map/ppermute | solution.py:15
  140.8 2.8 %collective-permute-done.18 = bf16[72,640]{1,0:T(8,128)(2,1)S(1)} collective-permute-done((bf16[72,640]{1,0:T(8,128)(2,1)S(1)}, bf16[72,640]{1,0:T(8,128)(2,1)S(1)}, u32[]{:S(2)}, u32[]{:S(2)}) %collective-permute-start.18) | collective-permute-done | bytes 92192 | tf_op jit(solution)/shard_map/ppermute | solution.py:15
  143.7 2.9 %collective-permute-done.9 = bf16[256,640]{1,0:T(8,128)(2,1)S(1)} collective-permute-done((bf16[256,640]{1,0:T(8,128)(2,1)S(1)}, bf16[256,640]{1,0:T(8,128)(2,1)S(1)}, u32[]{:S(2)}, u32[]{:S(2)}) %collective-permute-start.9) | collective-permute-done | bytes 327712 | tf_op jit(solution)/shard_map/ppermute | solution.py:15
  146.6 4.4 %collective-permute-start.19 = (bf16[1,9,16,640]{3,2,1,0:T(8,128)(2,1)S(1)}, bf16[1,9,16,640]{3,2,1,0:T(8,128)(2,1)S(1)}, u32[]{:S(2)}, u32[]{:S(2)}) collective-permute-start(bf16[1,9,16,640]{3,2,1,0:T(8,128)(2,1)S(1)} %bitcast.43), channel_id=1, source_target_pairs={{0,6},{1,7},{2,4},{3,5},{4,2},{5,3},{6,0},{7,1},{8,14},{9,15},{10,... | collective-permute-start | bytes 552968 | tf_op jit(solution)/shard_map/ppermute | solution.py:15
  161.8 5.3 %collective-permute-done.20 = bf16[2,9,16,640]{3,2,1,0:T(8,128)(2,1)S(1)} collective-permute-done((bf16[2,9,16,640]{3,2,1,0:T(8,128)(2,1)S(1)}, bf16[2,9,16,640]{3,2,1,0:T(8,128)(2,1)S(1)}, u32[]{:S(2)}, u32[]{:S(2)}) %collective-permute-start.20) | collective-permute-done | bytes 368672 | tf_op jit(solution)/shard_map/ppermute | solution.py:15
  167.9 3.6 %collective-permute-start.21 = (bf16[4,9,16,640]{3,2,1,0:T(8,128)(2,1)}, bf16[4,9,16,640]{3,2,1,0:T(8,128)(2,1)}, u32[]{:S(2)}, u32[]{:S(2)}) collective-permute-start(bf16[4,9,16,640]{3,2,1,0:T(8,128)(2,1)} %constant_dynamic-update-slice_fusion.mine_ref), channel_id=1, source_target_pairs={{0,1},{1,0},{2,3},{3,2},{4,5},{5,4},{6,7},{7,6},{8,9},{9,8},{10,11... | collective-permute-start | bytes 2211848 | tf_op jit(solution)/shard_map/ppermute | solution.py:15
  177.3 45.8 %shard_map.86 = bf16[9,8,16,640]{3,2,1,0:T(8,128)(2,1)} custom-call(s32[1]{0:T(128)} %bitcast.2.label_ref, bf16[4,9,16,640]{3,2,1,0:T(8,128)(2,1)} %constant_dynamic-update-slice_fusion.mine_ref, bf16[4,9,16,640]{3,2,1,0:T(8,128)(2,1)} %collective-permute-done.21.other_ref), custom_call_target="tpu_custom_call" | custom-call | bytes 3000000 | tf_op jit(solution)/shard_map/pallas_call | solution.py:86
  (81 shorter events, 62.3 us)
Async XLA Ops:
  3.0 18.0 %copy-start.2 = (bf16[256,640]{1,0:T(8,128)(2,1)S(1)}, bf16[256,640]{1,0:T(8,128)(2,1)}, u32[]{:S(2)}) copy-start(bf16[256,640]{1,0:T(8,128)(2,1)} %param.8) | copy-start | bytes 983044
  3.0 18.0 %copy-start.8 = (s32[256]{0:T(256)S(1)}, s32[256]{0:T(256)}, u32[]{:S(2)}) copy-start(s32[256]{0:T(256)} %param.9) | copy-start | bytes 3076
  3.0 20.3 %collective-permute-start.3 = (bf16[256,640]{1,0:T(8,128)(2,1)S(1)}, bf16[256,640]{1,0:T(8,128)(2,1)}, u32[]{:S(2)}, u32[]{:S(2)}) collective-permute-start(bf16[256,640]{1,0:T(8,128)(2,1)S(1)} %fusion.68), channel_id=1, source_target_pairs={{0,15},{1,14},{2,13},{3,12},{4,11},{5,10},{6,9},{7,8},{8,7},{9,6},... | collective-permute-start | bytes 983048 | tf_op jit(solution)/shard_map/ppermute | solution.py:15
  10.3 16.9 %collective-permute-start.2 = (bf16[256,640]{1,0:T(8,128)(2,1)S(1)}, bf16[256,640]{1,0:T(8,128)(2,1)}, u32[]{:S(2)}, u32[]{:S(2)}) collective-permute-start(bf16[256,640]{1,0:T(8,128)(2,1)S(1)} %fusion.68), channel_id=1, source_target_pairs={{0,7},{1,6},{2,5},{3,4},{4,3},{5,2},{6,1},{7,0},{8,15},{9,14},{10,... | collective-permute-start | bytes 983048 | tf_op jit(solution)/shard_map/ppermute | solution.py:15
  12.2 17.6 %collective-permute-start = (bf16[256,640]{1,0:T(8,128)(2,1)S(1)}, bf16[256,640]{1,0:T(8,128)(2,1)}, u32[]{:S(2)}, u32[]{:S(2)}) collective-permute-start(bf16[256,640]{1,0:T(8,128)(2,1)S(1)} %fusion.68), channel_id=1, source_target_pairs={{0,1},{1,0},{2,3},{3,2},{4,5},{5,4},{6,7},{7,6},{8,9},{9,8},{10,11... | collective-permute-start | bytes 983048 | tf_op jit(solution)/shard_map/ppermute | solution.py:15
  15.8 16.8 %collective-permute-start.1 = (bf16[256,640]{1,0:T(8,128)(2,1)S(1)}, bf16[256,640]{1,0:T(8,128)(2,1)S(1)}, u32[]{:S(2)}, u32[]{:S(2)}) collective-permute-start(bf16[256,640]{1,0:T(8,128)(2,1)S(1)} %fusion.68), channel_id=1, source_target_pairs={{0,3},{1,2},{2,1},{3,0},{4,7},{5,6},{6,5},{7,4},{8,11},{9,10},{10,... | collective-permute-start | bytes 983048 | tf_op jit(solution)/shard_map/ppermute | solution.py:15
  39.7 4.2 %collective-permute-start.4 = (bf16[4,9,16,640]{3,2,1,0:T(8,128)(2,1)S(1)}, bf16[4,9,16,640]{3,2,1,0:T(8,128)(2,1)S(1)}, u32[]{:S(2)}, u32[]{:S(2)}) collective-permute-start(bf16[4,9,16,640]{3,2,1,0:T(8,128)(2,1)S(1)} %get-tuple-element.8), channel_id=1, source_target_pairs={{0,1},{1,0},{2,3},{3,2},{4,5},{5,4},{6,7},{7,6},{8,9},{9,8},{10,11... | collective-permute-start | bytes 2211848 | tf_op jit(solution)/shard_map/ppermute | solution.py:15
  44.1 11.7 %collective-permute-start.5 = (bf16[2,9,16,640]{3,2,1,0:T(8,128)(2,1)S(1)}, bf16[2,9,16,640]{3,2,1,0:T(8,128)(2,1)S(1)}, u32[]{:S(2)}, u32[]{:S(2)}) collective-permute-start(bf16[2,9,16,640]{3,2,1,0:T(8,128)(2,1)S(1)} %slice.36), channel_id=1, source_target_pairs={{0,2},{1,3},{2,0},{3,1},{4,6},{5,7},{6,4},{7,5},{8,10},{9,11},{10,... | collective-permute-start | bytes 1105928 | tf_op jit(solution)/shard_map/ppermute | solution.py:15
  56.6 8.2 %collective-permute-start.6 = (bf16[1,9,16,640]{3,2,1,0:T(8,128)(2,1)}, bf16[1,9,16,640]{3,2,1,0:T(8,128)(2,1)S(1)}, u32[]{:S(2)}, u32[]{:S(2)}) collective-permute-start(bf16[1,9,16,640]{3,2,1,0:T(8,128)(2,1)} %slice.37), channel_id=1, source_target_pairs={{0,6},{1,7},{2,4},{3,5},{4,2},{5,3},{6,0},{7,1},{8,14},{9,15},{10,... | collective-permute-start | bytes 552968 | tf_op jit(solution)/shard_map/ppermute | solution.py:15
  65.6 5.3 %collective-permute-start.7 = (bf16[72,640]{1,0:T(8,128)(2,1)S(1)}, bf16[72,640]{1,0:T(8,128)(2,1)S(1)}, u32[]{:S(2)}, u32[]{:S(2)}) collective-permute-start(bf16[72,640]{1,0:T(8,128)(2,1)S(1)} %dynamic-slice_convert_fusion), channel_id=1, source_target_pairs={{0,128},{1,129},{2,130},{3,131},{4,132},{5,133},{6,134},{7,135},{8... | collective-permute-start | bytes 276488 | tf_op jit(solution)/shard_map/ppermute | solution.py:15
  71.9 6.1 %collective-permute-start.12 = (bf16[40,640]{1,0:T(8,128)(2,1)S(1)}, bf16[40,640]{1,0:T(8,128)(2,1)S(1)}, u32[]{:S(2)}, u32[]{:S(2)}) collective-permute-start(bf16[40,640]{1,0:T(8,128)(2,1)S(1)} %dynamic-slice_convert_fusion.1), channel_id=1, source_target_pairs={{0,384},{1,385},{2,386},{3,387},{4,388},{5,389},{6,390},{7,391},{8... | collective-permute-start | bytes 153608 | tf_op jit(solution)/shard_map/ppermute | solution.py:15
  77.9 6.7 %collective-permute-start.13 = (bf16[40,640]{1,0:T(8,128)(2,1)S(1)}, bf16[40,640]{1,0:T(8,128)(2,1)S(1)}, u32[]{:S(2)}, u32[]{:S(2)}) collective-permute-start(bf16[40,640]{1,0:T(8,128)(2,1)S(1)} %add_convert_fusion.4), channel_id=1, source_target_pairs={{0,8},{1,9},{2,10},{3,11},{4,12},{5,13},{6,14},{7,15},{8,0},{9,1},... | collective-permute-start | bytes 153608 | tf_op jit(solution)/shard_map/ppermute | solution.py:15
  84.6 5.8 %collective-permute-start.14 = (bf16[40,640]{1,0:T(8,128)(2,1)S(1)}, bf16[40,640]{1,0:T(8,128)(2,1)S(1)}, u32[]{:S(2)}, u32[]{:S(2)}) collective-permute-start(bf16[40,640]{1,0:T(8,128)(2,1)S(1)} %add_convert_fusion.3), channel_id=1, source_target_pairs={{0,16},{1,17},{2,18},{3,19},{4,20},{5,21},{6,22},{7,23},{8,24},{9,... | collective-permute-start | bytes 153608 | tf_op jit(solution)/shard_map/ppermute | solution.py:15
  90.4 8.8 %collective-permute-start.15 = (bf16[40,640]{1,0:T(8,128)(2,1)S(1)}, bf16[40,640]{1,0:T(8,128)(2,1)S(1)}, u32[]{:S(2)}, u32[]{:S(2)}) collective-permute-start(bf16[40,640]{1,0:T(8,128)(2,1)S(1)} %add_convert_fusion.2), channel_id=1, source_target_pairs={{0,32},{1,33},{2,34},{3,35},{4,36},{5,37},{6,38},{7,39},{8,40},{9,... | collective-permute-start | bytes 153608 | tf_op jit(solution)/shard_map/ppermute | solution.py:15
  99.2 9.0 %collective-permute-start.16 = (bf16[40,640]{1,0:T(8,128)(2,1)S(1)}, bf16[40,640]{1,0:T(8,128)(2,1)S(1)}, u32[]{:S(2)}, u32[]{:S(2)}) collective-permute-start(bf16[40,640]{1,0:T(8,128)(2,1)S(1)} %add_convert_fusion.1), channel_id=1, source_target_pairs={{0,120},{1,121},{2,122},{3,123},{4,124},{5,125},{6,126},{7,127},{8... | collective-permute-start | bytes 153608 | tf_op jit(solution)/shard_map/ppermute | solution.py:15
  108.2 29.2 %collective-permute-start.17 = (bf16[40,640]{1,0:T(8,128)(2,1)S(1)}, bf16[40,640]{1,0:T(8,128)(2,1)S(1)}, u32[]{:S(2)}, u32[]{:S(2)}) collective-permute-start(bf16[40,640]{1,0:T(8,128)(2,1)S(1)} %add_convert_fusion), channel_id=1, source_target_pairs={{0,384},{1,385},{2,386},{3,387},{4,388},{5,389},{6,390},{7,391},{8... | collective-permute-start | bytes 153608 | tf_op jit(solution)/shard_map/ppermute | solution.py:15
  114.0 29.6 %collective-permute-start.11 = (bf16[256,640]{1,0:T(8,128)(2,1)S(1)}, bf16[256,640]{1,0:T(8,128)(2,1)S(1)}, u32[]{:S(2)}, u32[]{:S(2)}) collective-permute-start(bf16[256,640]{1,0:T(8,128)(2,1)S(1)} %multiply_convert_fusion.1), channel_id=1, source_target_pairs={{0,15},{1,14},{2,13},{3,12},{4,11},{5,10},{6,9},{7,8},{8,7},{9,6},... | collective-permute-start | bytes 983048 | tf_op jit(solution)/shard_map/ppermute | solution.py:15
  131.0 12.7 %collective-permute-start.10 = (bf16[256,640]{1,0:T(8,128)(2,1)S(1)}, bf16[256,640]{1,0:T(8,128)(2,1)S(1)}, u32[]{:S(2)}, u32[]{:S(2)}) collective-permute-start(bf16[256,640]{1,0:T(8,128)(2,1)S(1)} %multiply_convert_fusion.1), channel_id=1, source_target_pairs={{0,7},{1,6},{2,5},{3,4},{4,3},{5,2},{6,1},{7,0},{8,15},{9,14},{10,... | collective-permute-start | bytes 983048 | tf_op jit(solution)/shard_map/ppermute | solution.py:15
  132.9 10.8 %collective-permute-start.8 = (bf16[256,640]{1,0:T(8,128)(2,1)S(1)}, bf16[256,640]{1,0:T(8,128)(2,1)S(1)}, u32[]{:S(2)}, u32[]{:S(2)}) collective-permute-start(bf16[256,640]{1,0:T(8,128)(2,1)S(1)} %multiply_convert_fusion.1), channel_id=1, source_target_pairs={{0,1},{1,0},{2,3},{3,2},{4,5},{5,4},{6,7},{7,6},{8,9},{9,8},{10,11... | collective-permute-start | bytes 983048 | tf_op jit(solution)/shard_map/ppermute | solution.py:15
  135.4 11.2 %collective-permute-start.9 = (bf16[256,640]{1,0:T(8,128)(2,1)S(1)}, bf16[256,640]{1,0:T(8,128)(2,1)S(1)}, u32[]{:S(2)}, u32[]{:S(2)}) collective-permute-start(bf16[256,640]{1,0:T(8,128)(2,1)S(1)} %multiply_convert_fusion.1), channel_id=1, source_target_pairs={{0,3},{1,2},{2,1},{3,0},{4,7},{5,6},{6,5},{7,4},{8,11},{9,10},{10,... | collective-permute-start | bytes 983048 | tf_op jit(solution)/shard_map/ppermute | solution.py:15
  137.4 6.2 %collective-permute-start.18 = (bf16[72,640]{1,0:T(8,128)(2,1)S(1)}, bf16[72,640]{1,0:T(8,128)(2,1)S(1)}, u32[]{:S(2)}, u32[]{:S(2)}) collective-permute-start(bf16[72,640]{1,0:T(8,128)(2,1)S(1)} %maximum_select_fusion.1), channel_id=1, source_target_pairs={{0,128},{1,129},{2,130},{3,131},{4,132},{5,133},{6,134},{7,135},{8... | collective-permute-start | bytes 276488 | tf_op jit(solution)/shard_map/ppermute | solution.py:15
  146.6 9.3 %collective-permute-start.19 = (bf16[1,9,16,640]{3,2,1,0:T(8,128)(2,1)S(1)}, bf16[1,9,16,640]{3,2,1,0:T(8,128)(2,1)S(1)}, u32[]{:S(2)}, u32[]{:S(2)}) collective-permute-start(bf16[1,9,16,640]{3,2,1,0:T(8,128)(2,1)S(1)} %bitcast.43), channel_id=1, source_target_pairs={{0,6},{1,7},{2,4},{3,5},{4,2},{5,3},{6,0},{7,1},{8,14},{9,15},{10,... | collective-permute-start | bytes 552968 | tf_op jit(solution)/shard_map/ppermute | solution.py:15
  156.0 11.2 %collective-permute-start.20 = (bf16[2,9,16,640]{3,2,1,0:T(8,128)(2,1)S(1)}, bf16[2,9,16,640]{3,2,1,0:T(8,128)(2,1)S(1)}, u32[]{:S(2)}, u32[]{:S(2)}) collective-permute-start(bf16[2,9,16,640]{3,2,1,0:T(8,128)(2,1)S(1)} %pad_maximum_fusion), channel_id=1, source_target_pairs={{0,2},{1,3},{2,0},{3,1},{4,6},{5,7},{6,4},{7,5},{8,10},{9,11},{10,... | collective-permute-start | bytes 1105928 | tf_op jit(solution)/shard_map/ppermute | solution.py:15
  167.9 9.4 %collective-permute-start.21 = (bf16[4,9,16,640]{3,2,1,0:T(8,128)(2,1)}, bf16[4,9,16,640]{3,2,1,0:T(8,128)(2,1)}, u32[]{:S(2)}, u32[]{:S(2)}) collective-permute-start(bf16[4,9,16,640]{3,2,1,0:T(8,128)(2,1)} %constant_dynamic-update-slice_fusion.mine_ref), channel_id=1, source_target_pairs={{0,1},{1,0},{2,3},{3,2},{4,5},{5,4},{6,7},{7,6},{8,9},{9,8},{10,11... | collective-permute-start | bytes 2211848 | tf_op jit(solution)/shard_map/ppermute | solution.py:15
  (7 other events, 33.2 us)

commit v2 on v0

v2 whole, which is shorter than its diff:
```python
import jax
import jax.numpy as jnp
from jax import lax
from jax.experimental import pallas as pl
from jax.experimental.pallas import tpu as pltpu
from jax.sharding import PartitionSpec as P

D = 1152
E = 640
ROWS = 256
F32 = jnp.float32
BF16 = jnp.bfloat16
OWNERS, SLABS = 16, 12
SMEM = pl.BlockSpec(memory_space=pltpu.SMEM)
VMEM = pl.BlockSpec(memory_space=pltpu.VMEM)


def group(bits):
    mask = sum(1 << b for b in bits)
    members = [
        sum((k >> j & 1) << b for j, b in enumerate(bits)) for k in range(1 << len(bits))
    ]
    return [[base | m for m in members] for base in range(512) if not base & mask]


PLANE = group((1, 2, 7, 8))


def swap(value, mask):
    pairs = [(source, source ^ mask) for source in range(lax.axis_size("dp"))]
    return lax.ppermute(value, "dp", pairs)


def exchange(value):
    return lax.all_to_all(value, "dp", 0, 0, axis_index_groups=PLANE, tiled=True)


def after(value, *others):
    return lax.optimization_barrier((value,) + others)[0]


def shape(*dims, dtype=F32):
    return jax.ShapeDtypeStruct(dims, dtype)


def dot(left, right, left_dim=1, right_dim=0):
    return lax.dot_general(
        left, right, (((left_dim,), (right_dim,)), ((), ())), preferred_element_type=F32
    )


def call(kernel, out_shape, specs, flops, *operands, scratch=(), out_specs=None):
    return pl.pallas_call(
        kernel,
        out_shape=out_shape,
        in_specs=specs,
        out_specs=out_specs if out_specs is not None else jax.tree.map(lambda _: VMEM, out_shape),
        scratch_shapes=scratch,
        compiler_params=pltpu.CompilerParams(vmem_limit_bytes=32 << 20),
        cost_estimate=pl.CostEstimate(flops=flops, bytes_accessed=100000, transcendentals=0),
    )(*operands)


def inverse_norm(value):
    return lax.rsqrt(jnp.sum(value * value, axis=-1, keepdims=True) + 1e-06)


def tangent(d_unit, unit, inverse):
    return ((d_unit - unit * jnp.sum(unit * d_unit, axis=-1, keepdims=True)) * inverse).astype(BF16)


def text_kernel(core_ref, txt_ref, feat_ref, rows_ref, packed_ref):
    value = txt_ref[...].astype(F32)
    rows = (value * inverse_norm(value)).astype(BF16)
    rows_ref[...] = rows
    packed_ref[:, :E] = rows
    start = pl.multiple_of(512 * (1 - core_ref[0]), 128)
    packed_ref[:, E:] = feat_ref[:, pl.ds(start, E)]


def image_kernel(
    scale_ref, bias_ref, labels_ref, feat_ref, head_ref, txt_ref,
    unit_ref, inverse_ref, rows_ref, d_img_ref, d_txt_ref,
):
    proj = dot(feat_ref[...], head_ref[...])
    inverse = inverse_norm(proj)
    unit = proj * inverse
    rows = unit.astype(BF16)
    txt = txt_ref[...]
    unit_ref[...] = unit
    inverse_ref[...] = inverse
    rows_ref[...] = rows
    across = jnp.broadcast_to(labels_ref[...].astype(F32), (ROWS, ROWS))
    sign = jnp.where(across == across.T, 1.0, -1.0)
    logits = scale_ref[0] * dot(rows, txt, 1, 1) + bias_ref[0]
    grad = (-sign * jax.nn.sigmoid(-sign * logits)).astype(BF16)
    d_img_ref[...] = dot(grad, txt)
    d_txt_ref[...] = dot(grad, rows, 0, 0)


def pair_term(scale_ref, bias_ref, rows, others):
    logits = scale_ref[0] * dot(rows, others, 1, 1) + bias_ref[0]
    return dot(jax.nn.sigmoid(logits).astype(BF16), others)


def pair_kernel(scale_ref, bias_ref, total_ref, rows_ref, other_ref, out_ref):
    out_ref[...] = total_ref[...] + pair_term(scale_ref, bias_ref, rows_ref[...], other_ref[...])


def packed_text_kernel(scale_ref, bias_ref, total_ref, rows_ref, packed_ref, out_ref):
    term = pair_term(scale_ref, bias_ref, rows_ref[...], packed_ref[:, :E])
    out_ref[...] = total_ref[...] + term


def image_end_kernel(
    scale_ref, bias_ref, total_ref, rows_ref, other_ref, unit_ref, inverse_ref, packed_ref
):
    rows = rows_ref[...]
    total = total_ref[...] + pair_term(scale_ref, bias_ref, rows, other_ref[...])
    packed_ref[:, :E] = tangent(scale_ref[0] * total, unit_ref[...], inverse_ref[...])
    packed_ref[:, E:] = rows


def packed_image_kernel(scale_ref, bias_ref, total_ref, rows_ref, packed_ref, out_ref):
    out_ref[...] = total_ref[...] + pair_term(scale_ref, bias_ref, rows_ref[...], packed_ref[:, E:])


def text_end_kernel(scale_ref, bias_ref, total_ref, rows_ref, a_ref, b_ref, c_ref, txt_ref, out_ref):
    rows = rows_ref[...]
    total = total_ref[...]
    for other_ref in (a_ref, b_ref, c_ref):
        total = total + pair_term(scale_ref, bias_ref, rows, other_ref[...])
    value = txt_ref[...].astype(F32)
    inverse = inverse_norm(value)
    out_ref[...] = tangent(scale_ref[0] * total, value * inverse, inverse)


def head_kernel(core_ref, feat_ref, other_feat_ref, mine_ref, theirs_ref, out_ref):
    core = core_ref[0]
    mine, theirs = mine_ref[:, :E], theirs_ref[:, :E]

    def product(column):
        here = pl.multiple_of(column, 128)
        there = pl.multiple_of(E + column - 512 * core, 128)
        total = dot(feat_ref[:, pl.ds(here, 128)], mine, 0, 0)
        return total + dot(other_feat_ref[:, pl.ds(there, 128)], theirs, 0, 0)

    def store(band, rows):
        for t in range(5):
            slab = band * 5 + t
            out_ref[slab // SLABS, slab % SLABS] = rows[:, 128 * t : 128 * t + 128].astype(BF16)

    for block in range(4):
        total = product(5 * 128 * core + 128 * block)
        for j in range(8):
            store(8 * block + j, total[16 * j : 16 * j + 16])
    total = product(512)
    total = jnp.where(core == 0, total[:64], total[64:])
    for j in range(4):
        store(32 + j, total[16 * j : 16 * j + 16])
    out_ref[OWNERS - 1] = jnp.zeros((SLABS, 16, 128), BF16)


def place_kernel(core_ref, mine_ref, theirs_ref, out_ref, whole, sems):
    core = core_ref[0]
    copies = []
    for block in range(9):
        for band in range(8 * block, 8 * block + 8):
            owner = int(band >= 36)
            own = band if band < 36 else band - 40 if band >= 40 else band - 4
            for t in range(5):
                slab = own * 5 + t
                at = (slab // SLABS, slab % SLABS)
                value = jnp.where(core == owner, mine_ref[at], theirs_ref[at])
                whole[16 * band : 16 * band + 16, 128 * t : 128 * t + 128] = value
        rows = pl.ds(128 * block, 128)
        copies.append(pltpu.make_async_copy(whole.at[rows], out_ref.at[rows], sems.at[block]))
        copies[-1].start()
    for copy in copies:
        copy.wait()


def per_device(img_feat, head_weight, txt_emb, labels, log_logit_scale, bias):
    core = (lax.axis_index("dp") & 1)[None]
    scale = jnp.exp(log_logit_scale)
    pair = ROWS * ROWS * E * 4
    little = pair // 100
    block = shape(ROWS, E)
    block16 = shape(ROWS, E, dtype=BF16)

    pair16 = shape(ROWS, 2 * E, dtype=BF16)
    txt_rows, packed_txt = call(
        text_kernel, (block16, pair16), [SMEM, VMEM, VMEM], 1000000, core, txt_emb, img_feat
    )
    txt_15 = swap(txt_rows, 15)
    txt_7 = swap(txt_rows, 7)
    txt_3 = swap(txt_rows, 3)
    packed_txt = swap(packed_txt, 1)

    unit, inverse, img_rows, d_img, d_txt = call(
        image_kernel,
        (block, shape(ROWS, 1), block16, block, block),
        [SMEM, SMEM, VMEM, VMEM, VMEM, VMEM],
        12 * pair,
        scale, bias, labels[None, :], img_feat, head_weight, txt_rows,
    )
    pair_specs = [SMEM, SMEM, VMEM, VMEM, VMEM]
    for kernel, other in (
        (pair_kernel, txt_15), (pair_kernel, txt_3), (packed_text_kernel, packed_txt),
    ):
        d_img = call(kernel, block, pair_specs, little, scale, bias, d_img, img_rows, other)
    img_3 = swap(img_rows, 3)
    d_img = after(d_img, img_3)
    packed_img = call(
        image_end_kernel, pair16, pair_specs + [VMEM, VMEM], little,
        scale, bias, d_img, img_rows, txt_7, unit, inverse,
    )
    other_img = swap(packed_img, 1)

    parts = call(
        head_kernel, shape(OWNERS, SLABS, 16, 128, dtype=BF16), [SMEM] + [VMEM] * 4,
        4 * ROWS * D * E // 2, core, img_feat, packed_txt, packed_img, other_img,
    )
    total = jnp.sum(exchange(parts).astype(F32), axis=0)
    d_img_feat = dot(packed_img[:, :E], head_weight, 1, 1).astype(BF16)
    d_txt = call(
        packed_image_kernel, block, pair_specs, 2 * pair,
        scale, bias, d_txt, txt_rows, other_img,
    )
    images = [img_3]
    for z, beside, c in ((15, None, 7), (4, d_img_feat, 15), (2, d_txt, None), (1, None, None)):
        mine = total.astype(BF16)
        sent = mine if beside is None else after(mine, beside, *images)
        if c is not None:
            images.append(swap(after(img_rows, mine), c))
        total = mine.astype(F32) + swap(sent, z * 8).astype(F32)
    part = total.astype(BF16)
    parts = exchange(after(jnp.broadcast_to(part[None], (OWNERS, SLABS, 16, 128))))
    d_head = call(
        place_kernel, shape(D, E, dtype=BF16), [SMEM, VMEM, VMEM], 0,
        core, parts, swap(parts, 1),
        scratch=[pltpu.VMEM((D, E), BF16), pltpu.SemaphoreType.DMA((9,))],
        out_specs=pl.BlockSpec(memory_space=pl.ANY),
    )

    d_txt_emb = call(
        text_end_kernel, block16, pair_specs + [VMEM] * 3, 3 * pair,
        scale, bias, d_txt, txt_rows, *images, txt_emb,
    )
    return (d_img_feat, d_txt_emb, d_head)


def solution(mesh):
    return jax.shard_map(
        per_device,
        mesh=mesh,
        in_specs=(P("dp", None), P(), P("dp", None), P("dp"), P(), P()),
        out_specs=(P("dp", None), P("dp", None), P()),
        check_vma=False,
    )
```

time: 310 us -> 139 us (0.45)
  blocking collectives: 199 us -> 31.6 us
  waiting for transfers between devices: 46.4 us -> 23.9 us
  starting transfers between devices: 41.4 us -> 62.6 us
  matrix products: 13.8 us -> 1.48 us
  Pallas kernels: 0 us -> 9.15 us
  local copies, waits for them, and re-layouts: 2.13 us -> 6.15 us
    psum x1 -> x0, blocking collectives: 199 us -> none  [per_device(): d_head = lax.psum(head_terms, 'dp').astype(jnp.bfloat16)]
    all_to_all x0 -> x2, blocking collectives: none -> 31.6 us  [exchange(): lax.all_to_all(value, 'dp', 0, 0, axis_index_groups=PLANE, tiled=True)]
    ppermute x14 -> x13, waiting for transfers between devices: 46.4 us -> 23.9 us  [swap(): return lax.ppermute(value, 'dp', pairs)]
    ppermute x14 -> x13, starting transfers between devices: 41.4 us -> 62.6 us  [swap(): return lax.ppermute(value, 'dp', pairs)]
    dot_general x18 -> x1, matrix products: 13.8 us -> 1.48 us  [dot(): lax.dot_general(left, right, (((left_dim,), (right_dim,)), ((), ())), pre...]
    pallas_call x0 -> x10, Pallas kernels: none -> 9.15 us  [call(): pl.pallas_call(kernel, out_shape=out_shape, in_specs=specs, out_specs=out...]
    unnamed x11 -> x24, local copies, waits for them, and re-layouts: 2.13 us -> 6.01 us
  transfers between devices with their start and end apart: 14 -> 13, of which waited for: 6 -> 7; matrix products, arithmetic and copies ran while one was open for 5% -> 1% of each run, Pallas kernels for 0% -> 5%
where the time goes in v2:
time: 139 us
  starting transfers between devices  62.6 us (45%)
  blocking collectives  31.6 us (23%)
  waiting for transfers between devices  23.9 us (17%)
  Pallas kernels  9.15 us (7%)
  local copies, waits for them, and re-layouts  6.15 us (4%)
  between operations  2.3 us (2%)
  matrix products  1.48 us (1%)
    ppermute x13, starting transfers between devices, swap(): return lax.ppermute(value, 'dp', pairs)  62.6 us
    all_to_all x2, blocking collectives, exchange(): lax.all_to_all(value, 'dp', 0, 0, axis_index_groups=PLANE, tiled=True)  31.6 us
    ppermute x13, waiting for transfers between devices, swap(): return lax.ppermute(value, 'dp', pairs)  23.9 us
    pallas_call x10, Pallas kernels, call(): pl.pallas_call(kernel, out_shape=out_shape, in_specs=specs, out_specs=out...  9.15 us
    unnamed x24, local copies, waits for them, and re-layouts  6.01 us
  transfers between devices with their start and end apart: 13, of which 7 were waited for; matrix products, arithmetic and copies ran while one was open for 1% of the time, Pallas kernels for 5%

profile of v2, /device:TPU:1, one launch (start us, length us, event | category | flops | bytes accessed | tf_op | source)
XLA Modules:
  0.0 138.5 jit_solution(9708320969573508718)
XLA Ops:
  2.8 8.8 %collective-permute-start.2 = (bf16[256,1280]{1,0:T(8,128)(2,1)S(1)}, bf16[256,1280]{1,0:T(8,128)(2,1)S(1)}, u32[]{:S(2)}, u32[]{:S(2)}) collective-permute-start(bf16[256,1280]{1,0:T(8,128)(2,1)S(1)} %get-tuple-element.18), channel_id=1, source_target_pairs={{0,1},{1,0},{2,3},{3,2},{4,5},{5,4},{6,7},{7,6},{8,9},{9,8},{10,11... | collective-permute-start | bytes 1966088 | tf_op jit(solution)/shard_map/ppermute | solution.py:31
  11.6 1.9 %collective-permute-start = (bf16[256,640]{1,0:T(8,128)(2,1)S(1)}, bf16[256,640]{1,0:T(8,128)(2,1)S(1)}, u32[]{:S(2)}, u32[]{:S(2)}) collective-permute-start(bf16[256,640]{1,0:T(8,128)(2,1)S(1)} %get-tuple-element.15.txt_ref.rows_ref), channel_id=1, source_target_pairs={{0,15},{1,14},{2,13},{3,12},{4,11},{5,10},{6,9},{7,8},{8,7},{9,6},... | collective-permute-start | bytes 983048 | tf_op jit(solution)/shard_map/ppermute | solution.py:31
  13.6 1.9 %collective-permute-start.1 = (bf16[256,640]{1,0:T(8,128)(2,1)S(1)}, bf16[256,640]{1,0:T(8,128)(2,1)S(1)}, u32[]{:S(2)}, u32[]{:S(2)}) collective-permute-start(bf16[256,640]{1,0:T(8,128)(2,1)S(1)} %get-tuple-element.15.txt_ref.rows_ref), channel_id=1, source_target_pairs={{0,3},{1,2},{2,1},{3,0},{4,7},{5,6},{6,5},{7,4},{8,11},{9,10},{10,... | collective-permute-start | bytes 983048 | tf_op jit(solution)/shard_map/ppermute | solution.py:31
  19.9 1.5 %shard_map.86 = (f32[256,640]{1,0:T(8,128)S(1)}, f32[256,1]{1,0:T(8,128)S(1)}, bf16[256,640]{1,0:T(8,128)(2,1)S(1)}, f32[256,640]{1,0:T(8,128)S(1)}, f32[256,640]{1,0:T(8,128)S(1)}) custom-call(f32[1]{0:T(128)S(6)} %exp.3.scale_ref, f32[1]{0:T(128)S(6)} %copy.10.bias_ref, s32[1,256]{1,0:T(1,128)S(1)} %bitcast.3, bf16[256,1152]{1,0:T(8,128)(2,1)S(1)} %copy-done.1, ...), custom_call_target="tpu_custom_call" | custom-call | flops 2013265920 | bytes 100000 | tf_op jit(solution)/shard_map/pallas_call | solution.py:53
  22.2 3.6 %collective-permute-start.3 = (bf16[256,640]{1,0:T(8,128)(2,1)S(1)}, bf16[256,640]{1,0:T(8,128)(2,1)S(1)}, u32[]{:S(2)}, u32[]{:S(2)}) collective-permute-start(bf16[256,640]{1,0:T(8,128)(2,1)S(1)} %get-tuple-element.24.rows_ref), channel_id=1, source_target_pairs={{0,3},{1,2},{2,1},{3,0},{4,7},{5,6},{6,5},{7,4},{8,11},{9,10},{10,... | collective-permute-start | bytes 983048 | tf_op jit(solution)/shard_map/ppermute | solution.py:31
  25.9 1.9 %collective-permute-start.4 = (bf16[256,640]{1,0:T(8,128)(2,1)S(1)}, bf16[256,640]{1,0:T(8,128)(2,1)S(1)}, u32[]{:S(2)}, u32[]{:S(2)}) collective-permute-start(bf16[256,640]{1,0:T(8,128)(2,1)S(1)} %get-tuple-element.15.txt_ref.rows_ref), channel_id=1, source_target_pairs={{0,7},{1,6},{2,5},{3,4},{4,3},{5,2},{6,1},{7,0},{8,15},{9,14},{10,... | collective-permute-start | bytes 983048 | tf_op jit(solution)/shard_map/ppermute | solution.py:31
  29.8 3.9 %collective-permute-done.3.a_ref = bf16[256,640]{1,0:T(8,128)(2,1)S(1)} collective-permute-done((bf16[256,640]{1,0:T(8,128)(2,1)S(1)}, bf16[256,640]{1,0:T(8,128)(2,1)S(1)}, u32[]{:S(2)}, u32[]{:S(2)}) %collective-permute-start.3) | collective-permute-done | bytes 327712 | tf_op jit(solution)/shard_map/ppermute | solution.py:31
  33.8 4.6 %collective-permute-done.4.other_ref = bf16[256,640]{1,0:T(8,128)(2,1)S(1)} collective-permute-done((bf16[256,640]{1,0:T(8,128)(2,1)S(1)}, bf16[256,640]{1,0:T(8,128)(2,1)S(1)}, u32[]{:S(2)}, u32[]{:S(2)}) %collective-permute-start.4) | collective-permute-done | bytes 327712 | tf_op jit(solution)/shard_map/ppermute | solution.py:31
  39.1 2.0 %collective-permute-start.5 = (bf16[256,1280]{1,0:T(8,128)(2,1)S(1)}, bf16[256,1280]{1,0:T(8,128)(2,1)S(1)}, u32[]{:S(2)}, u32[]{:S(2)}) collective-permute-start(bf16[256,1280]{1,0:T(8,128)(2,1)S(1)} %shard_map.90.mine_ref), channel_id=1, source_target_pairs={{0,1},{1,0},{2,3},{3,2},{4,5},{5,4},{6,7},{7,6},{8,9},{9,8},{10,11... | collective-permute-start | bytes 1966088 | tf_op jit(solution)/shard_map/ppermute | solution.py:31
  41.0 2.0 %collective-permute-done.5.packed_ref.theirs_ref = bf16[256,1280]{1,0:T(8,128)(2,1)S(1)} collective-permute-done((bf16[256,1280]{1,0:T(8,128)(2,1)S(1)}, bf16[256,1280]{1,0:T(8,128)(2,1)S(1)}, u32[]{:S(2)}, u32[]{:S(2)}) %collective-permute-start.5) | collective-permute-done | bytes 655392 | tf_op jit(solution)/shard_map/ppermute | solution.py:31
  43.8 17.4 %all_to_all.10 = bf16[16,12,16,128]{3,2,1,0:T(8,128)(2,1)} all-to-all(bf16[16,12,16,128]{3,2,1,0:T(8,128)(2,1)S(1)} %shard_map.92), channel_id=1, replica_groups={{0,2,4,6,128,130,132,134,256,258,260,262,384,386,388,390},{1,3,5,7,129,..., dimensions={0} | all-to-all | bytes 1572864 | tf_op jit(solution)/shard_map/all_to_all | solution.py:35
  62.4 10.1 %collective-permute-start.7 = (bf16[12,16,128]{2,1,0:T(8,128)(2,1)S(1)}, bf16[12,16,128]{2,1,0:T(8,128)(2,1)S(1)}, u32[]{:S(2)}, u32[]{:S(2)}) collective-permute-start(bf16[12,16,128]{2,1,0:T(8,128)(2,1)S(1)} %reduce_sum.12), channel_id=1, source_target_pairs={{0,120},{1,121},{2,122},{3,123},{4,124},{5,125},{6,126},{7,127},{8... | collective-permute-start | bytes 147464 | tf_op jit(solution)/shard_map/ppermute | solution.py:31
  72.5 3.9 %collective-permute-start.6 = (bf16[256,640]{1,0:T(8,128)(2,1)S(1)}, bf16[256,640]{1,0:T(8,128)(2,1)S(1)}, u32[]{:S(2)}, u32[]{:S(2)}) collective-permute-start(bf16[256,640]{1,0:T(8,128)(2,1)S(1)} %get-tuple-element.24.rows_ref), channel_id=1, source_target_pairs={{0,7},{1,6},{2,5},{3,4},{4,3},{5,2},{6,1},{7,0},{8,15},{9,14},{10,... | collective-permute-start | bytes 983048 | tf_op jit(solution)/shard_map/ppermute | solution.py:31
  76.5 4.2 %collective-permute-start.8 = (bf16[256,640]{1,0:T(8,128)(2,1)S(1)}, bf16[256,640]{1,0:T(8,128)(2,1)S(1)}, u32[]{:S(2)}, u32[]{:S(2)}) collective-permute-start(bf16[256,640]{1,0:T(8,128)(2,1)S(1)} %get-tuple-element.24.rows_ref), channel_id=1, source_target_pairs={{0,15},{1,14},{2,13},{3,12},{4,11},{5,10},{6,9},{7,8},{8,7},{9,6},... | collective-permute-start | bytes 983048 | tf_op jit(solution)/shard_map/ppermute | solution.py:31
  80.7 1.5 %convolution_convert_fusion = bf16[256,1152]{1,0:T(8,128)(2,1)} fusion(bf16[1152,640]{1,0:T(8,128)(2,1)S(1)} %copy-done.4, bf16[256,1280]{1,0:T(8,128)(2,1)S(1)} %shard_map.90.mine_ref), kind=kOutput, calls=%fused_computation | convolution fusion | flops 377782272 | bytes 2392064 | tf_op jit(solution)/shard_map/dot_general | solution.py:47
  82.2 9.6 %collective-permute-done.6.b_ref = bf16[256,640]{1,0:T(8,128)(2,1)S(1)} collective-permute-done((bf16[256,640]{1,0:T(8,128)(2,1)S(1)}, bf16[256,640]{1,0:T(8,128)(2,1)S(1)}, u32[]{:S(2)}, u32[]{:S(2)}) %collective-permute-start.6) | collective-permute-done | bytes 327712 | tf_op jit(solution)/shard_map/ppermute | solution.py:31
  91.8 7.9 %collective-permute-start.9 = (bf16[12,16,128]{2,1,0:T(8,128)(2,1)S(1)}, bf16[12,16,128]{2,1,0:T(8,128)(2,1)S(1)}, u32[]{:S(2)}, u32[]{:S(2)}) collective-permute-start(bf16[12,16,128]{2,1,0:T(8,128)(2,1)S(1)} %add_convert_fusion.3), channel_id=1, source_target_pairs={{0,32},{1,33},{2,34},{3,35},{4,36},{5,37},{6,38},{7,39},{8,40},{9,... | collective-permute-start | bytes 147464 | tf_op jit(solution)/shard_map/ppermute | solution.py:31
  101.2 4.4 %collective-permute-start.10 = (bf16[12,16,128]{2,1,0:T(8,128)(2,1)S(1)}, bf16[12,16,128]{2,1,0:T(8,128)(2,1)S(1)}, u32[]{:S(2)}, u32[]{:S(2)}) collective-permute-start(bf16[12,16,128]{2,1,0:T(8,128)(2,1)S(1)} %add_convert_fusion.2), channel_id=1, source_target_pairs={{0,16},{1,17},{2,18},{3,19},{4,20},{5,21},{6,22},{7,23},{8,24},{9,... | collective-permute-start | bytes 147464 | tf_op jit(solution)/shard_map/ppermute | solution.py:31
  105.6 1.5 %collective-permute-done.10 = bf16[12,16,128]{2,1,0:T(8,128)(2,1)S(1)} collective-permute-done((bf16[12,16,128]{2,1,0:T(8,128)(2,1)S(1)}, bf16[12,16,128]{2,1,0:T(8,128)(2,1)S(1)}, u32[]{:S(2)}, u32[]{:S(2)}) %collective-permute-start.10) | collective-permute-done | bytes 49184 | tf_op jit(solution)/shard_map/ppermute | solution.py:31
  107.1 3.4 %collective-permute-start.11 = (bf16[12,16,128]{2,1,0:T(8,128)(2,1)S(1)}, bf16[12,16,128]{2,1,0:T(8,128)(2,1)S(1)}, u32[]{:S(2)}, u32[]{:S(2)}) collective-permute-start(bf16[12,16,128]{2,1,0:T(8,128)(2,1)S(1)} %add_convert_fusion.1), channel_id=1, source_target_pairs={{0,8},{1,9},{2,10},{3,11},{4,12},{5,13},{6,14},{7,15},{8,0},{9,1},... | collective-permute-start | bytes 147464 | tf_op jit(solution)/shard_map/ppermute | solution.py:31
  110.5 1.5 %collective-permute-done.11 = bf16[12,16,128]{2,1,0:T(8,128)(2,1)S(1)} collective-permute-done((bf16[12,16,128]{2,1,0:T(8,128)(2,1)S(1)}, bf16[12,16,128]{2,1,0:T(8,128)(2,1)S(1)}, u32[]{:S(2)}, u32[]{:S(2)}) %collective-permute-start.11) | collective-permute-done | bytes 49184 | tf_op jit(solution)/shard_map/ppermute | solution.py:31
  112.2 14.3 %all_to_all.11.mine_ref = bf16[16,12,16,128]{3,2,1,0:T(8,128)(2,1)S(1)} all-to-all(bf16[16,12,16,128]{3,2,1,0:T(8,128)(2,1)S(1)} %broadcast_in_dim.14), channel_id=1, replica_groups={{0,2,4,6,128,130,132,134,256,258,260,262,384,386,388,390},{1,3,5,7,129,..., dimensions={0} | all-to-all | bytes 1572864 | tf_op jit(solution)/shard_map/all_to_all | solution.py:35
  126.4 8.6 %collective-permute-start.12 = (bf16[16,12,16,128]{3,2,1,0:T(8,128)(2,1)S(1)}, bf16[16,12,16,128]{3,2,1,0:T(8,128)(2,1)S(1)}, u32[]{:S(2)}, u32[]{:S(2)}) collective-permute-start(bf16[16,12,16,128]{3,2,1,0:T(8,128)(2,1)S(1)} %all_to_all.11.mine_ref), channel_id=1, source_target_pairs={{0,1},{1,0},{2,3},{3,2},{4,5},{5,4},{6,7},{7,6},{8,9},{9,8},{10,11... | collective-permute-start | bytes 2359304 | tf_op jit(solution)/shard_map/ppermute | solution.py:31
  135.1 2.3 %shard_map.93 = bf16[256,640]{1,0:T(8,128)(2,1)} custom-call(f32[1]{0:T(128)S(6)} %exp.3.scale_ref, f32[1]{0:T(128)S(6)} %copy.10.bias_ref, f32[256,640]{1,0:T(8,128)S(1)} %shard_map.91.total_ref, bf16[256,640]{1,0:T(8,128)(2,1)S(1)} %get-tuple-element.15.txt_ref.rows_ref, bf16[256,640]{1,0:T(8,128)(2,1)S(1)} %copy-done.10, ...), custom_call_target="tpu_custom_call" | custom-call | flops 503316480 | bytes 100000 | tf_op jit(solution)/shard_map/pallas_call | solution.py:53
  (45 shorter events, 13.7 us)
Async XLA Ops:
  0.6 1.1 copy-start
  1.7 1.0 copy-start.5
  2.8 26.3 %collective-permute-start.2 = (bf16[256,1280]{1,0:T(8,128)(2,1)S(1)}, bf16[256,1280]{1,0:T(8,128)(2,1)S(1)}, u32[]{:S(2)}, u32[]{:S(2)}) collective-permute-start(bf16[256,1280]{1,0:T(8,128)(2,1)S(1)} %get-tuple-element.18), channel_id=1, source_target_pairs={{0,1},{1,0},{2,3},{3,2},{4,5},{5,4},{6,7},{7,6},{8,9},{9,8},{10,11... | collective-permute-start | bytes 1966088 | tf_op jit(solution)/shard_map/ppermute | solution.py:31
  11.6 16.2 %collective-permute-start = (bf16[256,640]{1,0:T(8,128)(2,1)S(1)}, bf16[256,640]{1,0:T(8,128)(2,1)S(1)}, u32[]{:S(2)}, u32[]{:S(2)}) collective-permute-start(bf16[256,640]{1,0:T(8,128)(2,1)S(1)} %get-tuple-element.15.txt_ref.rows_ref), channel_id=1, source_target_pairs={{0,15},{1,14},{2,13},{3,12},{4,11},{5,10},{6,9},{7,8},{8,7},{9,6},... | collective-permute-start | bytes 983048 | tf_op jit(solution)/shard_map/ppermute | solution.py:31
  13.6 14.9 %collective-permute-start.1 = (bf16[256,640]{1,0:T(8,128)(2,1)S(1)}, bf16[256,640]{1,0:T(8,128)(2,1)S(1)}, u32[]{:S(2)}, u32[]{:S(2)}) collective-permute-start(bf16[256,640]{1,0:T(8,128)(2,1)S(1)} %get-tuple-element.15.txt_ref.rows_ref), channel_id=1, source_target_pairs={{0,3},{1,2},{2,1},{3,0},{4,7},{5,6},{6,5},{7,4},{8,11},{9,10},{10,... | collective-permute-start | bytes 983048 | tf_op jit(solution)/shard_map/ppermute | solution.py:31
  16.8 1.1 copy-start.1
  17.9 1.4 copy-start.3
  21.4 0.8 copy-start.7
  22.2 11.5 %collective-permute-start.3 = (bf16[256,640]{1,0:T(8,128)(2,1)S(1)}, bf16[256,640]{1,0:T(8,128)(2,1)S(1)}, u32[]{:S(2)}, u32[]{:S(2)}) collective-permute-start(bf16[256,640]{1,0:T(8,128)(2,1)S(1)} %get-tuple-element.24.rows_ref), channel_id=1, source_target_pairs={{0,3},{1,2},{2,1},{3,0},{4,7},{5,6},{6,5},{7,4},{8,11},{9,10},{10,... | collective-permute-start | bytes 983048 | tf_op jit(solution)/shard_map/ppermute | solution.py:31
  25.9 12.4 %collective-permute-start.4 = (bf16[256,640]{1,0:T(8,128)(2,1)S(1)}, bf16[256,640]{1,0:T(8,128)(2,1)S(1)}, u32[]{:S(2)}, u32[]{:S(2)}) collective-permute-start(bf16[256,640]{1,0:T(8,128)(2,1)S(1)} %get-tuple-element.15.txt_ref.rows_ref), channel_id=1, source_target_pairs={{0,7},{1,6},{2,5},{3,4},{4,3},{5,2},{6,1},{7,0},{8,15},{9,14},{10,... | collective-permute-start | bytes 983048 | tf_op jit(solution)/shard_map/ppermute | solution.py:31
  29.8 13.3 %copy-start.2 = (bf16[256,1152]{1,0:T(8,128)(2,1)S(1)}, bf16[256,1152]{1,0:T(8,128)(2,1)}, u32[]{:S(2)}) copy-start(bf16[256,1152]{1,0:T(8,128)(2,1)} %feat_ref.5) | copy-start | bytes 1769476
  33.8 10.0 %copy-start.9 = (bf16[256,640]{1,0:T(8,128)(2,1)}, bf16[256,640]{1,0:T(8,128)(2,1)S(1)}, u32[]{:S(2)}) copy-start(bf16[256,640]{1,0:T(8,128)(2,1)S(1)} %collective-permute-done.3.a_ref) | copy-start | bytes 983044
  39.1 4.0 %collective-permute-start.5 = (bf16[256,1280]{1,0:T(8,128)(2,1)S(1)}, bf16[256,1280]{1,0:T(8,128)(2,1)S(1)}, u32[]{:S(2)}, u32[]{:S(2)}) collective-permute-start(bf16[256,1280]{1,0:T(8,128)(2,1)S(1)} %shard_map.90.mine_ref), channel_id=1, source_target_pairs={{0,1},{1,0},{2,3},{3,2},{4,5},{5,4},{6,7},{7,6},{8,9},{9,8},{10,11... | collective-permute-start | bytes 1966088 | tf_op jit(solution)/shard_map/ppermute | solution.py:31
  43.8 36.9 %copy-start.4 = (bf16[1152,640]{1,0:T(8,128)(2,1)S(1)}, bf16[1152,640]{1,0:T(8,128)(2,1)}, u32[]{:S(2)}) copy-start(bf16[1152,640]{1,0:T(8,128)(2,1)} %head_ref.1) | copy-start | bytes 4423684
  62.4 37.3 %copy-start.8 = (f32[256,640]{1,0:T(8,128)S(1)}, f32[256,640]{1,0:T(8,128)}, u32[]{:S(2)}) copy-start(f32[256,640]{1,0:T(8,128)} %copy-done.7) | copy-start | bytes 1966084
  62.4 14.0 %collective-permute-start.7 = (bf16[12,16,128]{2,1,0:T(8,128)(2,1)S(1)}, bf16[12,16,128]{2,1,0:T(8,128)(2,1)S(1)}, u32[]{:S(2)}, u32[]{:S(2)}) collective-permute-start(bf16[12,16,128]{2,1,0:T(8,128)(2,1)S(1)} %reduce_sum.12), channel_id=1, source_target_pairs={{0,120},{1,121},{2,122},{3,123},{4,124},{5,125},{6,126},{7,127},{8... | collective-permute-start | bytes 147464 | tf_op jit(solution)/shard_map/ppermute | solution.py:31
  72.5 19.3 %collective-permute-start.6 = (bf16[256,640]{1,0:T(8,128)(2,1)S(1)}, bf16[256,640]{1,0:T(8,128)(2,1)S(1)}, u32[]{:S(2)}, u32[]{:S(2)}) collective-permute-start(bf16[256,640]{1,0:T(8,128)(2,1)S(1)} %get-tuple-element.24.rows_ref), channel_id=1, source_target_pairs={{0,7},{1,6},{2,5},{3,4},{4,3},{5,2},{6,1},{7,0},{8,15},{9,14},{10,... | collective-permute-start | bytes 983048 | tf_op jit(solution)/shard_map/ppermute | solution.py:31
  76.5 24.8 %collective-permute-start.8 = (bf16[256,640]{1,0:T(8,128)(2,1)S(1)}, bf16[256,640]{1,0:T(8,128)(2,1)S(1)}, u32[]{:S(2)}, u32[]{:S(2)}) collective-permute-start(bf16[256,640]{1,0:T(8,128)(2,1)S(1)} %get-tuple-element.24.rows_ref), channel_id=1, source_target_pairs={{0,15},{1,14},{2,13},{3,12},{4,11},{5,10},{6,9},{7,8},{8,7},{9,6},... | collective-permute-start | bytes 983048 | tf_op jit(solution)/shard_map/ppermute | solution.py:31
  91.8 9.4 %collective-permute-start.9 = (bf16[12,16,128]{2,1,0:T(8,128)(2,1)S(1)}, bf16[12,16,128]{2,1,0:T(8,128)(2,1)S(1)}, u32[]{:S(2)}, u32[]{:S(2)}) collective-permute-start(bf16[12,16,128]{2,1,0:T(8,128)(2,1)S(1)} %add_convert_fusion.3), channel_id=1, source_target_pairs={{0,32},{1,33},{2,34},{3,35},{4,36},{5,37},{6,38},{7,39},{8,40},{9,... | collective-permute-start | bytes 147464 | tf_op jit(solution)/shard_map/ppermute | solution.py:31
  100.4 34.6 %copy-start.6 = (bf16[256,640]{1,0:T(8,128)(2,1)S(1)}, bf16[256,640]{1,0:T(8,128)(2,1)}, u32[]{:S(2)}) copy-start(bf16[256,640]{1,0:T(8,128)(2,1)} %txt_ref.3) | copy-start | bytes 983044
  100.4 34.6 %copy-start.10 = (bf16[256,640]{1,0:T(8,128)(2,1)S(1)}, bf16[256,640]{1,0:T(8,128)(2,1)}, u32[]{:S(2)}) copy-start(bf16[256,640]{1,0:T(8,128)(2,1)} %copy-done.9) | copy-start | bytes 983044
  101.2 5.8 %collective-permute-start.10 = (bf16[12,16,128]{2,1,0:T(8,128)(2,1)S(1)}, bf16[12,16,128]{2,1,0:T(8,128)(2,1)S(1)}, u32[]{:S(2)}, u32[]{:S(2)}) collective-permute-start(bf16[12,16,128]{2,1,0:T(8,128)(2,1)S(1)} %add_convert_fusion.2), channel_id=1, source_target_pairs={{0,16},{1,17},{2,18},{3,19},{4,20},{5,21},{6,22},{7,23},{8,24},{9,... | collective-permute-start | bytes 147464 | tf_op jit(solution)/shard_map/ppermute | solution.py:31
  107.1 4.9 %collective-permute-start.11 = (bf16[12,16,128]{2,1,0:T(8,128)(2,1)S(1)}, bf16[12,16,128]{2,1,0:T(8,128)(2,1)S(1)}, u32[]{:S(2)}, u32[]{:S(2)}) collective-permute-start(bf16[12,16,128]{2,1,0:T(8,128)(2,1)S(1)} %add_convert_fusion.1), channel_id=1, source_target_pairs={{0,8},{1,9},{2,10},{3,11},{4,12},{5,13},{6,14},{7,15},{8,0},{9,1},... | collective-permute-start | bytes 147464 | tf_op jit(solution)/shard_map/ppermute | solution.py:31
  126.4 10.9 %collective-permute-start.12 = (bf16[16,12,16,128]{3,2,1,0:T(8,128)(2,1)S(1)}, bf16[16,12,16,128]{3,2,1,0:T(8,128)(2,1)S(1)}, u32[]{:S(2)}, u32[]{:S(2)}) collective-permute-start(bf16[16,12,16,128]{3,2,1,0:T(8,128)(2,1)S(1)} %all_to_all.11.mine_ref), channel_id=1, source_target_pairs={{0,1},{1,0},{2,3},{3,2},{4,5},{5,4},{6,7},{7,6},{8,9},{9,8},{10,11... | collective-permute-start | bytes 2359304 | tf_op jit(solution)/shard_map/ppermute | solution.py:31
  (1 other events, 0.7 us)

commit v3 on v2

--- a/solution.py
+++ b/solution.py
@@ -24,6 +24,7 @@
 
 
 PLANE = group((1, 2, 7, 8))
+LINE = group((3, 4, 5, 6))
 
 
 def swap(value, mask):
@@ -31,8 +32,8 @@
     return lax.ppermute(value, "dp", pairs)
 
 
-def exchange(value):
-    return lax.all_to_all(value, "dp", 0, 0, axis_index_groups=PLANE, tiled=True)
+def exchange(value, members):
+    return lax.all_to_all(value, "dp", 0, 0, axis_index_groups=members, tiled=True)
 
 
 def after(value, *others):
@@ -69,18 +70,14 @@
     return ((d_unit - unit * jnp.sum(unit * d_unit, axis=-1, keepdims=True)) * inverse).astype(BF16)
 
 
-def text_kernel(core_ref, txt_ref, feat_ref, rows_ref, packed_ref):
+def text_kernel(txt_ref, rows_ref):
     value = txt_ref[...].astype(F32)
-    rows = (value * inverse_norm(value)).astype(BF16)
-    rows_ref[...] = rows
-    packed_ref[:, :E] = rows
-    start = pl.multiple_of(512 * (1 - core_ref[0]), 128)
-    packed_ref[:, E:] = feat_ref[:, pl.ds(start, E)]
+    rows_ref[...] = (value * inverse_norm(value)).astype(BF16)
 
 
 def image_kernel(
-    scale_ref, bias_ref, labels_ref, feat_ref, head_ref, txt_ref,
-    unit_ref, inverse_ref, rows_ref, d_img_ref, d_txt_ref,
+    core_ref, scale_ref, bias_ref, labels_ref, feat_ref, head_ref, txt_ref,
+    unit_ref, inverse_ref, rows_ref, d_img_ref, d_txt_ref, other_ref,
 ):
     proj = dot(feat_ref[...], head_ref[...])
     inverse = inverse_norm(proj)
@@ -96,6 +93,7 @@
     grad = (-sign * jax.nn.sigmoid(-sign * logits)).astype(BF16)
     d_img_ref[...] = dot(grad, txt)
     d_txt_ref[...] = dot(grad, rows, 0, 0)
+    other_ref[...] = feat_ref[:, pl.ds(pl.multiple_of(512 * (1 - core_ref[0]), 128), E)]
 
 
 def pair_term(scale_ref, bias_ref, rows, others):
@@ -105,11 +103,6 @@
 
 def pair_kernel(scale_ref, bias_ref, total_ref, rows_ref, other_ref, out_ref):
     out_ref[...] = total_ref[...] + pair_term(scale_ref, bias_ref, rows_ref[...], other_ref[...])
-
-
-def packed_text_kernel(scale_ref, bias_ref, total_ref, rows_ref, packed_ref, out_ref):
-    term = pair_term(scale_ref, bias_ref, rows_ref[...], packed_ref[:, :E])
-    out_ref[...] = total_ref[...] + term
 
 
 def image_end_kernel(
@@ -121,13 +114,11 @@
     packed_ref[:, E:] = rows
 
 
-def packed_image_kernel(scale_ref, bias_ref, total_ref, rows_ref, packed_ref, out_ref):
-    out_ref[...] = total_ref[...] + pair_term(scale_ref, bias_ref, rows_ref[...], packed_ref[:, E:])
-
-
-def text_end_kernel(scale_ref, bias_ref, total_ref, rows_ref, a_ref, b_ref, c_ref, txt_ref, out_ref):
+def text_end_kernel(
+    scale_ref, bias_ref, total_ref, rows_ref, packed_ref, a_ref, b_ref, c_ref, txt_ref, out_ref
+):
     rows = rows_ref[...]
-    total = total_ref[...]
+    total = total_ref[...] + pair_term(scale_ref, bias_ref, rows, packed_ref[:, E:])
     for other_ref in (a_ref, b_ref, c_ref):
         total = total + pair_term(scale_ref, bias_ref, rows, other_ref[...])
     value = txt_ref[...].astype(F32)
@@ -135,13 +126,29 @@
     out_ref[...] = tangent(scale_ref[0] * total, value * inverse, inverse)
 
 
+def sum_of(parts_ref):
+    total = parts_ref[0].astype(F32)
+    for k in range(1, OWNERS):
+        total = total + parts_ref[k].astype(F32)
+    return total.astype(BF16)
+
+
+def plane_sum_kernel(parts_ref, out_ref):
+    out_ref[:SLABS] = sum_of(parts_ref)
+    out_ref[SLABS:] = jnp.zeros((OWNERS - SLABS, 16, 128), BF16)
+
+
+def line_sum_kernel(parts_ref, out_ref):
+    out_ref[...] = jnp.broadcast_to(sum_of(parts_ref)[None], (OWNERS, 16, 128))
+
+
 def head_kernel(core_ref, feat_ref, other_feat_ref, mine_ref, theirs_ref, out_ref):
     core = core_ref[0]
     mine, theirs = mine_ref[:, :E], theirs_ref[:, :E]
 
     def product(column):
         here = pl.multiple_of(column, 128)
-        there = pl.multiple_of(E + column - 512 * core, 128)
+        there = pl.multiple_of(column - 512 * core, 128)
         total = dot(feat_ref[:, pl.ds(here, 128)], mine, 0, 0)
         return total + dot(other_feat_ref[:, pl.ds(there, 128)], theirs, 0, 0)
 
@@ -189,53 +196,40 @@
     block16 = shape(ROWS, E, dtype=BF16)
 
     pair16 = shape(ROWS, 2 * E, dtype=BF16)
-    txt_rows, packed_txt = call(
-        text_kernel, (block16, pair16), [SMEM, VMEM, VMEM], 1000000, core, txt_emb, img_feat
-    )
-    txt_15 = swap(txt_rows, 15)
-    txt_7 = swap(txt_rows, 7)
-    txt_3 = swap(txt_rows, 3)
-    packed_txt = swap(packed_txt, 1)
-
-    unit, inverse, img_rows, d_img, d_txt = call(
+    txt_rows = call(text_kernel, block16, [VMEM], 1000000, txt_emb)
+    text = {c: swap(txt_rows, c) for c in (15, 3, 1, 7)}
+
+    unit, inverse, img_rows, d_img, d_txt, other_feat = call(
         image_kernel,
-        (block, shape(ROWS, 1), block16, block, block),
-        [SMEM, SMEM, VMEM, VMEM, VMEM, VMEM],
+        (block, shape(ROWS, 1), block16, block, block, block16),
+        [SMEM, SMEM, SMEM, VMEM, VMEM, VMEM, VMEM],
         12 * pair,
-        scale, bias, labels[None, :], img_feat, head_weight, txt_rows,
-    )
+        core, scale, bias, labels[None, :], img_feat, head_weight, txt_rows,
+    )
+    other_feat = swap(other_feat, 1)
     pair_specs = [SMEM, SMEM, VMEM, VMEM, VMEM]
-    for kernel, other in (
-        (pair_kernel, txt_15), (pair_kernel, txt_3), (packed_text_kernel, packed_txt),
-    ):
-        d_img = call(kernel, block, pair_specs, little, scale, bias, d_img, img_rows, other)
-    img_3 = swap(img_rows, 3)
-    d_img = after(d_img, img_3)
+    for c in (15, 3, 1):
+        d_img = call(pair_kernel, block, pair_specs, little, scale, bias, d_img, img_rows, text[c])
     packed_img = call(
         image_end_kernel, pair16, pair_specs + [VMEM, VMEM], little,
-        scale, bias, d_img, img_rows, txt_7, unit, inverse,
-    )
-    other_img = swap(packed_img, 1)
+        scale, bias, d_img, img_rows, text[7], unit, inverse,
+    )
+    other_img = swap(after(packed_img, other_feat), 1)
+    d_img_feat = dot(packed_img[:, :E], head_weight, 1, 1).astype(BF16)
 
     parts = call(
         head_kernel, shape(OWNERS, SLABS, 16, 128, dtype=BF16), [SMEM] + [VMEM] * 4,
-        4 * ROWS * D * E // 2, core, img_feat, packed_txt, packed_img, other_img,
-    )
-    total = jnp.sum(exchange(parts).astype(F32), axis=0)
-    d_img_feat = dot(packed_img[:, :E], head_weight, 1, 1).astype(BF16)
-    d_txt = call(
-        packed_image_kernel, block, pair_specs, 2 * pair,
-        scale, bias, d_txt, txt_rows, other_img,
-    )
-    images = [img_3]
-    for z, beside, c in ((15, None, 7), (4, d_img_feat, 15), (2, d_txt, None), (1, None, None)):
-        mine = total.astype(BF16)
-        sent = mine if beside is None else after(mine, beside, *images)
-        if c is not None:
-            images.append(swap(after(img_rows, mine), c))
-        total = mine.astype(F32) + swap(sent, z * 8).astype(F32)
-    part = total.astype(BF16)
-    parts = exchange(after(jnp.broadcast_to(part[None], (OWNERS, SLABS, 16, 128))))
+        4 * ROWS * D * E // 2, core, img_feat, other_feat, packed_img, other_img,
+    )
+    parts = exchange(after(parts, d_img_feat), PLANE)
+    line = shape(OWNERS, 16, 128, dtype=BF16)
+    part = call(plane_sum_kernel, line, [VMEM], little, parts)
+    late = after(img_rows, part)
+    images = [swap(late, c) for c in (7, 15, 3)]
+    part = call(line_sum_kernel, line, [VMEM], little, exchange(part, LINE))
+    part = exchange(part, LINE)[:SLABS]
+    part = after(part, *images)
+    parts = exchange(after(jnp.broadcast_to(part[None], (OWNERS, SLABS, 16, 128))), PLANE)
     d_head = call(
         place_kernel, shape(D, E, dtype=BF16), [SMEM, VMEM, VMEM], 0,
         core, parts, swap(parts, 1),
@@ -244,8 +238,8 @@
     )
 
     d_txt_emb = call(
-        text_end_kernel, block16, pair_specs + [VMEM] * 3, 3 * pair,
-        scale, bias, d_txt, txt_rows, *images, txt_emb,
+        text_end_kernel, block16, pair_specs + [VMEM] * 4, 4 * pair,
+        scale, bias, d_txt, txt_rows, other_img, *images, txt_emb,
     )
     return (d_img_feat, d_txt_emb, d_head)
 

time: 139 us -> 126 us (0.906)
  blocking collectives: 31.6 us -> 59.1 us
  waiting for transfers between devices: 23.9 us -> 2.35 us
  starting transfers between devices: 62.6 us -> 46.7 us
  local copies, waits for them, and re-layouts: 6.15 us -> 4.24 us
    ppermute x13 -> x10, starting transfers between devices: 62.6 us -> 32.5 us  [swap(): return lax.ppermute(value, 'dp', pairs)]
    all_to_all x2 -> x3, blocking collectives: 31.6 us -> 59.1 us  [exchange(): lax.all_to_all(value, 'dp', 0, 0, axis_index_groups=members, tiled=True)]
    ppermute x13 -> x10, waiting for transfers between devices: 23.9 us -> 1.2 us  [swap(): return lax.ppermute(value, 'dp', pairs)]
    all_to_all x0 -> x1, starting transfers between devices: none -> 14.1 us  [exchange(): lax.all_to_all(value, 'dp', 0, 0, axis_index_groups=members, tiled=True)]
    unnamed x24 -> x14, local copies, waits for them, and re-layouts: 6.01 us -> 4.09 us
    pallas_call x10 -> x11, Pallas kernels: 9.15 us -> 9.67 us  [call(): pl.pallas_call(kernel, out_shape=out_shape, in_specs=specs, out_specs=out...]
  transfers between devices with their start and end apart: 13 -> 11, of which waited for: 7 -> 3; matrix products, arithmetic and copies ran while one was open for 1% -> 1% of each run, Pallas kernels for 5% -> 5%
where the time goes in v3:
time: 126 us
  blocking collectives  59.1 us (47%)
  starting transfers between devices  46.7 us (37%)
  Pallas kernels  9.67 us (8%)
  local copies, waits for them, and re-layouts  4.24 us (3%)
  waiting for transfers between devices  2.35 us (2%)
  between operations  2.21 us (2%)
  matrix products  1.48 us (1%)
    all_to_all x3, blocking collectives, exchange(): lax.all_to_all(value, 'dp', 0, 0, axis_index_groups=members, tiled=True)  59.1 us
    ppermute x10, starting transfers between devices, swap(): return lax.ppermute(value, 'dp', pairs)  32.5 us
    all_to_all x1, starting transfers between devices, exchange(): lax.all_to_all(value, 'dp', 0, 0, axis_index_groups=members, tiled=True)  14.1 us
    pallas_call x11, Pallas kernels, call(): pl.pallas_call(kernel, out_shape=out_shape, in_specs=specs, out_specs=out...  9.67 us
    unnamed x14, local copies, waits for them, and re-layouts  4.09 us
  transfers between devices with their start and end apart: 11, of which 3 were waited for; matrix products, arithmetic and copies ran while one was open for 1% of the time, Pallas kernels for 5%

profile of v3, /device:TPU:1, one launch (start us, length us, event | category | flops | bytes accessed | tf_op | source)
XLA Modules:
  0.0 125.7 jit_solution(7414265850542805253)
XLA Ops:
  0.6 1.0 copy-done.2
  1.8 7.1 %collective-permute-start = (bf16[256,640]{1,0:T(8,128)(2,1)S(1)}, bf16[256,640]{1,0:T(8,128)(2,1)S(1)}, u32[]{:S(2)}, u32[]{:S(2)}) collective-permute-start(bf16[256,640]{1,0:T(8,128)(2,1)S(1)} %shard_map.85.txt_ref.rows_ref), channel_id=1, source_target_pairs={{0,15},{1,14},{2,13},{3,12},{4,11},{5,10},{6,9},{7,8},{8,7},{9,6},... | collective-permute-start | bytes 983048 | tf_op jit(solution)/shard_map/ppermute | solution.py:32
  8.9 1.9 %collective-permute-start.1 = (bf16[256,640]{1,0:T(8,128)(2,1)S(1)}, bf16[256,640]{1,0:T(8,128)(2,1)S(1)}, u32[]{:S(2)}, u32[]{:S(2)}) collective-permute-start(bf16[256,640]{1,0:T(8,128)(2,1)S(1)} %shard_map.85.txt_ref.rows_ref), channel_id=1, source_target_pairs={{0,3},{1,2},{2,1},{3,0},{4,7},{5,6},{6,5},{7,4},{8,11},{9,10},{10,... | collective-permute-start | bytes 983048 | tf_op jit(solution)/shard_map/ppermute | solution.py:32
  10.8 3.6 %collective-permute-start.2 = (bf16[256,640]{1,0:T(8,128)(2,1)S(1)}, bf16[256,640]{1,0:T(8,128)(2,1)S(1)}, u32[]{:S(2)}, u32[]{:S(2)}) collective-permute-start(bf16[256,640]{1,0:T(8,128)(2,1)S(1)} %shard_map.85.txt_ref.rows_ref), channel_id=1, source_target_pairs={{0,1},{1,0},{2,3},{3,2},{4,5},{5,4},{6,7},{7,6},{8,9},{9,8},{10,11... | collective-permute-start | bytes 983048 | tf_op jit(solution)/shard_map/ppermute | solution.py:32
  14.4 1.9 %collective-permute-start.3 = (bf16[256,640]{1,0:T(8,128)(2,1)S(1)}, bf16[256,640]{1,0:T(8,128)(2,1)S(1)}, u32[]{:S(2)}, u32[]{:S(2)}) collective-permute-start(bf16[256,640]{1,0:T(8,128)(2,1)S(1)} %shard_map.85.txt_ref.rows_ref), channel_id=1, source_target_pairs={{0,7},{1,6},{2,5},{3,4},{4,3},{5,2},{6,1},{7,0},{8,15},{9,14},{10,... | collective-permute-start | bytes 983048 | tf_op jit(solution)/shard_map/ppermute | solution.py:32
  17.7 1.4 %copy-done = bf16[1152,640]{1,0:T(8,128)(2,1)S(1)} copy-done((bf16[1152,640]{1,0:T(8,128)(2,1)S(1)}, bf16[1152,640]{1,0:T(8,128)(2,1)}, u32[]{:S(2)}) %copy-start) | copy-done | bytes 1474584
  19.1 1.1 copy-done.4
  20.8 1.5 %shard_map.86 = (f32[256,640]{1,0:T(8,128)S(1)}, f32[256,1]{1,0:T(8,128)S(1)}, bf16[256,640]{1,0:T(8,128)(2,1)S(1)}, f32[256,640]{1,0:T(8,128)S(1)}, f32[256,640...) custom-call(s32[1]{0:T(128)} %bitcast.core_ref, f32[1]{0:T(128)S(6)} %exp.3.scale_ref, f32[1]{0:T(128)S(6)} %copy.10.bias_ref, ...), custom_call_target="tpu_custom_call" | custom-call | flops 2013265920 | bytes 100000 | tf_op jit(solution)/shard_map/pallas_call | solution.py:54
  22.3 1.9 %collective-permute-start.4 = (bf16[256,640]{1,0:T(8,128)(2,1)S(1)}, bf16[256,640]{1,0:T(8,128)(2,1)S(1)}, u32[]{:S(2)}, u32[]{:S(2)}) collective-permute-start(bf16[256,640]{1,0:T(8,128)(2,1)S(1)} %get-tuple-element.18), channel_id=1, source_target_pairs={{0,1},{1,0},{2,3},{3,2},{4,5},{5,4},{6,7},{7,6},{8,9},{9,8},{10,11... | collective-permute-start | bytes 983048 | tf_op jit(solution)/shard_map/ppermute | solution.py:32
  26.8 0.8 shard_map.90.mine_ref
  27.6 2.1 %collective-permute-start.5 = (bf16[256,1280]{1,0:T(8,128)(2,1)S(1)}, bf16[256,1280]{1,0:T(8,128)(2,1)S(1)}, u32[]{:S(2)}, u32[]{:S(2)}) collective-permute-start(bf16[256,1280]{1,0:T(8,128)(2,1)S(1)} %shard_map.90.mine_ref), channel_id=1, source_target_pairs={{0,1},{1,0},{2,3},{3,2},{4,5},{5,4},{6,7},{7,6},{8,9},{9,8},{10,11... | collective-permute-start | bytes 1966088 | tf_op jit(solution)/shard_map/ppermute | solution.py:32
  29.8 1.5 %convolution_convert_fusion = bf16[256,1152]{1,0:T(8,128)(2,1)} fusion(bf16[1152,640]{1,0:T(8,128)(2,1)S(1)} %copy-done.1, bf16[256,1280]{1,0:T(8,128)(2,1)S(1)} %shard_map.90.mine_ref), kind=kOutput, calls=%fused_computation | convolution fusion | flops 377782272 | bytes 2392064 | tf_op jit(solution)/shard_map/dot_general | solution.py:48
  32.5 19.5 %all_to_all.20.parts_ref = bf16[16,12,16,128]{3,2,1,0:T(8,128)(2,1)S(1)} all-to-all(bf16[16,12,16,128]{3,2,1,0:T(8,128)(2,1)S(1)} %shard_map.91), channel_id=1, replica_groups={{0,2,4,6,128,130,132,134,256,258,260,262,384,386,388,390},{1,3,5,7,129,..., dimensions={0} | all-to-all | bytes 1572864 | tf_op jit(solution)/shard_map/all_to_all | solution.py:36
  52.0 0.7 shard_map.92
  52.8 14.1 %all-to-all-start.1 = ((bf16[16,16,128]{2,1,0:T(8,128)(2,1)}), bf16[16,16,128]{2,1,0:T(8,128)(2,1)S(1)}, u32[]{:S(2)}, u32[]{:S(2)}) async-start(bf16[16,16,128]{2,1,0:T(8,128)(2,1)} %shard_map.92), calls=%async_computation.1 | async-start | bytes 131072 | tf_op jit(solution)/shard_map/all_to_all | solution.py:36
  66.9 3.6 %collective-permute-start.6 = (bf16[256,640]{1,0:T(8,128)(2,1)S(1)}, bf16[256,640]{1,0:T(8,128)(2,1)S(1)}, u32[]{:S(2)}, u32[]{:S(2)}) collective-permute-start(bf16[256,640]{1,0:T(8,128)(2,1)S(1)} %get-tuple-element.21.rows_ref), channel_id=1, source_target_pairs={{0,7},{1,6},{2,5},{3,4},{4,3},{5,2},{6,1},{7,0},{8,15},{9,14},{10,... | collective-permute-start | bytes 983048 | tf_op jit(solution)/shard_map/ppermute | solution.py:32
  70.5 4.2 %collective-permute-start.7 = (bf16[256,640]{1,0:T(8,128)(2,1)S(1)}, bf16[256,640]{1,0:T(8,128)(2,1)S(1)}, u32[]{:S(2)}, u32[]{:S(2)}) collective-permute-start(bf16[256,640]{1,0:T(8,128)(2,1)S(1)} %get-tuple-element.21.rows_ref), channel_id=1, source_target_pairs={{0,15},{1,14},{2,13},{3,12},{4,11},{5,10},{6,9},{7,8},{8,7},{9,6},... | collective-permute-start | bytes 983048 | tf_op jit(solution)/shard_map/ppermute | solution.py:32
  74.8 2.7 %collective-permute-start.8 = (bf16[256,640]{1,0:T(8,128)(2,1)S(1)}, bf16[256,640]{1,0:T(8,128)(2,1)S(1)}, u32[]{:S(2)}, u32[]{:S(2)}) collective-permute-start(bf16[256,640]{1,0:T(8,128)(2,1)S(1)} %get-tuple-element.21.rows_ref), channel_id=1, source_target_pairs={{0,3},{1,2},{2,1},{3,0},{4,7},{5,6},{6,5},{7,4},{8,11},{9,10},{10,... | collective-permute-start | bytes 983048 | tf_op jit(solution)/shard_map/ppermute | solution.py:32
  77.5 1.2 all-to-all-done.1.parts_ref
  78.7 20.6 %all_to_all.21 = bf16[16,16,128]{2,1,0:T(8,128)(2,1)S(1)} all-to-all(bf16[16,16,128]{2,1,0:T(8,128)(2,1)S(1)} %shard_map.94), channel_id=1, replica_groups={{0,8,16,24,32,40,48,56,64,72,80,88,96,104,112,120},{1,9,17,25,33,41,49,..., dimensions={0} | all-to-all | bytes 131072 | tf_op jit(solution)/shard_map/all_to_all | solution.py:36
  99.5 19.0 %all_to_all.22.mine_ref = bf16[16,12,16,128]{3,2,1,0:T(8,128)(2,1)S(1)} all-to-all(bf16[16,12,16,128]{3,2,1,0:T(8,128)(2,1)S(1)} %broadcast_in_dim.14), channel_id=1, replica_groups={{0,2,4,6,128,130,132,134,256,258,260,262,384,386,388,390},{1,3,5,7,129,..., dimensions={0} | all-to-all | bytes 1572864 | tf_op jit(solution)/shard_map/all_to_all | solution.py:36
  118.4 3.4 %collective-permute-start.9 = (bf16[16,12,16,128]{3,2,1,0:T(8,128)(2,1)S(1)}, bf16[16,12,16,128]{3,2,1,0:T(8,128)(2,1)S(1)}, u32[]{:S(2)}, u32[]{:S(2)}) collective-permute-start(bf16[16,12,16,128]{3,2,1,0:T(8,128)(2,1)S(1)} %all_to_all.22.mine_ref), channel_id=1, source_target_pairs={{0,1},{1,0},{2,3},{3,2},{4,5},{5,4},{6,7},{7,6},{8,9},{9,8},{10,11... | collective-permute-start | bytes 2359304 | tf_op jit(solution)/shard_map/ppermute | solution.py:32
  121.9 2.7 %shard_map.93 = bf16[256,640]{1,0:T(8,128)(2,1)} custom-call(f32[1]{0:T(128)S(6)} %exp.3.scale_ref, f32[1]{0:T(128)S(6)} %copy.10.bias_ref, f32[256,640]{1,0:T(8,128)S(1)} %get-tuple-element.17.total_ref, bf16[256,640]{1,0:T(8,128)(2,1)S(1)} %shard_map.85.txt_ref.rows_ref, bf16[256,1280]{1,0:T(8,128)(2,1)S(1)} %collective-permute-done.5.theirs_ref.packed_ref, ...), custom_call_target="tpu_custom_call" | custom-call | flops 671088640 | bytes 100000 | tf_op jit(solution)/shard_map/pallas_call | solution.py:54
  124.5 1.2 shard_map.95
  (29 shorter events, 4.9 us)
Async XLA Ops:
  0.6 1.0 copy-start.2
  1.8 22.4 %collective-permute-start = (bf16[256,640]{1,0:T(8,128)(2,1)S(1)}, bf16[256,640]{1,0:T(8,128)(2,1)S(1)}, u32[]{:S(2)}, u32[]{:S(2)}) collective-permute-start(bf16[256,640]{1,0:T(8,128)(2,1)S(1)} %shard_map.85.txt_ref.rows_ref), channel_id=1, source_target_pairs={{0,15},{1,14},{2,13},{3,12},{4,11},{5,10},{6,9},{7,8},{8,7},{9,6},... | collective-permute-start | bytes 983048 | tf_op jit(solution)/shard_map/ppermute | solution.py:32
  8.9 16.0 %collective-permute-start.1 = (bf16[256,640]{1,0:T(8,128)(2,1)S(1)}, bf16[256,640]{1,0:T(8,128)(2,1)S(1)}, u32[]{:S(2)}, u32[]{:S(2)}) collective-permute-start(bf16[256,640]{1,0:T(8,128)(2,1)S(1)} %shard_map.85.txt_ref.rows_ref), channel_id=1, source_target_pairs={{0,3},{1,2},{2,1},{3,0},{4,7},{5,6},{6,5},{7,4},{8,11},{9,10},{10,... | collective-permute-start | bytes 983048 | tf_op jit(solution)/shard_map/ppermute | solution.py:32
  10.8 14.7 %collective-permute-start.2 = (bf16[256,640]{1,0:T(8,128)(2,1)S(1)}, bf16[256,640]{1,0:T(8,128)(2,1)S(1)}, u32[]{:S(2)}, u32[]{:S(2)}) collective-permute-start(bf16[256,640]{1,0:T(8,128)(2,1)S(1)} %shard_map.85.txt_ref.rows_ref), channel_id=1, source_target_pairs={{0,1},{1,0},{2,3},{3,2},{4,5},{5,4},{6,7},{7,6},{8,9},{9,8},{10,11... | collective-permute-start | bytes 983048 | tf_op jit(solution)/shard_map/ppermute | solution.py:32
  14.4 12.4 %collective-permute-start.3 = (bf16[256,640]{1,0:T(8,128)(2,1)S(1)}, bf16[256,640]{1,0:T(8,128)(2,1)S(1)}, u32[]{:S(2)}, u32[]{:S(2)}) collective-permute-start(bf16[256,640]{1,0:T(8,128)(2,1)S(1)} %shard_map.85.txt_ref.rows_ref), channel_id=1, source_target_pairs={{0,7},{1,6},{2,5},{3,4},{4,3},{5,2},{6,1},{7,0},{8,15},{9,14},{10,... | collective-permute-start | bytes 983048 | tf_op jit(solution)/shard_map/ppermute | solution.py:32
  17.7 1.4 %copy-start = (bf16[1152,640]{1,0:T(8,128)(2,1)S(1)}, bf16[1152,640]{1,0:T(8,128)(2,1)}, u32[]{:S(2)}) copy-start(bf16[1152,640]{1,0:T(8,128)(2,1)} %head_ref.1) | copy-start | bytes 4423684
  19.1 1.1 copy-start.4
  20.1 0.7 copy-start.6
  22.3 5.4 %collective-permute-start.4 = (bf16[256,640]{1,0:T(8,128)(2,1)S(1)}, bf16[256,640]{1,0:T(8,128)(2,1)S(1)}, u32[]{:S(2)}, u32[]{:S(2)}) collective-permute-start(bf16[256,640]{1,0:T(8,128)(2,1)S(1)} %get-tuple-element.18), channel_id=1, source_target_pairs={{0,1},{1,0},{2,3},{3,2},{4,5},{5,4},{6,7},{7,6},{8,9},{9,8},{10,11... | collective-permute-start | bytes 983048 | tf_op jit(solution)/shard_map/ppermute | solution.py:32
  26.2 3.6 %copy-start.1 = (bf16[1152,640]{1,0:T(8,128)(2,1)S(1)}, bf16[1152,640]{1,0:T(8,128)(2,1)}, u32[]{:S(2)}) copy-start(bf16[1152,640]{1,0:T(8,128)(2,1)} %head_ref.1) | copy-start | bytes 4423684
  27.6 4.1 %copy-start.5 = (bf16[256,1152]{1,0:T(8,128)(2,1)S(1)}, bf16[256,1152]{1,0:T(8,128)(2,1)}, u32[]{:S(2)}) copy-start(bf16[256,1152]{1,0:T(8,128)(2,1)} %feat_ref.3) | copy-start | bytes 1769476
  27.6 4.1 %collective-permute-start.5 = (bf16[256,1280]{1,0:T(8,128)(2,1)S(1)}, bf16[256,1280]{1,0:T(8,128)(2,1)S(1)}, u32[]{:S(2)}, u32[]{:S(2)}) collective-permute-start(bf16[256,1280]{1,0:T(8,128)(2,1)S(1)} %shard_map.90.mine_ref), channel_id=1, source_target_pairs={{0,1},{1,0},{2,3},{3,2},{4,5},{5,4},{6,7},{7,6},{8,9},{9,8},{10,11... | collective-permute-start | bytes 1966088 | tf_op jit(solution)/shard_map/ppermute | solution.py:32
  52.8 69.1 %copy-start.3 = (bf16[256,640]{1,0:T(8,128)(2,1)S(1)}, bf16[256,640]{1,0:T(8,128)(2,1)}, u32[]{:S(2)}) copy-start(bf16[256,640]{1,0:T(8,128)(2,1)} %txt_ref.3) | copy-start | bytes 983044
  52.8 25.9 %all-to-all-start.1 = ((bf16[16,16,128]{2,1,0:T(8,128)(2,1)}), bf16[16,16,128]{2,1,0:T(8,128)(2,1)S(1)}, u32[]{:S(2)}, u32[]{:S(2)}) async-start(bf16[16,16,128]{2,1,0:T(8,128)(2,1)} %shard_map.92), calls=%async_computation.1 | async-start | bytes 131072 | tf_op jit(solution)/shard_map/all_to_all | solution.py:36
  66.9 32.4 %collective-permute-start.6 = (bf16[256,640]{1,0:T(8,128)(2,1)S(1)}, bf16[256,640]{1,0:T(8,128)(2,1)S(1)}, u32[]{:S(2)}, u32[]{:S(2)}) collective-permute-start(bf16[256,640]{1,0:T(8,128)(2,1)S(1)} %get-tuple-element.21.rows_ref), channel_id=1, source_target_pairs={{0,7},{1,6},{2,5},{3,4},{4,3},{5,2},{6,1},{7,0},{8,15},{9,14},{10,... | collective-permute-start | bytes 983048 | tf_op jit(solution)/shard_map/ppermute | solution.py:32
  70.5 28.8 %collective-permute-start.7 = (bf16[256,640]{1,0:T(8,128)(2,1)S(1)}, bf16[256,640]{1,0:T(8,128)(2,1)S(1)}, u32[]{:S(2)}, u32[]{:S(2)}) collective-permute-start(bf16[256,640]{1,0:T(8,128)(2,1)S(1)} %get-tuple-element.21.rows_ref), channel_id=1, source_target_pairs={{0,15},{1,14},{2,13},{3,12},{4,11},{5,10},{6,9},{7,8},{8,7},{9,6},... | collective-permute-start | bytes 983048 | tf_op jit(solution)/shard_map/ppermute | solution.py:32
  74.8 24.5 %collective-permute-start.8 = (bf16[256,640]{1,0:T(8,128)(2,1)S(1)}, bf16[256,640]{1,0:T(8,128)(2,1)S(1)}, u32[]{:S(2)}, u32[]{:S(2)}) collective-permute-start(bf16[256,640]{1,0:T(8,128)(2,1)S(1)} %get-tuple-element.21.rows_ref), channel_id=1, source_target_pairs={{0,3},{1,2},{2,1},{3,0},{4,7},{5,6},{6,5},{7,4},{8,11},{9,10},{10,... | collective-permute-start | bytes 983048 | tf_op jit(solution)/shard_map/ppermute | solution.py:32
  118.4 6.1 %collective-permute-start.9 = (bf16[16,12,16,128]{3,2,1,0:T(8,128)(2,1)S(1)}, bf16[16,12,16,128]{3,2,1,0:T(8,128)(2,1)S(1)}, u32[]{:S(2)}, u32[]{:S(2)}) collective-permute-start(bf16[16,12,16,128]{3,2,1,0:T(8,128)(2,1)S(1)} %all_to_all.22.mine_ref), channel_id=1, source_target_pairs={{0,1},{1,0},{2,3},{3,2},{4,5},{5,4},{6,7},{7,6},{8,9},{9,8},{10,11... | collective-permute-start | bytes 2359304 | tf_op jit(solution)/shard_map/ppermute | solution.py:32

commit v4 on v3

--- a/solution.py
+++ b/solution.py
@@ -24,7 +24,7 @@
 
 
 PLANE = group((1, 2, 7, 8))
-LINE = group((3, 4, 5, 6))
+NEAR, FAR = group((3, 4)), group((5, 6))
 
 
 def swap(value, mask):
@@ -106,19 +106,20 @@
 
 
 def image_end_kernel(
-    scale_ref, bias_ref, total_ref, rows_ref, other_ref, unit_ref, inverse_ref, packed_ref
+    scale_ref, bias_ref, total_ref, rows_ref, other_ref, unit_ref, inverse_ref, feat_ref, packed_ref
 ):
     rows = rows_ref[...]
     total = total_ref[...] + pair_term(scale_ref, bias_ref, rows, other_ref[...])
     packed_ref[:, :E] = tangent(scale_ref[0] * total, unit_ref[...], inverse_ref[...])
-    packed_ref[:, E:] = rows
+    packed_ref[:, E : 2 * E] = rows
+    packed_ref[:, 2 * E :] = feat_ref[...]
 
 
 def text_end_kernel(
     scale_ref, bias_ref, total_ref, rows_ref, packed_ref, a_ref, b_ref, c_ref, txt_ref, out_ref
 ):
     rows = rows_ref[...]
-    total = total_ref[...] + pair_term(scale_ref, bias_ref, rows, packed_ref[:, E:])
+    total = total_ref[...] + pair_term(scale_ref, bias_ref, rows, packed_ref[:, E : 2 * E])
     for other_ref in (a_ref, b_ref, c_ref):
         total = total + pair_term(scale_ref, bias_ref, rows, other_ref[...])
     value = txt_ref[...].astype(F32)
@@ -126,31 +127,29 @@
     out_ref[...] = tangent(scale_ref[0] * total, value * inverse, inverse)
 
 
-def sum_of(parts_ref):
+def sum_kernel(parts_ref, out_ref):
     total = parts_ref[0].astype(F32)
-    for k in range(1, OWNERS):
+    for k in range(1, parts_ref.shape[0]):
         total = total + parts_ref[k].astype(F32)
-    return total.astype(BF16)
-
-
-def plane_sum_kernel(parts_ref, out_ref):
-    out_ref[:SLABS] = sum_of(parts_ref)
-    out_ref[SLABS:] = jnp.zeros((OWNERS - SLABS, 16, 128), BF16)
-
-
-def line_sum_kernel(parts_ref, out_ref):
-    out_ref[...] = jnp.broadcast_to(sum_of(parts_ref)[None], (OWNERS, 16, 128))
-
-
-def head_kernel(core_ref, feat_ref, other_feat_ref, mine_ref, theirs_ref, out_ref):
+    out_ref[...] = total.astype(BF16)
+
+
+def spread_sum_kernel(parts_ref, out_ref):
+    total = parts_ref[0].astype(F32)
+    for k in range(1, parts_ref.shape[0]):
+        total = total + parts_ref[k].astype(F32)
+    out_ref[...] = jnp.broadcast_to(total.astype(BF16)[None], out_ref.shape)
+
+
+def head_kernel(core_ref, feat_ref, mine_ref, theirs_ref, out_ref):
     core = core_ref[0]
     mine, theirs = mine_ref[:, :E], theirs_ref[:, :E]
 
     def product(column):
         here = pl.multiple_of(column, 128)
-        there = pl.multiple_of(column - 512 * core, 128)
+        there = pl.multiple_of(2 * E + column - 512 * core, 128)
         total = dot(feat_ref[:, pl.ds(here, 128)], mine, 0, 0)
-        return total + dot(other_feat_ref[:, pl.ds(there, 128)], theirs, 0, 0)
+        return total + dot(theirs_ref[:, pl.ds(there, 128)], theirs, 0, 0)
 
     def store(band, rows):
         for t in range(5):
@@ -195,8 +194,8 @@
     block = shape(ROWS, E)
     block16 = shape(ROWS, E, dtype=BF16)
 
-    pair16 = shape(ROWS, 2 * E, dtype=BF16)
-    txt_rows = call(text_kernel, block16, [VMEM], 1000000, txt_emb)
+    packed = shape(ROWS, 3 * E, dtype=BF16)
+    txt_rows = call(text_kernel, block16, [VMEM], 40 * pair, txt_emb)
     text = {c: swap(txt_rows, c) for c in (15, 3, 1, 7)}
 
     unit, inverse, img_rows, d_img, d_txt, other_feat = call(
@@ -206,29 +205,31 @@
         12 * pair,
         core, scale, bias, labels[None, :], img_feat, head_weight, txt_rows,
     )
-    other_feat = swap(other_feat, 1)
+    img_3 = swap(img_rows, 3)
     pair_specs = [SMEM, SMEM, VMEM, VMEM, VMEM]
     for c in (15, 3, 1):
         d_img = call(pair_kernel, block, pair_specs, little, scale, bias, d_img, img_rows, text[c])
     packed_img = call(
-        image_end_kernel, pair16, pair_specs + [VMEM, VMEM], little,
-        scale, bias, d_img, img_rows, text[7], unit, inverse,
-    )
-    other_img = swap(after(packed_img, other_feat), 1)
+        image_end_kernel, packed, pair_specs + [VMEM] * 3, little,
+        scale, bias, d_img, img_rows, text[7], unit, inverse, other_feat,
+    )
+    other_img = swap(after(packed_img, img_3), 1)
     d_img_feat = dot(packed_img[:, :E], head_weight, 1, 1).astype(BF16)
 
     parts = call(
-        head_kernel, shape(OWNERS, SLABS, 16, 128, dtype=BF16), [SMEM] + [VMEM] * 4,
-        4 * ROWS * D * E // 2, core, img_feat, other_feat, packed_img, other_img,
+        head_kernel, shape(OWNERS, SLABS, 16, 128, dtype=BF16), [SMEM] + [VMEM] * 3,
+        4 * ROWS * D * E // 2, core, img_feat, packed_img, other_img,
     )
     parts = exchange(after(parts, d_img_feat), PLANE)
-    line = shape(OWNERS, 16, 128, dtype=BF16)
-    part = call(plane_sum_kernel, line, [VMEM], little, parts)
+    slab = (16, 128)
+    part = call(sum_kernel, shape(SLABS, *slab, dtype=BF16), [VMEM], little, parts)
     late = after(img_rows, part)
-    images = [swap(late, c) for c in (7, 15, 3)]
-    part = call(line_sum_kernel, line, [VMEM], little, exchange(part, LINE))
-    part = exchange(part, LINE)[:SLABS]
-    part = after(part, *images)
+    images = [img_3, swap(late, 7), swap(late, 15)]
+    quarters = shape(4, SLABS // 4, *slab, dtype=BF16)
+    parts = exchange(part.reshape(quarters.shape), NEAR)
+    parts = exchange(call(spread_sum_kernel, quarters, [VMEM], little, parts), FAR)
+    parts = exchange(call(spread_sum_kernel, quarters, [VMEM], little, parts), NEAR)
+    part = after(parts.reshape(SLABS, *slab), *images)
     parts = exchange(after(jnp.broadcast_to(part[None], (OWNERS, SLABS, 16, 128))), PLANE)
     d_head = call(
         place_kernel, shape(D, E, dtype=BF16), [SMEM, VMEM, VMEM], 0,

time: 126 us -> 132 us (1.048)
  Pallas kernels: 9.67 us -> 15.9 us
  waiting for transfers between devices: 2.35 us -> 7.08 us
  starting transfers between devices: 46.7 us -> 43.5 us
  local copies, waits for them, and re-layouts: 4.24 us -> 2.31 us
    all_to_all x1 -> x2, starting transfers between devices: 14.1 us -> 7.68 us  [exchange(): lax.all_to_all(value, 'dp', 0, 0, axis_index_groups=members, tiled=True)]
    pallas_call x11 -> x12, Pallas kernels: 9.67 us -> 15.9 us  [call(): pl.pallas_call(kernel, out_shape=out_shape, in_specs=specs, out_specs=out...]
    ppermute x10 -> x9, starting transfers between devices: 32.5 us -> 35.9 us  [swap(): return lax.ppermute(value, 'dp', pairs)]
    all_to_all x1 -> x2, waiting for transfers between devices: 1.16 us -> 4.5 us  [exchange(): lax.all_to_all(value, 'dp', 0, 0, axis_index_groups=members, tiled=True)]
    unnamed x14 -> x16, local copies, waits for them, and re-layouts: 4.09 us -> 2.16 us
    ppermute x10 -> x9, waiting for transfers between devices: 1.2 us -> 2.58 us  [swap(): return lax.ppermute(value, 'dp', pairs)]
  transfers between devices with their start and end apart: 11 -> 11, of which waited for: 3 -> 3; matrix products, arithmetic and copies ran while one was open for 1% -> 1% of each run, Pallas kernels for 5% -> 9%
where the time goes in v4:
time: 132 us; the launch traced here: 131 us
  blocking collectives  58.2 us (44%)
  starting transfers between devices  43.5 us (33%)
  Pallas kernels  15.9 us (12%)
  waiting for transfers between devices  7.08 us (5%)
  local copies, waits for them, and re-layouts  2.31 us (2%)
  between operations  2.24 us (2%)
  matrix products  1.49 us (1%)
    all_to_all x3, blocking collectives, exchange(): lax.all_to_all(value, 'dp', 0, 0, axis_index_groups=members, tiled=True)  58.2 us
    ppermute x9, starting transfers between devices, swap(): return lax.ppermute(value, 'dp', pairs)  35.9 us
    pallas_call x12, Pallas kernels, call(): pl.pallas_call(kernel, out_shape=out_shape, in_specs=specs, out_specs=out...  15.9 us
    all_to_all x2, starting transfers between devices, exchange(): lax.all_to_all(value, 'dp', 0, 0, axis_index_groups=members, tiled=True)  7.68 us
    all_to_all x2, waiting for transfers between devices, exchange(): lax.all_to_all(value, 'dp', 0, 0, axis_index_groups=members, tiled=True)  4.5 us
  transfers between devices with their start and end apart: 11, of which 3 were waited for; matrix products, arithmetic and copies ran while one was open for 1% of the time, Pallas kernels for 9%

profile of v4, /device:TPU:1, one launch (start us, length us, event | category | flops | bytes accessed | tf_op | source)
XLA Modules:
  0.0 130.8 jit_solution(12084743991384078362)
XLA Ops:
  0.7 1.1 copy-done.3
  2.6 7.1 %collective-permute-start = (bf16[256,640]{1,0:T(8,128)(2,1)}, bf16[256,640]{1,0:T(8,128)(2,1)}, u32[]{:S(2)}, u32[]{:S(2)}) collective-permute-start(bf16[256,640]{1,0:T(8,128)(2,1)} %shard_map.85.txt_ref.rows_ref), channel_id=1, source_target_pairs={{0,15},{1,14},{2,13},{3,12},{4,11},{5,10},{6,9},{7,8},{8,7},{9,6},... | collective-permute-start | bytes 983048 | tf_op jit(solution)/shard_map/ppermute | solution.py:32
  9.7 1.9 %collective-permute-start.1 = (bf16[256,640]{1,0:T(8,128)(2,1)}, bf16[256,640]{1,0:T(8,128)(2,1)}, u32[]{:S(2)}, u32[]{:S(2)}) collective-permute-start(bf16[256,640]{1,0:T(8,128)(2,1)} %shard_map.85.txt_ref.rows_ref), channel_id=1, source_target_pairs={{0,3},{1,2},{2,1},{3,0},{4,7},{5,6},{6,5},{7,4},{8,11},{9,10},{10,... | collective-permute-start | bytes 983048 | tf_op jit(solution)/shard_map/ppermute | solution.py:32
  11.7 3.6 %collective-permute-start.2 = (bf16[256,640]{1,0:T(8,128)(2,1)}, bf16[256,640]{1,0:T(8,128)(2,1)}, u32[]{:S(2)}, u32[]{:S(2)}) collective-permute-start(bf16[256,640]{1,0:T(8,128)(2,1)} %shard_map.85.txt_ref.rows_ref), channel_id=1, source_target_pairs={{0,1},{1,0},{2,3},{3,2},{4,5},{5,4},{6,7},{7,6},{8,9},{9,8},{10,11... | collective-permute-start | bytes 983048 | tf_op jit(solution)/shard_map/ppermute | solution.py:32
  15.2 1.9 %collective-permute-start.3 = (bf16[256,640]{1,0:T(8,128)(2,1)}, bf16[256,640]{1,0:T(8,128)(2,1)S(1)}, u32[]{:S(2)}, u32[]{:S(2)}) collective-permute-start(bf16[256,640]{1,0:T(8,128)(2,1)} %shard_map.85.txt_ref.rows_ref), channel_id=1, source_target_pairs={{0,7},{1,6},{2,5},{3,4},{4,3},{5,2},{6,1},{7,0},{8,15},{9,14},{10,... | collective-permute-start | bytes 983048 | tf_op jit(solution)/shard_map/ppermute | solution.py:32
  19.6 2.5 %shard_map.86 = (f32[256,640]{1,0:T(8,128)S(1)}, f32[256,1]{1,0:T(8,128)S(1)}, bf16[256,640]{1,0:T(8,128)(2,1)S(1)}, f32[256,640]{1,0:T(8,128)S(1)}, f32[256,640...) custom-call(s32[1]{0:T(128)} %bitcast.core_ref, f32[1]{0:T(128)S(6)} %exp.3.scale_ref, f32[1]{0:T(128)S(6)} %copy.10.bias_ref, ...), custom_call_target="tpu_custom_call" | custom-call | flops 2013265920 | bytes 100000 | tf_op jit(solution)/shard_map/pallas_call | solution.py:54
  22.1 3.6 %collective-permute-start.4 = (bf16[256,640]{1,0:T(8,128)(2,1)S(1)}, bf16[256,640]{1,0:T(8,128)(2,1)S(1)}, u32[]{:S(2)}, u32[]{:S(2)}) collective-permute-start(bf16[256,640]{1,0:T(8,128)(2,1)S(1)} %get-tuple-element.21.rows_ref), channel_id=1, source_target_pairs={{0,3},{1,2},{2,1},{3,0},{4,7},{5,6},{6,5},{7,4},{8,11},{9,10},{10,... | collective-permute-start | bytes 983048 | tf_op jit(solution)/shard_map/ppermute | solution.py:32
  25.7 1.6 %shard_map.87.total_ref = f32[256,640]{1,0:T(8,128)S(1)} custom-call(f32[1]{0:T(128)S(6)} %exp.3.scale_ref, f32[1]{0:T(128)S(6)} %copy.10.bias_ref, f32[256,640]{1,0:T(8,128)S(1)} %get-tuple-element.13.total_ref, bf16[256,640]{1,0:T(8,128)(2,1)S(1)} %get-tuple-element.21.rows_ref, bf16[256,640]{1,0:T(8,128)(2,1)} %collective-permute-done.other_ref), custom_call_target="tpu_custom_call" | custom-call | flops 1677721 | bytes 100000 | tf_op jit(solution)/shard_map/pallas_call | solution.py:54
  27.4 1.6 %shard_map.88.total_ref = f32[256,640]{1,0:T(8,128)S(1)} custom-call(f32[1]{0:T(128)S(6)} %exp.3.scale_ref, f32[1]{0:T(128)S(6)} %copy.10.bias_ref, f32[256,640]{1,0:T(8,128)S(1)} %shard_map.87.total_ref, bf16[256,640]{1,0:T(8,128)(2,1)S(1)} %get-tuple-element.21.rows_ref, bf16[256,640]{1,0:T(8,128)(2,1)} %collective-permute-done.1.other_ref), custom_call_target="tpu_custom_call" | custom-call | flops 1677721 | bytes 100000 | tf_op jit(solution)/shard_map/pallas_call | solution.py:54
  29.0 1.6 %shard_map.89.total_ref = f32[256,640]{1,0:T(8,128)S(1)} custom-call(f32[1]{0:T(128)S(6)} %exp.3.scale_ref, f32[1]{0:T(128)S(6)} %copy.10.bias_ref, f32[256,640]{1,0:T(8,128)S(1)} %shard_map.88.total_ref, bf16[256,640]{1,0:T(8,128)(2,1)S(1)} %get-tuple-element.21.rows_ref, bf16[256,640]{1,0:T(8,128)(2,1)} %collective-permute-done.2.other_ref), custom_call_target="tpu_custom_call" | custom-call | flops 1677721 | bytes 100000 | tf_op jit(solution)/shard_map/pallas_call | solution.py:54
  31.4 1.8 %collective-permute-done.4.a_ref = bf16[256,640]{1,0:T(8,128)(2,1)S(1)} collective-permute-done((bf16[256,640]{1,0:T(8,128)(2,1)S(1)}, bf16[256,640]{1,0:T(8,128)(2,1)S(1)}, u32[]{:S(2)}, u32[]{:S(2)}) %collective-permute-start.4) | collective-permute-done | bytes 327712 | tf_op jit(solution)/shard_map/ppermute | solution.py:32
  33.3 2.2 %collective-permute-start.5 = (bf16[256,1920]{1,0:T(8,128)(2,1)S(1)}, bf16[256,1920]{1,0:T(8,128)(2,1)S(1)}, u32[]{:S(2)}, u32[]{:S(2)}) collective-permute-start(bf16[256,1920]{1,0:T(8,128)(2,1)S(1)} %shard_map.90.mine_ref), channel_id=1, source_target_pairs={{0,1},{1,0},{2,3},{3,2},{4,5},{5,4},{6,7},{7,6},{8,9},{9,8},{10,11... | collective-permute-start | bytes 2949128 | tf_op jit(solution)/shard_map/ppermute | solution.py:32
  35.5 1.5 %convolution_convert_fusion = bf16[256,1152]{1,0:T(8,128)(2,1)} fusion(bf16[1152,640]{1,0:T(8,128)(2,1)S(1)} %copy-done, bf16[256,1920]{1,0:T(8,128)(2,1)S(1)} %shard_map.90.mine_ref), kind=kOutput, calls=%fused_computation | convolution fusion | flops 377782272 | bytes 2392064 | tf_op jit(solution)/shard_map/dot_general | solution.py:48
  38.5 20.1 %all_to_all.25.parts_ref = bf16[16,12,16,128]{3,2,1,0:T(8,128)(2,1)S(1)} all-to-all(bf16[16,12,16,128]{3,2,1,0:T(8,128)(2,1)S(1)} %shard_map.91), channel_id=1, replica_groups={{0,2,4,6,128,130,132,134,256,258,260,262,384,386,388,390},{1,3,5,7,129,..., dimensions={0} | all-to-all | bytes 1572864 | tf_op jit(solution)/shard_map/all_to_all | solution.py:36
  59.3 4.4 %all-to-all-start.1 = ((bf16[4,3,16,128]{3,2,1,0:T(8,128)(2,1)}), bf16[4,3,16,128]{3,2,1,0:T(8,128)(2,1)S(1)}, u32[]{:S(2)}, u32[]{:S(2)}) async-start(bf16[4,3,16,128]{3,2,1,0:T(8,128)(2,1)} %bitcast.2), calls=%async_computation.1 | async-start | bytes 98304 | tf_op jit(solution)/shard_map/all_to_all | solution.py:36
  63.7 3.9 %collective-permute-start.6 = (bf16[256,640]{1,0:T(8,128)(2,1)S(1)}, bf16[256,640]{1,0:T(8,128)(2,1)S(1)}, u32[]{:S(2)}, u32[]{:S(2)}) collective-permute-start(bf16[256,640]{1,0:T(8,128)(2,1)S(1)} %get-tuple-element.21.rows_ref), channel_id=1, source_target_pairs={{0,7},{1,6},{2,5},{3,4},{4,3},{5,2},{6,1},{7,0},{8,15},{9,14},{10,... | collective-permute-start | bytes 983048 | tf_op jit(solution)/shard_map/ppermute | solution.py:32
  67.6 4.0 %collective-permute-start.7 = (bf16[256,640]{1,0:T(8,128)(2,1)S(1)}, bf16[256,640]{1,0:T(8,128)(2,1)S(1)}, u32[]{:S(2)}, u32[]{:S(2)}) collective-permute-start(bf16[256,640]{1,0:T(8,128)(2,1)S(1)} %get-tuple-element.21.rows_ref), channel_id=1, source_target_pairs={{0,15},{1,14},{2,13},{3,12},{4,11},{5,10},{6,9},{7,8},{8,7},{9,6},... | collective-permute-start | bytes 983048 | tf_op jit(solution)/shard_map/ppermute | solution.py:32
  71.7 24.8 %all_to_all.26.parts_ref = bf16[4,3,16,128]{3,2,1,0:T(8,128)(2,1)S(1)} all-to-all(bf16[4,3,16,128]{3,2,1,0:T(8,128)(2,1)S(1)} %shard_map.94), channel_id=1, replica_groups={{0,32,64,96},{1,33,65,97},{2,34,66,98},{3,35,67,99},{4,36,68,100},{5,37..., dimensions={0} | all-to-all | bytes 98304 | tf_op jit(solution)/shard_map/all_to_all | solution.py:36
  97.1 3.3 %all-to-all-start.3 = ((bf16[4,3,16,128]{3,2,1,0:T(8,128)(2,1)}), bf16[4,3,16,128]{3,2,1,0:T(8,128)(2,1)S(1)}, u32[]{:S(2)}, u32[]{:S(2)}) async-start(bf16[4,3,16,128]{3,2,1,0:T(8,128)(2,1)} %shard_map.95), calls=%async_computation.3 | async-start | bytes 98304 | tf_op jit(solution)/shard_map/all_to_all | solution.py:36
  100.4 4.5 %all-to-all-done.3 = bf16[4,3,16,128]{3,2,1,0:T(8,128)(2,1)S(1)} async-done(((bf16[4,3,16,128]{3,2,1,0:T(8,128)(2,1)}), bf16[4,3,16,128]{3,2,1,0:T(8,128)(2,1)S(1)}, u32[]{:S(2)}, u32[]{:S(2)}) %all-to-all-start.3) | async-done | bytes 49184 | tf_op jit(solution)/shard_map/all_to_all | solution.py:36
  105.0 13.3 %all_to_all.27.mine_ref = bf16[16,12,16,128]{3,2,1,0:T(8,128)(2,1)S(1)} all-to-all(bf16[16,12,16,128]{3,2,1,0:T(8,128)(2,1)S(1)} %broadcast_in_dim.14), channel_id=1, replica_groups={{0,2,4,6,128,130,132,134,256,258,260,262,384,386,388,390},{1,3,5,7,129,..., dimensions={0} | all-to-all | bytes 1572864 | tf_op jit(solution)/shard_map/all_to_all | solution.py:36
  118.4 7.5 %collective-permute-start.8 = (bf16[16,12,16,128]{3,2,1,0:T(8,128)(2,1)S(1)}, bf16[16,12,16,128]{3,2,1,0:T(8,128)(2,1)S(1)}, u32[]{:S(2)}, u32[]{:S(2)}) collective-permute-start(bf16[16,12,16,128]{3,2,1,0:T(8,128)(2,1)S(1)} %all_to_all.27.mine_ref), channel_id=1, source_target_pairs={{0,1},{1,0},{2,3},{3,2},{4,5},{5,4},{6,7},{7,6},{8,9},{9,8},{10,11... | collective-permute-start | bytes 2359304 | tf_op jit(solution)/shard_map/ppermute | solution.py:32
  125.9 3.6 %shard_map.93 = bf16[256,640]{1,0:T(8,128)(2,1)} custom-call(f32[1]{0:T(128)S(6)} %exp.3.scale_ref, f32[1]{0:T(128)S(6)} %copy.10.bias_ref, f32[256,640]{1,0:T(8,128)S(1)} %get-tuple-element.18.total_ref, bf16[256,640]{1,0:T(8,128)(2,1)} %shard_map.85.txt_ref.rows_ref, bf16[256,1920]{1,0:T(8,128)(2,1)S(1)} %collective-permute-done.5.theirs_ref.packed_ref, ...), custom_call_target="tpu_custom_call" | custom-call | flops 671088640 | bytes 100000 | tf_op jit(solution)/shard_map/pallas_call | solution.py:54
  129.5 1.2 shard_map.96
  (31 shorter events, 5.7 us)
Async XLA Ops:
  0.6 17.9 %copy-start = (bf16[1152,640]{1,0:T(8,128)(2,1)S(1)}, bf16[1152,640]{1,0:T(8,128)(2,1)}, u32[]{:S(2)}) copy-start(bf16[1152,640]{1,0:T(8,128)(2,1)} %head_ref.1) | copy-start | bytes 4423684
  0.6 1.1 copy-start.3
  1.7 16.8 %copy-start.7 = (s32[256]{0:T(256)S(1)}, s32[256]{0:T(256)}, u32[]{:S(2)}) copy-start(s32[256]{0:T(256)} %param.9) | copy-start | bytes 3076
  2.6 23.1 %collective-permute-start = (bf16[256,640]{1,0:T(8,128)(2,1)}, bf16[256,640]{1,0:T(8,128)(2,1)}, u32[]{:S(2)}, u32[]{:S(2)}) collective-permute-start(bf16[256,640]{1,0:T(8,128)(2,1)} %shard_map.85.txt_ref.rows_ref), channel_id=1, source_target_pairs={{0,15},{1,14},{2,13},{3,12},{4,11},{5,10},{6,9},{7,8},{8,7},{9,6},... | collective-permute-start | bytes 983048 | tf_op jit(solution)/shard_map/ppermute | solution.py:32
  9.7 17.6 %collective-permute-start.1 = (bf16[256,640]{1,0:T(8,128)(2,1)}, bf16[256,640]{1,0:T(8,128)(2,1)}, u32[]{:S(2)}, u32[]{:S(2)}) collective-permute-start(bf16[256,640]{1,0:T(8,128)(2,1)} %shard_map.85.txt_ref.rows_ref), channel_id=1, source_target_pairs={{0,3},{1,2},{2,1},{3,0},{4,7},{5,6},{6,5},{7,4},{8,11},{9,10},{10,... | collective-permute-start | bytes 983048 | tf_op jit(solution)/shard_map/ppermute | solution.py:32
  11.7 17.3 %collective-permute-start.2 = (bf16[256,640]{1,0:T(8,128)(2,1)}, bf16[256,640]{1,0:T(8,128)(2,1)}, u32[]{:S(2)}, u32[]{:S(2)}) collective-permute-start(bf16[256,640]{1,0:T(8,128)(2,1)} %shard_map.85.txt_ref.rows_ref), channel_id=1, source_target_pairs={{0,1},{1,0},{2,3},{3,2},{4,5},{5,4},{6,7},{7,6},{8,9},{9,8},{10,11... | collective-permute-start | bytes 983048 | tf_op jit(solution)/shard_map/ppermute | solution.py:32
  15.2 15.4 %collective-permute-start.3 = (bf16[256,640]{1,0:T(8,128)(2,1)}, bf16[256,640]{1,0:T(8,128)(2,1)S(1)}, u32[]{:S(2)}, u32[]{:S(2)}) collective-permute-start(bf16[256,640]{1,0:T(8,128)(2,1)} %shard_map.85.txt_ref.rows_ref), channel_id=1, source_target_pairs={{0,7},{1,6},{2,5},{3,4},{4,3},{5,2},{6,1},{7,0},{8,15},{9,14},{10,... | collective-permute-start | bytes 983048 | tf_op jit(solution)/shard_map/ppermute | solution.py:32
  18.5 1.1 copy-start.1
  22.1 11.2 %collective-permute-start.4 = (bf16[256,640]{1,0:T(8,128)(2,1)S(1)}, bf16[256,640]{1,0:T(8,128)(2,1)S(1)}, u32[]{:S(2)}, u32[]{:S(2)}) collective-permute-start(bf16[256,640]{1,0:T(8,128)(2,1)S(1)} %get-tuple-element.21.rows_ref), channel_id=1, source_target_pairs={{0,3},{1,2},{2,1},{3,0},{4,7},{5,6},{6,5},{7,4},{8,11},{9,10},{10,... | collective-permute-start | bytes 983048 | tf_op jit(solution)/shard_map/ppermute | solution.py:32
  31.4 6.3 %copy-start.2 = (bf16[256,1152]{1,0:T(8,128)(2,1)S(1)}, bf16[256,1152]{1,0:T(8,128)(2,1)}, u32[]{:S(2)}) copy-start(bf16[256,1152]{1,0:T(8,128)(2,1)} %feat_ref.3) | copy-start | bytes 1769476
  33.3 5.2 %copy-start.5 = (bf16[256,640]{1,0:T(8,128)(2,1)}, bf16[256,640]{1,0:T(8,128)(2,1)S(1)}, u32[]{:S(2)}) copy-start(bf16[256,640]{1,0:T(8,128)(2,1)S(1)} %collective-permute-done.4.a_ref) | copy-start | bytes 983044
  33.3 4.4 %collective-permute-start.5 = (bf16[256,1920]{1,0:T(8,128)(2,1)S(1)}, bf16[256,1920]{1,0:T(8,128)(2,1)S(1)}, u32[]{:S(2)}, u32[]{:S(2)}) collective-permute-start(bf16[256,1920]{1,0:T(8,128)(2,1)S(1)} %shard_map.90.mine_ref), channel_id=1, source_target_pairs={{0,1},{1,0},{2,3},{3,2},{4,5},{5,4},{6,7},{7,6},{8,9},{9,8},{10,11... | collective-permute-start | bytes 2949128 | tf_op jit(solution)/shard_map/ppermute | solution.py:32
  59.3 66.6 %copy-start.4 = (bf16[256,640]{1,0:T(8,128)(2,1)S(1)}, bf16[256,640]{1,0:T(8,128)(2,1)}, u32[]{:S(2)}) copy-start(bf16[256,640]{1,0:T(8,128)(2,1)} %txt_ref.3) | copy-start | bytes 983044
  59.3 66.6 %copy-start.6 = (bf16[256,640]{1,0:T(8,128)(2,1)S(1)}, bf16[256,640]{1,0:T(8,128)(2,1)}, u32[]{:S(2)}) copy-start(bf16[256,640]{1,0:T(8,128)(2,1)} %copy-done.5) | copy-start | bytes 983044
  59.3 12.4 %all-to-all-start.1 = ((bf16[4,3,16,128]{3,2,1,0:T(8,128)(2,1)}), bf16[4,3,16,128]{3,2,1,0:T(8,128)(2,1)S(1)}, u32[]{:S(2)}, u32[]{:S(2)}) async-start(bf16[4,3,16,128]{3,2,1,0:T(8,128)(2,1)} %bitcast.2), calls=%async_computation.1 | async-start | bytes 98304 | tf_op jit(solution)/shard_map/all_to_all | solution.py:36
  63.7 36.7 %collective-permute-start.6 = (bf16[256,640]{1,0:T(8,128)(2,1)S(1)}, bf16[256,640]{1,0:T(8,128)(2,1)S(1)}, u32[]{:S(2)}, u32[]{:S(2)}) collective-permute-start(bf16[256,640]{1,0:T(8,128)(2,1)S(1)} %get-tuple-element.21.rows_ref), channel_id=1, source_target_pairs={{0,7},{1,6},{2,5},{3,4},{4,3},{5,2},{6,1},{7,0},{8,15},{9,14},{10,... | collective-permute-start | bytes 983048 | tf_op jit(solution)/shard_map/ppermute | solution.py:32
  67.6 32.8 %collective-permute-start.7 = (bf16[256,640]{1,0:T(8,128)(2,1)S(1)}, bf16[256,640]{1,0:T(8,128)(2,1)S(1)}, u32[]{:S(2)}, u32[]{:S(2)}) collective-permute-start(bf16[256,640]{1,0:T(8,128)(2,1)S(1)} %get-tuple-element.21.rows_ref), channel_id=1, source_target_pairs={{0,15},{1,14},{2,13},{3,12},{4,11},{5,10},{6,9},{7,8},{8,7},{9,6},... | collective-permute-start | bytes 983048 | tf_op jit(solution)/shard_map/ppermute | solution.py:32
  97.1 7.8 %all-to-all-start.3 = ((bf16[4,3,16,128]{3,2,1,0:T(8,128)(2,1)}), bf16[4,3,16,128]{3,2,1,0:T(8,128)(2,1)S(1)}, u32[]{:S(2)}, u32[]{:S(2)}) async-start(bf16[4,3,16,128]{3,2,1,0:T(8,128)(2,1)} %shard_map.95), calls=%async_computation.3 | async-start | bytes 98304 | tf_op jit(solution)/shard_map/all_to_all | solution.py:36
  118.4 11.2 %collective-permute-start.8 = (bf16[16,12,16,128]{3,2,1,0:T(8,128)(2,1)S(1)}, bf16[16,12,16,128]{3,2,1,0:T(8,128)(2,1)S(1)}, u32[]{:S(2)}, u32[]{:S(2)}) collective-permute-start(bf16[16,12,16,128]{3,2,1,0:T(8,128)(2,1)S(1)} %all_to_all.27.mine_ref), channel_id=1, source_target_pairs={{0,1},{1,0},{2,3},{3,2},{4,5},{5,4},{6,7},{7,6},{8,9},{9,8},{10,11... | collective-permute-start | bytes 2359304 | tf_op jit(solution)/shard_map/ppermute | solution.py:32

commit v5 on v4

--- a/solution.py
+++ b/solution.py
@@ -57,7 +57,7 @@
         in_specs=specs,
         out_specs=out_specs if out_specs is not None else jax.tree.map(lambda _: VMEM, out_shape),
         scratch_shapes=scratch,
-        compiler_params=pltpu.CompilerParams(vmem_limit_bytes=32 << 20),
+        compiler_params=pltpu.CompilerParams(vmem_limit_bytes=14 << 20),
         cost_estimate=pl.CostEstimate(flops=flops, bytes_accessed=100000, transcendentals=0),
     )(*operands)
 
@@ -196,8 +196,7 @@
 
     packed = shape(ROWS, 3 * E, dtype=BF16)
     txt_rows = call(text_kernel, block16, [VMEM], 40 * pair, txt_emb)
-    text = {c: swap(txt_rows, c) for c in (15, 3, 1, 7)}
-
+    txt_7 = swap(txt_rows, 7)
     unit, inverse, img_rows, d_img, d_txt, other_feat = call(
         image_kernel,
         (block, shape(ROWS, 1), block16, block, block, block16),
@@ -205,15 +204,18 @@
         12 * pair,
         core, scale, bias, labels[None, :], img_feat, head_weight, txt_rows,
     )
-    img_3 = swap(img_rows, 3)
+    late = after(txt_rows, img_rows)
+    txt_3, txt_1 = swap(late, 3), swap(late, 1)
+    img_7, img_3 = swap(img_rows, 7), swap(img_rows, 3)
+    txt_15, img_15 = swap(txt_7, 8), swap(img_7, 8)
     pair_specs = [SMEM, SMEM, VMEM, VMEM, VMEM]
-    for c in (15, 3, 1):
-        d_img = call(pair_kernel, block, pair_specs, little, scale, bias, d_img, img_rows, text[c])
+    for other in (txt_7, txt_3, txt_1):
+        d_img = call(pair_kernel, block, pair_specs, little, scale, bias, d_img, img_rows, other)
     packed_img = call(
         image_end_kernel, packed, pair_specs + [VMEM] * 3, little,
-        scale, bias, d_img, img_rows, text[7], unit, inverse, other_feat,
-    )
-    other_img = swap(after(packed_img, img_3), 1)
+        scale, bias, d_img, img_rows, txt_15, unit, inverse, other_feat,
+    )
+    other_img = swap(after(packed_img, img_3, img_7), 1)
     d_img_feat = dot(packed_img[:, :E], head_weight, 1, 1).astype(BF16)
 
     parts = call(
@@ -223,13 +225,12 @@
     parts = exchange(after(parts, d_img_feat), PLANE)
     slab = (16, 128)
     part = call(sum_kernel, shape(SLABS, *slab, dtype=BF16), [VMEM], little, parts)
-    late = after(img_rows, part)
-    images = [img_3, swap(late, 7), swap(late, 15)]
+    part = after(part, img_15)
     quarters = shape(4, SLABS // 4, *slab, dtype=BF16)
     parts = exchange(part.reshape(quarters.shape), NEAR)
     parts = exchange(call(spread_sum_kernel, quarters, [VMEM], little, parts), FAR)
     parts = exchange(call(spread_sum_kernel, quarters, [VMEM], little, parts), NEAR)
-    part = after(parts.reshape(SLABS, *slab), *images)
+    part = parts.reshape(SLABS, *slab)
     parts = exchange(after(jnp.broadcast_to(part[None], (OWNERS, SLABS, 16, 128))), PLANE)
     d_head = call(
         place_kernel, shape(D, E, dtype=BF16), [SMEM, VMEM, VMEM], 0,
@@ -240,7 +241,7 @@
 
     d_txt_emb = call(
         text_end_kernel, block16, pair_specs + [VMEM] * 4, 4 * pair,
-        scale, bias, d_txt, txt_rows, other_img, *images, txt_emb,
+        scale, bias, d_txt, txt_rows, other_img, img_3, img_7, img_15, txt_emb,
     )
     return (d_img_feat, d_txt_emb, d_head)
 

time: 132 us -> 129 us (0.977)
  waiting for transfers between devices: 7.08 us -> 18 us
  Pallas kernels: 15.9 us -> 11 us
  blocking collectives: 58.2 us -> 53.7 us
  starting transfers between devices: 43.5 us -> 39.8 us
    all_to_all x2 -> x1, waiting for transfers between devices: 4.5 us -> 11.4 us  [exchange(): lax.all_to_all(value, 'dp', 0, 0, axis_index_groups=members, tiled=True)]
    pallas_call x12, Pallas kernels: 15.9 us -> 11 us  [call(): pl.pallas_call(kernel, out_shape=out_shape, in_specs=specs, out_specs=out...]
    all_to_all x3 -> x4, blocking collectives: 58.2 us -> 53.7 us  [exchange(): lax.all_to_all(value, 'dp', 0, 0, axis_index_groups=members, tiled=True)]
    ppermute x9, waiting for transfers between devices: 2.58 us -> 6.63 us  [swap(): return lax.ppermute(value, 'dp', pairs)]
    all_to_all x2 -> x1, starting transfers between devices: 7.68 us -> 4.75 us  [exchange(): lax.all_to_all(value, 'dp', 0, 0, axis_index_groups=members, tiled=True)]
  transfers between devices with their start and end apart: 11 -> 10, of which waited for: 3 -> 4; matrix products, arithmetic and copies ran while one was open for 1% -> 1% of each run, Pallas kernels for 9% -> 6%
where the time goes in v5:
time: 129 us; the launch traced here: 128 us
  blocking collectives  53.7 us (42%)
  starting transfers between devices  39.8 us (31%)
  waiting for transfers between devices  18 us (14%)
  Pallas kernels  11 us (9%)
  between operations  2.24 us (2%)
  local copies, waits for them, and re-layouts  2.02 us (2%)
  matrix products  1.49 us (1%)
    all_to_all x4, blocking collectives, exchange(): lax.all_to_all(value, 'dp', 0, 0, axis_index_groups=members, tiled=True)  53.7 us
    ppermute x9, starting transfers between devices, swap(): return lax.ppermute(value, 'dp', pairs)  35.1 us
    all_to_all x1, waiting for transfers between devices, exchange(): lax.all_to_all(value, 'dp', 0, 0, axis_index_groups=members, tiled=True)  11.4 us
    pallas_call x12, Pallas kernels, call(): pl.pallas_call(kernel, out_shape=out_shape, in_specs=specs, out_specs=out...  11 us
    ppermute x9, waiting for transfers between devices, swap(): return lax.ppermute(value, 'dp', pairs)  6.63 us
    all_to_all x1, starting transfers between devices, exchange(): lax.all_to_all(value, 'dp', 0, 0, axis_index_groups=members, tiled=True)  4.75 us
  transfers between devices with their start and end apart: 10, of which 4 were waited for; matrix products, arithmetic and copies ran while one was open for 1% of the time, Pallas kernels for 6%

profile of v5, /device:TPU:1, one launch (start us, length us, event | category | flops | bytes accessed | tf_op | source)
XLA Modules:
  0.0 128.2 jit_solution(1703403423862699300)
XLA Ops:
  0.7 1.1 copy-done.3
  1.9 5.8 %collective-permute-start = (bf16[256,640]{1,0:T(8,128)(2,1)S(1)}, bf16[256,640]{1,0:T(8,128)(2,1)S(1)}, u32[]{:S(2)}, u32[]{:S(2)}) collective-permute-start(bf16[256,640]{1,0:T(8,128)(2,1)S(1)} %shard_map.85.txt_ref.rows_ref), channel_id=1, source_target_pairs={{0,7},{1,6},{2,5},{3,4},{4,3},{5,2},{6,1},{7,0},{8,15},{9,14},{10,... | collective-permute-start | bytes 983048 | tf_op jit(solution)/shard_map/ppermute | solution.py:32
  9.1 1.5 %shard_map.86 = (f32[256,640]{1,0:T(8,128)S(1)}, f32[256,1]{1,0:T(8,128)S(1)}, bf16[256,640]{1,0:T(8,128)(2,1)S(1)}, f32[256,640]{1,0:T(8,128)S(1)}, f32[256,640...) custom-call(s32[1]{0:T(128)} %bitcast.core_ref, f32[1]{0:T(128)S(6)} %exp.3.scale_ref, f32[1]{0:T(128)S(6)} %copy.10.bias_ref, ...), custom_call_target="tpu_custom_call" | custom-call | flops 2013265920 | bytes 100000 | tf_op jit(solution)/shard_map/pallas_call | solution.py:54
  10.5 1.9 %collective-permute-start.1 = (bf16[256,640]{1,0:T(8,128)(2,1)S(1)}, bf16[256,640]{1,0:T(8,128)(2,1)S(1)}, u32[]{:S(2)}, u32[]{:S(2)}) collective-permute-start(bf16[256,640]{1,0:T(8,128)(2,1)S(1)} %shard_map.85.txt_ref.rows_ref), channel_id=1, source_target_pairs={{0,3},{1,2},{2,1},{3,0},{4,7},{5,6},{6,5},{7,4},{8,11},{9,10},{10,... | collective-permute-start | bytes 983048 | tf_op jit(solution)/shard_map/ppermute | solution.py:32
  12.5 4.9 %collective-permute-start.2 = (bf16[256,640]{1,0:T(8,128)(2,1)S(1)}, bf16[256,640]{1,0:T(8,128)(2,1)S(1)}, u32[]{:S(2)}, u32[]{:S(2)}) collective-permute-start(bf16[256,640]{1,0:T(8,128)(2,1)S(1)} %shard_map.85.txt_ref.rows_ref), channel_id=1, source_target_pairs={{0,1},{1,0},{2,3},{3,2},{4,5},{5,4},{6,7},{7,6},{8,9},{9,8},{10,11... | collective-permute-start | bytes 983048 | tf_op jit(solution)/shard_map/ppermute | solution.py:32
  17.4 2.2 %collective-permute-start.3 = (bf16[256,640]{1,0:T(8,128)(2,1)S(1)}, bf16[256,640]{1,0:T(8,128)(2,1)S(1)}, u32[]{:S(2)}, u32[]{:S(2)}) collective-permute-start(bf16[256,640]{1,0:T(8,128)(2,1)S(1)} %collective-permute-done.other_ref), channel_id=1, source_target_pairs={{0,8},{1,9},{2,10},{3,11},{4,12},{5,13},{6,14},{7,15},{8,0},{9,1},... | collective-permute-start | bytes 983048 | tf_op jit(solution)/shard_map/ppermute | solution.py:32
  19.6 5.0 %collective-permute-start.5 = (bf16[256,640]{1,0:T(8,128)(2,1)S(1)}, bf16[256,640]{1,0:T(8,128)(2,1)S(1)}, u32[]{:S(2)}, u32[]{:S(2)}) collective-permute-start(bf16[256,640]{1,0:T(8,128)(2,1)S(1)} %get-tuple-element.14.rows_ref), channel_id=1, source_target_pairs={{0,7},{1,6},{2,5},{3,4},{4,3},{5,2},{6,1},{7,0},{8,15},{9,14},{10,... | collective-permute-start | bytes 983048 | tf_op jit(solution)/shard_map/ppermute | solution.py:32
  24.6 2.6 %collective-permute-start.4 = (bf16[256,640]{1,0:T(8,128)(2,1)S(1)}, bf16[256,640]{1,0:T(8,128)(2,1)S(1)}, u32[]{:S(2)}, u32[]{:S(2)}) collective-permute-start(bf16[256,640]{1,0:T(8,128)(2,1)S(1)} %get-tuple-element.14.rows_ref), channel_id=1, source_target_pairs={{0,3},{1,2},{2,1},{3,0},{4,7},{5,6},{6,5},{7,4},{8,11},{9,10},{10,... | collective-permute-start | bytes 983048 | tf_op jit(solution)/shard_map/ppermute | solution.py:32
  30.1 2.8 %collective-permute-done.5.b_ref = bf16[256,640]{1,0:T(8,128)(2,1)S(1)} collective-permute-done((bf16[256,640]{1,0:T(8,128)(2,1)S(1)}, bf16[256,640]{1,0:T(8,128)(2,1)S(1)}, u32[]{:S(2)}, u32[]{:S(2)}) %collective-permute-start.5) | collective-permute-done | bytes 327712 | tf_op jit(solution)/shard_map/ppermute | solution.py:32
  32.9 2.8 %collective-permute-done.4.a_ref = bf16[256,640]{1,0:T(8,128)(2,1)S(1)} collective-permute-done((bf16[256,640]{1,0:T(8,128)(2,1)S(1)}, bf16[256,640]{1,0:T(8,128)(2,1)S(1)}, u32[]{:S(2)}, u32[]{:S(2)}) %collective-permute-start.4) | collective-permute-done | bytes 327712 | tf_op jit(solution)/shard_map/ppermute | solution.py:32
  36.4 1.9 %collective-permute-start.6 = (bf16[256,1920]{1,0:T(8,128)(2,1)S(1)}, bf16[256,1920]{1,0:T(8,128)(2,1)S(1)}, u32[]{:S(2)}, u32[]{:S(2)}) collective-permute-start(bf16[256,1920]{1,0:T(8,128)(2,1)S(1)} %shard_map.90.mine_ref), channel_id=1, source_target_pairs={{0,1},{1,0},{2,3},{3,2},{4,5},{5,4},{6,7},{7,6},{8,9},{9,8},{10,11... | collective-permute-start | bytes 2949128 | tf_op jit(solution)/shard_map/ppermute | solution.py:32
  38.3 1.5 %convolution_convert_fusion = bf16[256,1152]{1,0:T(8,128)(2,1)} fusion(bf16[1152,640]{1,0:T(8,128)(2,1)S(1)} %copy-done, bf16[256,1920]{1,0:T(8,128)(2,1)S(1)} %shard_map.90.mine_ref), kind=kOutput, calls=%fused_computation | convolution fusion | flops 377782272 | bytes 2392064 | tf_op jit(solution)/shard_map/dot_general | solution.py:48
  39.8 1.0 collective-permute-done.6.packed_ref.theirs_ref
  40.9 1.6 %shard_map.92 = bf16[16,12,16,128]{3,2,1,0:T(8,128)(2,1)} custom-call(s32[1]{0:T(128)} %bitcast.core_ref, bf16[256,1152]{1,0:T(8,128)(2,1)S(1)} %copy-done.2, bf16[256,1920]{1,0:T(8,128)(2,1)S(1)} %shard_map.90.mine_ref, bf16[256,1920]{1,0:T(8,128)(2,1)S(1)} %collective-permute-done.6.packed_ref.theirs_ref), custom_call_target="tpu_custom_call" | custom-call | flops 377487360 | bytes 100000 | tf_op jit(solution)/shard_map/pallas_call | solution.py:54
  42.5 4.7 %all-to-all-start = ((bf16[16,12,16,128]{3,2,1,0:T(8,128)(2,1)}), bf16[16,12,16,128]{3,2,1,0:T(8,128)(2,1)S(1)}, u32[]{:S(2)}, u32[]{:S(2)}) async-start(bf16[16,12,16,128]{3,2,1,0:T(8,128)(2,1)} %shard_map.92), calls=%async_computation | async-start | bytes 1572864 | tf_op jit(solution)/shard_map/all_to_all | solution.py:36
  47.2 2.1 %collective-permute-start.7 = (bf16[256,640]{1,0:T(8,128)(2,1)S(1)}, bf16[256,640]{1,0:T(8,128)(2,1)}, u32[]{:S(2)}, u32[]{:S(2)}) collective-permute-start(bf16[256,640]{1,0:T(8,128)(2,1)S(1)} %copy-done.6), channel_id=1, source_target_pairs={{0,8},{1,9},{2,10},{3,11},{4,12},{5,13},{6,14},{7,15},{8,0},{9,1},... | collective-permute-start | bytes 983048 | tf_op jit(solution)/shard_map/ppermute | solution.py:32
  49.4 11.4 %all-to-all-done.parts_ref = bf16[16,12,16,128]{3,2,1,0:T(8,128)(2,1)S(1)} async-done(((bf16[16,12,16,128]{3,2,1,0:T(8,128)(2,1)}), bf16[16,12,16,128]{3,2,1,0:T(8,128)(2,1)S(1)}, u32[]{:S(2)}, u32[]{:S(2)}) %all-to-all-start) | async-done | bytes 786464 | tf_op jit(solution)/shard_map/all_to_all | solution.py:36
  60.9 8.8 %all_to_all.25.parts_ref = bf16[4,3,16,128]{3,2,1,0:T(8,128)(2,1)S(1)} all-to-all(bf16[4,3,16,128]{3,2,1,0:T(8,128)(2,1)S(1)} %bitcast.5), channel_id=1, replica_groups={{0,8,16,24},{1,9,17,25},{2,10,18,26},{3,11,19,27},{4,12,20,28},{5,13,21..., dimensions={0} | all-to-all | bytes 98304 | tf_op jit(solution)/shard_map/all_to_all | solution.py:36
  69.7 24.1 %all_to_all.26.parts_ref = bf16[4,3,16,128]{3,2,1,0:T(8,128)(2,1)S(1)} all-to-all(bf16[4,3,16,128]{3,2,1,0:T(8,128)(2,1)S(1)} %shard_map.94), channel_id=1, replica_groups={{0,32,64,96},{1,33,65,97},{2,34,66,98},{3,35,67,99},{4,36,68,100},{5,37..., dimensions={0} | all-to-all | bytes 98304 | tf_op jit(solution)/shard_map/all_to_all | solution.py:36
  93.8 6.9 %all_to_all.27 = bf16[4,3,16,128]{3,2,1,0:T(8,128)(2,1)S(1)} all-to-all(bf16[4,3,16,128]{3,2,1,0:T(8,128)(2,1)S(1)} %shard_map.95), channel_id=1, replica_groups={{0,8,16,24},{1,9,17,25},{2,10,18,26},{3,11,19,27},{4,12,20,28},{5,13,21..., dimensions={0} | all-to-all | bytes 98304 | tf_op jit(solution)/shard_map/all_to_all | solution.py:36
  100.8 13.9 %all_to_all.28.mine_ref = bf16[16,12,16,128]{3,2,1,0:T(8,128)(2,1)S(1)} all-to-all(bf16[16,12,16,128]{3,2,1,0:T(8,128)(2,1)S(1)} %broadcast_in_dim.16), channel_id=1, replica_groups={{0,2,4,6,128,130,132,134,256,258,260,262,384,386,388,390},{1,3,5,7,129,..., dimensions={0} | all-to-all | bytes 1572864 | tf_op jit(solution)/shard_map/all_to_all | solution.py:36
  114.8 8.6 %collective-permute-start.8 = (bf16[16,12,16,128]{3,2,1,0:T(8,128)(2,1)S(1)}, bf16[16,12,16,128]{3,2,1,0:T(8,128)(2,1)S(1)}, u32[]{:S(2)}, u32[]{:S(2)}) collective-permute-start(bf16[16,12,16,128]{3,2,1,0:T(8,128)(2,1)S(1)} %all_to_all.28.mine_ref), channel_id=1, source_target_pairs={{0,1},{1,0},{2,3},{3,2},{4,5},{5,4},{6,7},{7,6},{8,9},{9,8},{10,11... | collective-permute-start | bytes 2359304 | tf_op jit(solution)/shard_map/ppermute | solution.py:32
  123.4 3.6 %shard_map.91 = bf16[256,640]{1,0:T(8,128)(2,1)} custom-call(f32[1]{0:T(128)S(6)} %exp.3.scale_ref, f32[1]{0:T(128)S(6)} %copy.10.bias_ref, f32[256,640]{1,0:T(8,128)S(1)} %get-tuple-element.19.total_ref, bf16[256,640]{1,0:T(8,128)(2,1)S(1)} %shard_map.85.txt_ref.rows_ref, bf16[256,1920]{1,0:T(8,128)(2,1)S(1)} %collective-permute-done.6.packed_ref.theirs_ref, ...), custom_call_target="tpu_custom_call" | custom-call | flops 671088640 | bytes 100000 | tf_op jit(solution)/shard_map/pallas_call | solution.py:54
  127.0 1.2 shard_map.96
  (34 shorter events, 4.0 us)
Async XLA Ops:
  0.6 8.4 %copy-start = (bf16[1152,640]{1,0:T(8,128)(2,1)S(1)}, bf16[1152,640]{1,0:T(8,128)(2,1)}, u32[]{:S(2)}) copy-start(bf16[1152,640]{1,0:T(8,128)(2,1)} %head_ref.1) | copy-start | bytes 4423684
  0.6 8.4 %copy-start.1 = (bf16[256,1152]{1,0:T(8,128)(2,1)S(1)}, bf16[256,1152]{1,0:T(8,128)(2,1)}, u32[]{:S(2)}) copy-start(bf16[256,1152]{1,0:T(8,128)(2,1)} %feat_ref.3) | copy-start | bytes 1769476
  0.7 1.1 copy-start.3
  1.8 7.3 %copy-start.9 = (s32[256]{0:T(256)S(1)}, s32[256]{0:T(256)}, u32[]{:S(2)}) copy-start(s32[256]{0:T(256)} %param.9) | copy-start | bytes 3076
  1.9 15.5 %collective-permute-start = (bf16[256,640]{1,0:T(8,128)(2,1)S(1)}, bf16[256,640]{1,0:T(8,128)(2,1)S(1)}, u32[]{:S(2)}, u32[]{:S(2)}) collective-permute-start(bf16[256,640]{1,0:T(8,128)(2,1)S(1)} %shard_map.85.txt_ref.rows_ref), channel_id=1, source_target_pairs={{0,7},{1,6},{2,5},{3,4},{4,3},{5,2},{6,1},{7,0},{8,15},{9,14},{10,... | collective-permute-start | bytes 983048 | tf_op jit(solution)/shard_map/ppermute | solution.py:32
  10.5 17.4 %collective-permute-start.1 = (bf16[256,640]{1,0:T(8,128)(2,1)S(1)}, bf16[256,640]{1,0:T(8,128)(2,1)S(1)}, u32[]{:S(2)}, u32[]{:S(2)}) collective-permute-start(bf16[256,640]{1,0:T(8,128)(2,1)S(1)} %shard_map.85.txt_ref.rows_ref), channel_id=1, source_target_pairs={{0,3},{1,2},{2,1},{3,0},{4,7},{5,6},{6,5},{7,4},{8,11},{9,10},{10,... | collective-permute-start | bytes 983048 | tf_op jit(solution)/shard_map/ppermute | solution.py:32
  12.5 16.1 %collective-permute-start.2 = (bf16[256,640]{1,0:T(8,128)(2,1)S(1)}, bf16[256,640]{1,0:T(8,128)(2,1)S(1)}, u32[]{:S(2)}, u32[]{:S(2)}) collective-permute-start(bf16[256,640]{1,0:T(8,128)(2,1)S(1)} %shard_map.85.txt_ref.rows_ref), channel_id=1, source_target_pairs={{0,1},{1,0},{2,3},{3,2},{4,5},{5,4},{6,7},{7,6},{8,9},{9,8},{10,11... | collective-permute-start | bytes 983048 | tf_op jit(solution)/shard_map/ppermute | solution.py:32
  17.4 11.8 %collective-permute-start.3 = (bf16[256,640]{1,0:T(8,128)(2,1)S(1)}, bf16[256,640]{1,0:T(8,128)(2,1)S(1)}, u32[]{:S(2)}, u32[]{:S(2)}) collective-permute-start(bf16[256,640]{1,0:T(8,128)(2,1)S(1)} %collective-permute-done.other_ref), channel_id=1, source_target_pairs={{0,8},{1,9},{2,10},{3,11},{4,12},{5,13},{6,14},{7,15},{8,0},{9,1},... | collective-permute-start | bytes 983048 | tf_op jit(solution)/shard_map/ppermute | solution.py:32
  19.6 13.3 %collective-permute-start.5 = (bf16[256,640]{1,0:T(8,128)(2,1)S(1)}, bf16[256,640]{1,0:T(8,128)(2,1)S(1)}, u32[]{:S(2)}, u32[]{:S(2)}) collective-permute-start(bf16[256,640]{1,0:T(8,128)(2,1)S(1)} %get-tuple-element.14.rows_ref), channel_id=1, source_target_pairs={{0,7},{1,6},{2,5},{3,4},{4,3},{5,2},{6,1},{7,0},{8,15},{9,14},{10,... | collective-permute-start | bytes 983048 | tf_op jit(solution)/shard_map/ppermute | solution.py:32
  24.6 11.1 %collective-permute-start.4 = (bf16[256,640]{1,0:T(8,128)(2,1)S(1)}, bf16[256,640]{1,0:T(8,128)(2,1)S(1)}, u32[]{:S(2)}, u32[]{:S(2)}) collective-permute-start(bf16[256,640]{1,0:T(8,128)(2,1)S(1)} %get-tuple-element.14.rows_ref), channel_id=1, source_target_pairs={{0,3},{1,2},{2,1},{3,0},{4,7},{5,6},{6,5},{7,4},{8,11},{9,10},{10,... | collective-permute-start | bytes 983048 | tf_op jit(solution)/shard_map/ppermute | solution.py:32
  30.1 10.8 %copy-start.2 = (bf16[256,1152]{1,0:T(8,128)(2,1)S(1)}, bf16[256,1152]{1,0:T(8,128)(2,1)}, u32[]{:S(2)}) copy-start(bf16[256,1152]{1,0:T(8,128)(2,1)} %feat_ref.3) | copy-start | bytes 1769476
  32.9 2.8 %copy-start.5 = (bf16[256,640]{1,0:T(8,128)(2,1)}, bf16[256,640]{1,0:T(8,128)(2,1)S(1)}, u32[]{:S(2)}) copy-start(bf16[256,640]{1,0:T(8,128)(2,1)S(1)} %collective-permute-done.5.b_ref) | copy-start | bytes 983044
  35.7 0.7 copy-start.7
  36.4 4.4 %collective-permute-start.6 = (bf16[256,1920]{1,0:T(8,128)(2,1)S(1)}, bf16[256,1920]{1,0:T(8,128)(2,1)S(1)}, u32[]{:S(2)}, u32[]{:S(2)}) collective-permute-start(bf16[256,1920]{1,0:T(8,128)(2,1)S(1)} %shard_map.90.mine_ref), channel_id=1, source_target_pairs={{0,1},{1,0},{2,3},{3,2},{4,5},{5,4},{6,7},{7,6},{8,9},{9,8},{10,11... | collective-permute-start | bytes 2949128 | tf_op jit(solution)/shard_map/ppermute | solution.py:32
  42.5 4.8 %copy-start.6 = (bf16[256,640]{1,0:T(8,128)(2,1)S(1)}, bf16[256,640]{1,0:T(8,128)(2,1)}, u32[]{:S(2)}) copy-start(bf16[256,640]{1,0:T(8,128)(2,1)} %copy-done.5) | copy-start | bytes 983044
  42.5 18.3 %all-to-all-start = ((bf16[16,12,16,128]{3,2,1,0:T(8,128)(2,1)}), bf16[16,12,16,128]{3,2,1,0:T(8,128)(2,1)S(1)}, u32[]{:S(2)}, u32[]{:S(2)}) async-start(bf16[16,12,16,128]{3,2,1,0:T(8,128)(2,1)} %shard_map.92), calls=%async_computation | async-start | bytes 1572864 | tf_op jit(solution)/shard_map/all_to_all | solution.py:36
  47.2 13.6 %collective-permute-start.7 = (bf16[256,640]{1,0:T(8,128)(2,1)S(1)}, bf16[256,640]{1,0:T(8,128)(2,1)}, u32[]{:S(2)}, u32[]{:S(2)}) collective-permute-start(bf16[256,640]{1,0:T(8,128)(2,1)S(1)} %copy-done.6), channel_id=1, source_target_pairs={{0,8},{1,9},{2,10},{3,11},{4,12},{5,13},{6,14},{7,15},{8,0},{9,1},... | collective-permute-start | bytes 983048 | tf_op jit(solution)/shard_map/ppermute | solution.py:32
  60.8 62.5 %copy-start.4 = (bf16[256,640]{1,0:T(8,128)(2,1)S(1)}, bf16[256,640]{1,0:T(8,128)(2,1)}, u32[]{:S(2)}) copy-start(bf16[256,640]{1,0:T(8,128)(2,1)} %txt_ref.3) | copy-start | bytes 983044
  60.9 62.5 %copy-start.8 = (bf16[256,640]{1,0:T(8,128)(2,1)S(1)}, bf16[256,640]{1,0:T(8,128)(2,1)}, u32[]{:S(2)}) copy-start(bf16[256,640]{1,0:T(8,128)(2,1)} %copy-done.7) | copy-start | bytes 983044
  114.8 12.3 %collective-permute-start.8 = (bf16[16,12,16,128]{3,2,1,0:T(8,128)(2,1)S(1)}, bf16[16,12,16,128]{3,2,1,0:T(8,128)(2,1)S(1)}, u32[]{:S(2)}, u32[]{:S(2)}) collective-permute-start(bf16[16,12,16,128]{3,2,1,0:T(8,128)(2,1)S(1)} %all_to_all.28.mine_ref), channel_id=1, source_target_pairs={{0,1},{1,0},{2,3},{3,2},{4,5},{5,4},{6,7},{7,6},{8,9},{9,8},{10,11... | collective-permute-start | bytes 2359304 | tf_op jit(solution)/shard_map/ppermute | solution.py:32

commit v6 on v5

--- a/solution.py
+++ b/solution.py
@@ -115,12 +115,16 @@
     packed_ref[:, 2 * E :] = feat_ref[...]
 
 
-def text_end_kernel(
-    scale_ref, bias_ref, total_ref, rows_ref, packed_ref, a_ref, b_ref, c_ref, txt_ref, out_ref
-):
+def text_pairs_kernel(scale_ref, bias_ref, total_ref, rows_ref, packed_ref, other_ref, out_ref):
     rows = rows_ref[...]
     total = total_ref[...] + pair_term(scale_ref, bias_ref, rows, packed_ref[:, E : 2 * E])
-    for other_ref in (a_ref, b_ref, c_ref):
+    out_ref[...] = total + pair_term(scale_ref, bias_ref, rows, other_ref[...])
+
+
+def text_end_kernel(scale_ref, bias_ref, total_ref, rows_ref, a_ref, b_ref, txt_ref, out_ref):
+    rows = rows_ref[...]
+    total = total_ref[...]
+    for other_ref in (a_ref, b_ref):
         total = total + pair_term(scale_ref, bias_ref, rows, other_ref[...])
     value = txt_ref[...].astype(F32)
     inverse = inverse_norm(value)
@@ -207,29 +211,41 @@
     late = after(txt_rows, img_rows)
     txt_3, txt_1 = swap(late, 3), swap(late, 1)
     img_7, img_3 = swap(img_rows, 7), swap(img_rows, 3)
-    txt_15, img_15 = swap(txt_7, 8), swap(img_7, 8)
+    txt_15 = swap(txt_7, 8)
     pair_specs = [SMEM, SMEM, VMEM, VMEM, VMEM]
     for other in (txt_7, txt_3, txt_1):
         d_img = call(pair_kernel, block, pair_specs, little, scale, bias, d_img, img_rows, other)
+    d_img = after(d_img, img_7)
     packed_img = call(
         image_end_kernel, packed, pair_specs + [VMEM] * 3, little,
         scale, bias, d_img, img_rows, txt_15, unit, inverse, other_feat,
     )
-    other_img = swap(after(packed_img, img_3, img_7), 1)
+    other_img = swap(after(packed_img, img_3), 1)
     d_img_feat = dot(packed_img[:, :E], head_weight, 1, 1).astype(BF16)
 
     parts = call(
         head_kernel, shape(OWNERS, SLABS, 16, 128, dtype=BF16), [SMEM] + [VMEM] * 3,
         4 * ROWS * D * E // 2, core, img_feat, packed_img, other_img,
     )
-    parts = exchange(after(parts, d_img_feat), PLANE)
+    parts = after(parts, d_img_feat)
+    d_txt = call(
+        text_pairs_kernel, block, pair_specs + [VMEM], 2 * pair,
+        scale, bias, after(d_txt, parts), txt_rows, other_img, img_3,
+    )
+    parts = exchange(parts, PLANE)
     slab = (16, 128)
     part = call(sum_kernel, shape(SLABS, *slab, dtype=BF16), [VMEM], little, parts)
-    part = after(part, img_15)
     quarters = shape(4, SLABS // 4, *slab, dtype=BF16)
-    parts = exchange(part.reshape(quarters.shape), NEAR)
-    parts = exchange(call(spread_sum_kernel, quarters, [VMEM], little, parts), FAR)
-    parts = exchange(call(spread_sum_kernel, quarters, [VMEM], little, parts), NEAR)
+    parts = exchange(after(part, d_txt).reshape(quarters.shape), NEAR)
+    parts = call(spread_sum_kernel, quarters, [VMEM], little, parts)
+    img_15 = swap(after(img_7, parts), 8)
+    parts = exchange(parts, FAR)
+    parts = call(spread_sum_kernel, quarters, [VMEM], little, parts)
+    parts = exchange(after(parts, img_15), NEAR)
+    d_txt_emb = call(
+        text_end_kernel, block16, pair_specs + [VMEM] * 2, 4 * pair,
+        scale, bias, d_txt, txt_rows, img_7, img_15, txt_emb,
+    )
     part = parts.reshape(SLABS, *slab)
     parts = exchange(after(jnp.broadcast_to(part[None], (OWNERS, SLABS, 16, 128))), PLANE)
     d_head = call(
@@ -239,10 +255,6 @@
         out_specs=pl.BlockSpec(memory_space=pl.ANY),
     )
 
-    d_txt_emb = call(
-        text_end_kernel, block16, pair_specs + [VMEM] * 4, 4 * pair,
-        scale, bias, d_txt, txt_rows, other_img, img_3, img_7, img_15, txt_emb,
-    )
     return (d_img_feat, d_txt_emb, d_head)
 
 

time: 129 us -> 129 us (level)
    pallas_call x12 -> x13, Pallas kernels: 11 us -> 10.1 us  [call(): pl.pallas_call(kernel, out_shape=out_shape, in_specs=specs, out_specs=out...]
  transfers between devices with their start and end apart: 10 -> 10, of which waited for: 4 -> 5; matrix products, arithmetic and copies ran while one was open for 1% -> 1% of each run, Pallas kernels for 6% -> 5%
where the time goes in v6:
time: 129 us; the launch traced here: 128 us
  blocking collectives  53.7 us (42%)
  starting transfers between devices  39.9 us (31%)
  waiting for transfers between devices  17.9 us (14%)
  Pallas kernels  10.1 us (8%)
  local copies, waits for them, and re-layouts  2.95 us (2%)
  between operations  2.24 us (2%)
  matrix products  1.48 us (1%)
    all_to_all x4, blocking collectives, exchange(): lax.all_to_all(value, 'dp', 0, 0, axis_index_groups=members, tiled=True)  53.7 us
    ppermute x9, starting transfers between devices, swap(): return lax.ppermute(value, 'dp', pairs)  35.7 us
    all_to_all x1, waiting for transfers between devices, exchange(): lax.all_to_all(value, 'dp', 0, 0, axis_index_groups=members, tiled=True)  11.5 us
    pallas_call x13, Pallas kernels, call(): pl.pallas_call(kernel, out_shape=out_shape, in_specs=specs, out_specs=out...  10.1 us
    ppermute x9, waiting for transfers between devices, swap(): return lax.ppermute(value, 'dp', pairs)  6.42 us
    all_to_all x1, starting transfers between devices, exchange(): lax.all_to_all(value, 'dp', 0, 0, axis_index_groups=members, tiled=True)  4.19 us
    unnamed x20, local copies, waits for them, and re-layouts  2.8 us
  transfers between devices with their start and end apart: 10, of which 5 were waited for; matrix products, arithmetic and copies ran while one was open for 1% of the time, Pallas kernels for 5%

profile of v6, /device:TPU:1, one launch (start us, length us, event | category | flops | bytes accessed | tf_op | source)
XLA Modules:
  0.0 128.4 jit_solution(4835904871376416003)
XLA Ops:
  0.7 1.1 copy-done.5
  1.9 5.9 %collective-permute-start = (bf16[256,640]{1,0:T(8,128)(2,1)S(1)}, bf16[256,640]{1,0:T(8,128)(2,1)S(1)}, u32[]{:S(2)}, u32[]{:S(2)}) collective-permute-start(bf16[256,640]{1,0:T(8,128)(2,1)S(1)} %shard_map.85.txt_ref.rows_ref), channel_id=1, source_target_pairs={{0,7},{1,6},{2,5},{3,4},{4,3},{5,2},{6,1},{7,0},{8,15},{9,14},{10,... | collective-permute-start | bytes 983048 | tf_op jit(solution)/shard_map/ppermute | solution.py:32
  9.2 1.5 %shard_map.86 = (f32[256,640]{1,0:T(8,128)S(1)}, f32[256,1]{1,0:T(8,128)S(1)}, bf16[256,640]{1,0:T(8,128)(2,1)S(1)}, f32[256,640]{1,0:T(8,128)S(1)}, f32[256,640...) custom-call(s32[1]{0:T(128)} %bitcast.core_ref, f32[1]{0:T(128)S(6)} %exp.3.scale_ref, f32[1]{0:T(128)S(6)} %copy.10.bias_ref, ...), custom_call_target="tpu_custom_call" | custom-call | flops 2013265920 | bytes 100000 | tf_op jit(solution)/shard_map/pallas_call | solution.py:54
  10.6 1.9 %collective-permute-start.1 = (bf16[256,640]{1,0:T(8,128)(2,1)S(1)}, bf16[256,640]{1,0:T(8,128)(2,1)S(1)}, u32[]{:S(2)}, u32[]{:S(2)}) collective-permute-start(bf16[256,640]{1,0:T(8,128)(2,1)S(1)} %shard_map.85.txt_ref.rows_ref), channel_id=1, source_target_pairs={{0,3},{1,2},{2,1},{3,0},{4,7},{5,6},{6,5},{7,4},{8,11},{9,10},{10,... | collective-permute-start | bytes 983048 | tf_op jit(solution)/shard_map/ppermute | solution.py:32
  12.6 4.9 %collective-permute-start.2 = (bf16[256,640]{1,0:T(8,128)(2,1)S(1)}, bf16[256,640]{1,0:T(8,128)(2,1)S(1)}, u32[]{:S(2)}, u32[]{:S(2)}) collective-permute-start(bf16[256,640]{1,0:T(8,128)(2,1)S(1)} %shard_map.85.txt_ref.rows_ref), channel_id=1, source_target_pairs={{0,1},{1,0},{2,3},{3,2},{4,5},{5,4},{6,7},{7,6},{8,9},{9,8},{10,11... | collective-permute-start | bytes 983048 | tf_op jit(solution)/shard_map/ppermute | solution.py:32
  17.5 4.9 %collective-permute-start.3 = (bf16[256,640]{1,0:T(8,128)(2,1)S(1)}, bf16[256,640]{1,0:T(8,128)(2,1)S(1)}, u32[]{:S(2)}, u32[]{:S(2)}) collective-permute-start(bf16[256,640]{1,0:T(8,128)(2,1)S(1)} %get-tuple-element.18.rows_ref), channel_id=1, source_target_pairs={{0,7},{1,6},{2,5},{3,4},{4,3},{5,2},{6,1},{7,0},{8,15},{9,14},{10,... | collective-permute-start | bytes 983048 | tf_op jit(solution)/shard_map/ppermute | solution.py:32
  22.4 1.9 %collective-permute-start.4 = (bf16[256,640]{1,0:T(8,128)(2,1)S(1)}, bf16[256,640]{1,0:T(8,128)(2,1)S(1)}, u32[]{:S(2)}, u32[]{:S(2)}) collective-permute-start(bf16[256,640]{1,0:T(8,128)(2,1)S(1)} %collective-permute-done.other_ref), channel_id=1, source_target_pairs={{0,8},{1,9},{2,10},{3,11},{4,12},{5,13},{6,14},{7,15},{8,0},{9,1},... | collective-permute-start | bytes 983048 | tf_op jit(solution)/shard_map/ppermute | solution.py:32
  24.3 3.0 %collective-permute-start.5 = (bf16[256,640]{1,0:T(8,128)(2,1)S(1)}, bf16[256,640]{1,0:T(8,128)(2,1)S(1)}, u32[]{:S(2)}, u32[]{:S(2)}) collective-permute-start(bf16[256,640]{1,0:T(8,128)(2,1)S(1)} %get-tuple-element.18.rows_ref), channel_id=1, source_target_pairs={{0,3},{1,2},{2,1},{3,0},{4,7},{5,6},{6,5},{7,4},{8,11},{9,10},{10,... | collective-permute-start | bytes 983048 | tf_op jit(solution)/shard_map/ppermute | solution.py:32
  29.9 3.7 %collective-permute-done.4.other_ref = bf16[256,640]{1,0:T(8,128)(2,1)S(1)} collective-permute-done((bf16[256,640]{1,0:T(8,128)(2,1)S(1)}, bf16[256,640]{1,0:T(8,128)(2,1)S(1)}, u32[]{:S(2)}, u32[]{:S(2)}) %collective-permute-start.4) | collective-permute-done | bytes 327712 | tf_op jit(solution)/shard_map/ppermute | solution.py:32
  34.4 1.1 collective-permute-done.5.other_ref
  36.3 2.0 %collective-permute-start.6 = (bf16[256,1920]{1,0:T(8,128)(2,1)S(1)}, bf16[256,1920]{1,0:T(8,128)(2,1)S(1)}, u32[]{:S(2)}, u32[]{:S(2)}) collective-permute-start(bf16[256,1920]{1,0:T(8,128)(2,1)S(1)} %shard_map.90.mine_ref), channel_id=1, source_target_pairs={{0,1},{1,0},{2,3},{3,2},{4,5},{5,4},{6,7},{7,6},{8,9},{9,8},{10,11... | collective-permute-start | bytes 2949128 | tf_op jit(solution)/shard_map/ppermute | solution.py:32
  38.2 1.5 %convolution_convert_fusion = bf16[256,1152]{1,0:T(8,128)(2,1)} fusion(bf16[1152,640]{1,0:T(8,128)(2,1)S(1)} %copy-done, bf16[256,1920]{1,0:T(8,128)(2,1)S(1)} %shard_map.90.mine_ref), kind=kOutput, calls=%fused_computation | convolution fusion | flops 377782272 | bytes 2392064 | tf_op jit(solution)/shard_map/dot_general | solution.py:48
  39.7 1.0 collective-permute-done.6.theirs_ref.packed_ref
  40.7 1.6 %shard_map.91 = bf16[16,12,16,128]{3,2,1,0:T(8,128)(2,1)} custom-call(s32[1]{0:T(128)} %bitcast.core_ref, bf16[256,1152]{1,0:T(8,128)(2,1)S(1)} %copy-done.2, bf16[256,1920]{1,0:T(8,128)(2,1)S(1)} %shard_map.90.mine_ref, bf16[256,1920]{1,0:T(8,128)(2,1)S(1)} %collective-permute-done.6.theirs_ref.packed_ref), custom_call_target="tpu_custom_call" | custom-call | flops 377487360 | bytes 100000 | tf_op jit(solution)/shard_map/pallas_call | solution.py:54
  42.3 4.2 %all-to-all-start = ((bf16[16,12,16,128]{3,2,1,0:T(8,128)(2,1)}), bf16[16,12,16,128]{3,2,1,0:T(8,128)(2,1)S(1)}, u32[]{:S(2)}, u32[]{:S(2)}) async-start(bf16[16,12,16,128]{3,2,1,0:T(8,128)(2,1)} %shard_map.91), calls=%async_computation | async-start | bytes 1572864 | tf_op jit(solution)/shard_map/all_to_all | solution.py:36
  48.5 11.5 %all-to-all-done.parts_ref = bf16[16,12,16,128]{3,2,1,0:T(8,128)(2,1)S(1)} async-done(((bf16[16,12,16,128]{3,2,1,0:T(8,128)(2,1)}), bf16[16,12,16,128]{3,2,1,0:T(8,128)(2,1)S(1)}, u32[]{:S(2)}, u32[]{:S(2)}) %all-to-all-start) | async-done | bytes 786464 | tf_op jit(solution)/shard_map/all_to_all | solution.py:36
  60.1 8.7 %all_to_all.25.parts_ref = bf16[4,3,16,128]{3,2,1,0:T(8,128)(2,1)S(1)} all-to-all(bf16[4,3,16,128]{3,2,1,0:T(8,128)(2,1)S(1)} %bitcast.5), channel_id=1, replica_groups={{0,8,16,24},{1,9,17,25},{2,10,18,26},{3,11,19,27},{4,12,20,28},{5,13,21..., dimensions={0} | all-to-all | bytes 98304 | tf_op jit(solution)/shard_map/all_to_all | solution.py:36
  68.9 2.5 %collective-permute-start.7 = (bf16[256,640]{1,0:T(8,128)(2,1)}, bf16[256,640]{1,0:T(8,128)(2,1)S(1)}, u32[]{:S(2)}, u32[]{:S(2)}) collective-permute-start(bf16[256,640]{1,0:T(8,128)(2,1)} %copy-done.7), channel_id=1, source_target_pairs={{0,8},{1,9},{2,10},{3,11},{4,12},{5,13},{6,14},{7,15},{8,0},{9,1},... | collective-permute-start | bytes 983048 | tf_op jit(solution)/shard_map/ppermute | solution.py:32
  71.4 24.1 %all_to_all.26.parts_ref = bf16[4,3,16,128]{3,2,1,0:T(8,128)(2,1)S(1)} all-to-all(bf16[4,3,16,128]{3,2,1,0:T(8,128)(2,1)S(1)} %shard_map.94), channel_id=1, replica_groups={{0,32,64,96},{1,33,65,97},{2,34,66,98},{3,35,67,99},{4,36,68,100},{5,37..., dimensions={0} | all-to-all | bytes 98304 | tf_op jit(solution)/shard_map/all_to_all | solution.py:36
  95.5 6.9 %all_to_all.27 = bf16[4,3,16,128]{3,2,1,0:T(8,128)(2,1)S(1)} all-to-all(bf16[4,3,16,128]{3,2,1,0:T(8,128)(2,1)S(1)} %shard_map.96), channel_id=1, replica_groups={{0,8,16,24},{1,9,17,25},{2,10,18,26},{3,11,19,27},{4,12,20,28},{5,13,21..., dimensions={0} | all-to-all | bytes 98304 | tf_op jit(solution)/shard_map/all_to_all | solution.py:36
  102.6 14.0 %all_to_all.28.mine_ref = bf16[16,12,16,128]{3,2,1,0:T(8,128)(2,1)S(1)} all-to-all(bf16[16,12,16,128]{3,2,1,0:T(8,128)(2,1)S(1)} %broadcast_in_dim.16), channel_id=1, replica_groups={{0,2,4,6,128,130,132,134,256,258,260,262,384,386,388,390},{1,3,5,7,129,..., dimensions={0} | all-to-all | bytes 1572864 | tf_op jit(solution)/shard_map/all_to_all | solution.py:36
  116.5 8.7 %collective-permute-start.8 = (bf16[16,12,16,128]{3,2,1,0:T(8,128)(2,1)S(1)}, bf16[16,12,16,128]{3,2,1,0:T(8,128)(2,1)S(1)}, u32[]{:S(2)}, u32[]{:S(2)}) collective-permute-start(bf16[16,12,16,128]{3,2,1,0:T(8,128)(2,1)S(1)} %all_to_all.28.mine_ref), channel_id=1, source_target_pairs={{0,1},{1,0},{2,3},{3,2},{4,5},{5,4},{6,7},{7,6},{8,9},{9,8},{10,11... | collective-permute-start | bytes 2359304 | tf_op jit(solution)/shard_map/ppermute | solution.py:32
  125.3 1.9 %shard_map.95 = bf16[256,640]{1,0:T(8,128)(2,1)} custom-call(f32[1]{0:T(128)S(6)} %exp.3.scale_ref, f32[1]{0:T(128)S(6)} %copy.10.bias_ref, f32[256,640]{1,0:T(8,128)S(1)} %shard_map.92.total_ref, bf16[256,640]{1,0:T(8,128)(2,1)S(1)} %shard_map.85.txt_ref.rows_ref, bf16[256,640]{1,0:T(8,128)(2,1)S(1)} %copy-done.8, ...), custom_call_target="tpu_custom_call" | custom-call | flops 671088640 | bytes 100000 | tf_op jit(solution)/shard_map/pallas_call | solution.py:54
  127.1 1.2 shard_map.97
  (35 shorter events, 6.5 us)
Async XLA Ops:
  0.6 8.5 %copy-start = (bf16[1152,640]{1,0:T(8,128)(2,1)S(1)}, bf16[1152,640]{1,0:T(8,128)(2,1)}, u32[]{:S(2)}) copy-start(bf16[1152,640]{1,0:T(8,128)(2,1)} %head_ref.1) | copy-start | bytes 4423684
  0.6 1.1 copy-start.5
  1.7 7.4 %copy-start.1 = (bf16[256,1152]{1,0:T(8,128)(2,1)S(1)}, bf16[256,1152]{1,0:T(8,128)(2,1)}, u32[]{:S(2)}) copy-start(bf16[256,1152]{1,0:T(8,128)(2,1)} %feat_ref.3) | copy-start | bytes 1769476
  1.7 7.4 %copy-start.9 = (s32[256]{0:T(256)S(1)}, s32[256]{0:T(256)}, u32[]{:S(2)}) copy-start(s32[256]{0:T(256)} %param.9) | copy-start | bytes 3076
  1.9 20.5 %collective-permute-start = (bf16[256,640]{1,0:T(8,128)(2,1)S(1)}, bf16[256,640]{1,0:T(8,128)(2,1)S(1)}, u32[]{:S(2)}, u32[]{:S(2)}) collective-permute-start(bf16[256,640]{1,0:T(8,128)(2,1)S(1)} %shard_map.85.txt_ref.rows_ref), channel_id=1, source_target_pairs={{0,7},{1,6},{2,5},{3,4},{4,3},{5,2},{6,1},{7,0},{8,15},{9,14},{10,... | collective-permute-start | bytes 983048 | tf_op jit(solution)/shard_map/ppermute | solution.py:32
  10.6 17.4 %collective-permute-start.1 = (bf16[256,640]{1,0:T(8,128)(2,1)S(1)}, bf16[256,640]{1,0:T(8,128)(2,1)S(1)}, u32[]{:S(2)}, u32[]{:S(2)}) collective-permute-start(bf16[256,640]{1,0:T(8,128)(2,1)S(1)} %shard_map.85.txt_ref.rows_ref), channel_id=1, source_target_pairs={{0,3},{1,2},{2,1},{3,0},{4,7},{5,6},{6,5},{7,4},{8,11},{9,10},{10,... | collective-permute-start | bytes 983048 | tf_op jit(solution)/shard_map/ppermute | solution.py:32
  12.6 16.1 %collective-permute-start.2 = (bf16[256,640]{1,0:T(8,128)(2,1)S(1)}, bf16[256,640]{1,0:T(8,128)(2,1)S(1)}, u32[]{:S(2)}, u32[]{:S(2)}) collective-permute-start(bf16[256,640]{1,0:T(8,128)(2,1)S(1)} %shard_map.85.txt_ref.rows_ref), channel_id=1, source_target_pairs={{0,1},{1,0},{2,3},{3,2},{4,5},{5,4},{6,7},{7,6},{8,9},{9,8},{10,11... | collective-permute-start | bytes 983048 | tf_op jit(solution)/shard_map/ppermute | solution.py:32
  17.5 12.4 %collective-permute-start.3 = (bf16[256,640]{1,0:T(8,128)(2,1)S(1)}, bf16[256,640]{1,0:T(8,128)(2,1)S(1)}, u32[]{:S(2)}, u32[]{:S(2)}) collective-permute-start(bf16[256,640]{1,0:T(8,128)(2,1)S(1)} %get-tuple-element.18.rows_ref), channel_id=1, source_target_pairs={{0,7},{1,6},{2,5},{3,4},{4,3},{5,2},{6,1},{7,0},{8,15},{9,14},{10,... | collective-permute-start | bytes 983048 | tf_op jit(solution)/shard_map/ppermute | solution.py:32
  22.4 11.2 %collective-permute-start.4 = (bf16[256,640]{1,0:T(8,128)(2,1)S(1)}, bf16[256,640]{1,0:T(8,128)(2,1)S(1)}, u32[]{:S(2)}, u32[]{:S(2)}) collective-permute-start(bf16[256,640]{1,0:T(8,128)(2,1)S(1)} %collective-permute-done.other_ref), channel_id=1, source_target_pairs={{0,8},{1,9},{2,10},{3,11},{4,12},{5,13},{6,14},{7,15},{8,0},{9,1},... | collective-permute-start | bytes 983048 | tf_op jit(solution)/shard_map/ppermute | solution.py:32
  24.3 11.2 %collective-permute-start.5 = (bf16[256,640]{1,0:T(8,128)(2,1)S(1)}, bf16[256,640]{1,0:T(8,128)(2,1)S(1)}, u32[]{:S(2)}, u32[]{:S(2)}) collective-permute-start(bf16[256,640]{1,0:T(8,128)(2,1)S(1)} %get-tuple-element.18.rows_ref), channel_id=1, source_target_pairs={{0,3},{1,2},{2,1},{3,0},{4,7},{5,6},{6,5},{7,4},{8,11},{9,10},{10,... | collective-permute-start | bytes 983048 | tf_op jit(solution)/shard_map/ppermute | solution.py:32
  29.9 4.4 %copy-start.7 = (bf16[256,640]{1,0:T(8,128)(2,1)}, bf16[256,640]{1,0:T(8,128)(2,1)S(1)}, u32[]{:S(2)}) copy-start(bf16[256,640]{1,0:T(8,128)(2,1)S(1)} %collective-permute-done.3.a_ref) | copy-start | bytes 983044
  34.4 6.3 %copy-start.2 = (bf16[256,1152]{1,0:T(8,128)(2,1)S(1)}, bf16[256,1152]{1,0:T(8,128)(2,1)}, u32[]{:S(2)}) copy-start(bf16[256,1152]{1,0:T(8,128)(2,1)} %feat_ref.3) | copy-start | bytes 1769476
  35.5 0.7 copy-start.3
  36.3 4.4 %collective-permute-start.6 = (bf16[256,1920]{1,0:T(8,128)(2,1)S(1)}, bf16[256,1920]{1,0:T(8,128)(2,1)S(1)}, u32[]{:S(2)}, u32[]{:S(2)}) collective-permute-start(bf16[256,1920]{1,0:T(8,128)(2,1)S(1)} %shard_map.90.mine_ref), channel_id=1, source_target_pairs={{0,1},{1,0},{2,3},{3,2},{4,5},{5,4},{6,7},{7,6},{8,9},{9,8},{10,11... | collective-permute-start | bytes 2949128 | tf_op jit(solution)/shard_map/ppermute | solution.py:32
  42.3 17.7 %all-to-all-start = ((bf16[16,12,16,128]{3,2,1,0:T(8,128)(2,1)}), bf16[16,12,16,128]{3,2,1,0:T(8,128)(2,1)S(1)}, u32[]{:S(2)}, u32[]{:S(2)}) async-start(bf16[16,12,16,128]{3,2,1,0:T(8,128)(2,1)} %shard_map.91), calls=%async_computation | async-start | bytes 1572864 | tf_op jit(solution)/shard_map/all_to_all | solution.py:36
  46.5 1.0 copy-start.4
  60.1 65.1 %copy-start.6 = (bf16[256,640]{1,0:T(8,128)(2,1)S(1)}, bf16[256,640]{1,0:T(8,128)(2,1)}, u32[]{:S(2)}) copy-start(bf16[256,640]{1,0:T(8,128)(2,1)} %txt_ref.3) | copy-start | bytes 983044
  60.1 65.1 %copy-start.8 = (bf16[256,640]{1,0:T(8,128)(2,1)S(1)}, bf16[256,640]{1,0:T(8,128)(2,1)}, u32[]{:S(2)}) copy-start(bf16[256,640]{1,0:T(8,128)(2,1)} %copy-done.7) | copy-start | bytes 983044
  68.9 26.6 %collective-permute-start.7 = (bf16[256,640]{1,0:T(8,128)(2,1)}, bf16[256,640]{1,0:T(8,128)(2,1)S(1)}, u32[]{:S(2)}, u32[]{:S(2)}) collective-permute-start(bf16[256,640]{1,0:T(8,128)(2,1)} %copy-done.7), channel_id=1, source_target_pairs={{0,8},{1,9},{2,10},{3,11},{4,12},{5,13},{6,14},{7,15},{8,0},{9,1},... | collective-permute-start | bytes 983048 | tf_op jit(solution)/shard_map/ppermute | solution.py:32
  116.5 10.6 %collective-permute-start.8 = (bf16[16,12,16,128]{3,2,1,0:T(8,128)(2,1)S(1)}, bf16[16,12,16,128]{3,2,1,0:T(8,128)(2,1)S(1)}, u32[]{:S(2)}, u32[]{:S(2)}) collective-permute-start(bf16[16,12,16,128]{3,2,1,0:T(8,128)(2,1)S(1)} %all_to_all.28.mine_ref), channel_id=1, source_target_pairs={{0,1},{1,0},{2,3},{3,2},{4,5},{5,4},{6,7},{7,6},{8,9},{9,8},{10,11... | collective-permute-start | bytes 2359304 | tf_op jit(solution)/shard_map/ppermute | solution.py:32

commit v7 on v6

--- a/solution.py
+++ b/solution.py
@@ -51,6 +51,7 @@
 
 
 def call(kernel, out_shape, specs, flops, *operands, scratch=(), out_specs=None):
+    moved = sum(x.size * x.dtype.itemsize for x in (*operands, *jax.tree.leaves(out_shape)))
     return pl.pallas_call(
         kernel,
         out_shape=out_shape,
@@ -58,7 +59,7 @@
         out_specs=out_specs if out_specs is not None else jax.tree.map(lambda _: VMEM, out_shape),
         scratch_shapes=scratch,
         compiler_params=pltpu.CompilerParams(vmem_limit_bytes=14 << 20),
-        cost_estimate=pl.CostEstimate(flops=flops, bytes_accessed=100000, transcendentals=0),
+        cost_estimate=pl.CostEstimate(flops=flops, bytes_accessed=moved, transcendentals=0),
     )(*operands)
 
 
@@ -115,17 +116,19 @@
     packed_ref[:, 2 * E :] = feat_ref[...]
 
 
-def text_pairs_kernel(scale_ref, bias_ref, total_ref, rows_ref, packed_ref, other_ref, out_ref):
+def text_first_kernel(scale_ref, bias_ref, total_ref, rows_ref, packed_ref, out_ref):
+    term = pair_term(scale_ref, bias_ref, rows_ref[...], packed_ref[:, E : 2 * E])
+    out_ref[...] = total_ref[...] + term
+
+
+def text_pairs_kernel(scale_ref, bias_ref, total_ref, rows_ref, a_ref, b_ref, out_ref):
     rows = rows_ref[...]
-    total = total_ref[...] + pair_term(scale_ref, bias_ref, rows, packed_ref[:, E : 2 * E])
-    out_ref[...] = total + pair_term(scale_ref, bias_ref, rows, other_ref[...])
-
-
-def text_end_kernel(scale_ref, bias_ref, total_ref, rows_ref, a_ref, b_ref, txt_ref, out_ref):
-    rows = rows_ref[...]
-    total = total_ref[...]
-    for other_ref in (a_ref, b_ref):
-        total = total + pair_term(scale_ref, bias_ref, rows, other_ref[...])
+    total = total_ref[...] + pair_term(scale_ref, bias_ref, rows, a_ref[...])
+    out_ref[...] = total + pair_term(scale_ref, bias_ref, rows, b_ref[...])
+
+
+def text_end_kernel(scale_ref, bias_ref, total_ref, rows_ref, other_ref, txt_ref, out_ref):
+    total = total_ref[...] + pair_term(scale_ref, bias_ref, rows_ref[...], other_ref[...])
     value = txt_ref[...].astype(F32)
     inverse = inverse_norm(value)
     out_ref[...] = tangent(scale_ref[0] * total, value * inverse, inverse)
@@ -200,7 +203,7 @@
 
     packed = shape(ROWS, 3 * E, dtype=BF16)
     txt_rows = call(text_kernel, block16, [VMEM], 40 * pair, txt_emb)
-    txt_7 = swap(txt_rows, 7)
+    txt_15 = swap(txt_rows, 15)
     unit, inverse, img_rows, d_img, d_txt, other_feat = call(
         image_kernel,
         (block, shape(ROWS, 1), block16, block, block, block16),
@@ -208,19 +211,16 @@
         12 * pair,
         core, scale, bias, labels[None, :], img_feat, head_weight, txt_rows,
     )
+    pair_specs = [SMEM, SMEM, VMEM, VMEM, VMEM]
     late = after(txt_rows, img_rows)
-    txt_3, txt_1 = swap(late, 3), swap(late, 1)
-    img_7, img_3 = swap(img_rows, 7), swap(img_rows, 3)
-    txt_15 = swap(txt_7, 8)
-    pair_specs = [SMEM, SMEM, VMEM, VMEM, VMEM]
-    for other in (txt_7, txt_3, txt_1):
+    txt_3, txt_7, txt_1 = swap(late, 3), swap(late, 7), swap(late, 1)
+    for other in (txt_15, txt_3, txt_7):
         d_img = call(pair_kernel, block, pair_specs, little, scale, bias, d_img, img_rows, other)
-    d_img = after(d_img, img_7)
     packed_img = call(
         image_end_kernel, packed, pair_specs + [VMEM] * 3, little,
-        scale, bias, d_img, img_rows, txt_15, unit, inverse, other_feat,
-    )
-    other_img = swap(after(packed_img, img_3), 1)
+        scale, bias, d_img, img_rows, txt_1, unit, inverse, other_feat,
+    )
+    other_img = swap(packed_img, 1)
     d_img_feat = dot(packed_img[:, :E], head_weight, 1, 1).astype(BF16)
 
     parts = call(
@@ -228,23 +228,29 @@
         4 * ROWS * D * E // 2, core, img_feat, packed_img, other_img,
     )
     parts = after(parts, d_img_feat)
+    late = after(img_rows, parts)
+    img_7, img_15, img_3 = swap(late, 7), swap(late, 15), swap(late, 3)
     d_txt = call(
-        text_pairs_kernel, block, pair_specs + [VMEM], 2 * pair,
-        scale, bias, after(d_txt, parts), txt_rows, other_img, img_3,
+        text_first_kernel, block, pair_specs, pair,
+        scale, bias, after(d_txt, parts), txt_rows, other_img,
     )
     parts = exchange(parts, PLANE)
     slab = (16, 128)
     part = call(sum_kernel, shape(SLABS, *slab, dtype=BF16), [VMEM], little, parts)
+    part = after(part, d_txt)
     quarters = shape(4, SLABS // 4, *slab, dtype=BF16)
-    parts = exchange(after(part, d_txt).reshape(quarters.shape), NEAR)
+    parts = exchange(part.reshape(quarters.shape), NEAR)
     parts = call(spread_sum_kernel, quarters, [VMEM], little, parts)
-    img_15 = swap(after(img_7, parts), 8)
-    parts = exchange(parts, FAR)
+    d_txt = call(
+        text_pairs_kernel, block, pair_specs + [VMEM], 2 * pair,
+        scale, bias, after(d_txt, parts), txt_rows, img_3, img_7,
+    )
+    parts = after(exchange(parts, FAR), d_txt, img_15)
     parts = call(spread_sum_kernel, quarters, [VMEM], little, parts)
-    parts = exchange(after(parts, img_15), NEAR)
+    parts = exchange(parts, NEAR)
     d_txt_emb = call(
-        text_end_kernel, block16, pair_specs + [VMEM] * 2, 4 * pair,
-        scale, bias, d_txt, txt_rows, img_7, img_15, txt_emb,
+        text_end_kernel, block16, pair_specs + [VMEM], pair,
+        scale, bias, d_txt, txt_rows, img_15, txt_emb,
     )
     part = parts.reshape(SLABS, *slab)
     parts = exchange(after(jnp.broadcast_to(part[None], (OWNERS, SLABS, 16, 128))), PLANE)

time: 129 us -> 121 us (0.938)
  blocking collectives: 53.7 us -> 33.4 us
  starting transfers between devices: 39.9 us -> 51.8 us
  Pallas kernels: 10.1 us -> 12.2 us
    all_to_all x4 -> x3, blocking collectives: 53.7 us -> 33.4 us  [exchange(): lax.all_to_all(value, 'dp', 0, 0, axis_index_groups=members, tiled=True)]
    all_to_all x1 -> x2, starting transfers between devices: 4.19 us -> 16.8 us  [exchange(): lax.all_to_all(value, 'dp', 0, 0, axis_index_groups=members, tiled=True)]
    pallas_call x13 -> x14, Pallas kernels: 10.1 us -> 12.2 us  [call(): pl.pallas_call(kernel, out_shape=out_shape, in_specs=specs, out_specs=out...]
    all_to_all x1 -> x2, waiting for transfers between devices: 11.5 us -> 10.4 us  [exchange(): lax.all_to_all(value, 'dp', 0, 0, axis_index_groups=members, tiled=True)]
    unnamed x20 -> x16, local copies, waits for them, and re-layouts: 2.8 us -> 2.19 us
  transfers between devices with their start and end apart: 10 -> 11, of which waited for: 5 -> 6; matrix products, arithmetic and copies ran while one was open for 1% -> 1% of each run, Pallas kernels for 5% -> 7%
where the time goes in v7:
time: 121 us
  starting transfers between devices  51.8 us (43%)
  blocking collectives  33.4 us (28%)
  waiting for transfers between devices  17.1 us (14%)
  Pallas kernels  12.2 us (10%)
  local copies, waits for them, and re-layouts  2.33 us (2%)
  between operations  2.24 us (2%)
  matrix products  1.48 us (1%)
    ppermute x9, starting transfers between devices, swap(): return lax.ppermute(value, 'dp', pairs)  35 us
    all_to_all x3, blocking collectives, exchange(): lax.all_to_all(value, 'dp', 0, 0, axis_index_groups=members, tiled=True)  33.4 us
    all_to_all x2, starting transfers between devices, exchange(): lax.all_to_all(value, 'dp', 0, 0, axis_index_groups=members, tiled=True)  16.8 us
    pallas_call x14, Pallas kernels, call(): pl.pallas_call(kernel, out_shape=out_shape, in_specs=specs, out_specs=out...  12.2 us
    all_to_all x2, waiting for transfers between devices, exchange(): lax.all_to_all(value, 'dp', 0, 0, axis_index_groups=members, tiled=True)  10.4 us
    ppermute x9, waiting for transfers between devices, swap(): return lax.ppermute(value, 'dp', pairs)  6.67 us
  transfers between devices with their start and end apart: 11, of which 6 were waited for; matrix products, arithmetic and copies ran while one was open for 1% of the time, Pallas kernels for 7%

profile of v7, /device:TPU:1, one launch (start us, length us, event | category | flops | bytes accessed | tf_op | source)
XLA Modules:
  0.0 120.5 jit_solution(2905196557219307947)
XLA Ops:
  1.9 7.3 %collective-permute-start = (bf16[256,640]{1,0:T(8,128)(2,1)S(1)}, bf16[256,640]{1,0:T(8,128)(2,1)S(1)}, u32[]{:S(2)}, u32[]{:S(2)}) collective-permute-start(bf16[256,640]{1,0:T(8,128)(2,1)S(1)} %shard_map.85.txt_ref.rows_ref), channel_id=1, source_target_pairs={{0,15},{1,14},{2,13},{3,12},{4,11},{5,10},{6,9},{7,8},{8,7},{9,6},... | collective-permute-start | bytes 983048 | tf_op jit(solution)/shard_map/ppermute | solution.py:32
  10.5 1.5 %shard_map.86 = (f32[256,640]{1,0:T(8,128)S(1)}, f32[256,1]{1,0:T(8,128)S(1)}, bf16[256,640]{1,0:T(8,128)(2,1)S(1)}, f32[256,640]{1,0:T(8,128)S(1)}, f32[256,640...) custom-call(s32[1]{0:T(128)} %bitcast.core_ref, f32[1]{0:T(128)S(6)} %exp.3.scale_ref, f32[1]{0:T(128)S(6)} %copy.10.bias_ref, ...), custom_call_target="tpu_custom_call" | custom-call | flops 2013265920 | bytes 5015564 | tf_op jit(solution)/shard_map/pallas_call | solution.py:55
  12.0 1.9 %collective-permute-start.1 = (bf16[256,640]{1,0:T(8,128)(2,1)S(1)}, bf16[256,640]{1,0:T(8,128)(2,1)S(1)}, u32[]{:S(2)}, u32[]{:S(2)}) collective-permute-start(bf16[256,640]{1,0:T(8,128)(2,1)S(1)} %shard_map.85.txt_ref.rows_ref), channel_id=1, source_target_pairs={{0,3},{1,2},{2,1},{3,0},{4,7},{5,6},{6,5},{7,4},{8,11},{9,10},{10,... | collective-permute-start | bytes 983048 | tf_op jit(solution)/shard_map/ppermute | solution.py:32
  13.9 3.0 %collective-permute-start.2 = (bf16[256,640]{1,0:T(8,128)(2,1)S(1)}, bf16[256,640]{1,0:T(8,128)(2,1)S(1)}, u32[]{:S(2)}, u32[]{:S(2)}) collective-permute-start(bf16[256,640]{1,0:T(8,128)(2,1)S(1)} %shard_map.85.txt_ref.rows_ref), channel_id=1, source_target_pairs={{0,7},{1,6},{2,5},{3,4},{4,3},{5,2},{6,1},{7,0},{8,15},{9,14},{10,... | collective-permute-start | bytes 983048 | tf_op jit(solution)/shard_map/ppermute | solution.py:32
  16.9 2.5 %collective-permute-start.3 = (bf16[256,640]{1,0:T(8,128)(2,1)S(1)}, bf16[256,640]{1,0:T(8,128)(2,1)S(1)}, u32[]{:S(2)}, u32[]{:S(2)}) collective-permute-start(bf16[256,640]{1,0:T(8,128)(2,1)S(1)} %shard_map.85.txt_ref.rows_ref), channel_id=1, source_target_pairs={{0,1},{1,0},{2,3},{3,2},{4,5},{5,4},{6,7},{7,6},{8,9},{9,8},{10,11... | collective-permute-start | bytes 983048 | tf_op jit(solution)/shard_map/ppermute | solution.py:32
  20.1 3.1 %collective-permute-done.1.other_ref = bf16[256,640]{1,0:T(8,128)(2,1)S(1)} collective-permute-done((bf16[256,640]{1,0:T(8,128)(2,1)S(1)}, bf16[256,640]{1,0:T(8,128)(2,1)S(1)}, u32[]{:S(2)}, u32[]{:S(2)}) %collective-permute-start.1) | collective-permute-done | bytes 327712 | tf_op jit(solution)/shard_map/ppermute | solution.py:32
  23.9 2.5 %collective-permute-done.2.other_ref = bf16[256,640]{1,0:T(8,128)(2,1)S(1)} collective-permute-done((bf16[256,640]{1,0:T(8,128)(2,1)S(1)}, bf16[256,640]{1,0:T(8,128)(2,1)S(1)}, u32[]{:S(2)}, u32[]{:S(2)}) %collective-permute-start.2) | collective-permute-done | bytes 327712 | tf_op jit(solution)/shard_map/ppermute | solution.py:32
  27.8 3.3 %collective-permute-start.4 = (bf16[256,1920]{1,0:T(8,128)(2,1)S(1)}, bf16[256,1920]{1,0:T(8,128)(2,1)S(1)}, u32[]{:S(2)}, u32[]{:S(2)}) collective-permute-start(bf16[256,1920]{1,0:T(8,128)(2,1)S(1)} %shard_map.90.mine_ref), channel_id=1, source_target_pairs={{0,1},{1,0},{2,3},{3,2},{4,5},{5,4},{6,7},{7,6},{8,9},{9,8},{10,11... | collective-permute-start | bytes 2949128 | tf_op jit(solution)/shard_map/ppermute | solution.py:32
  31.1 1.5 %convolution_convert_fusion = bf16[256,1152]{1,0:T(8,128)(2,1)} fusion(bf16[1152,640]{1,0:T(8,128)(2,1)S(1)} %copy-done.1, bf16[256,1920]{1,0:T(8,128)(2,1)S(1)} %shard_map.90.mine_ref), kind=kOutput, calls=%fused_computation | convolution fusion | flops 377782272 | bytes 2392064 | tf_op jit(solution)/shard_map/dot_general | solution.py:48
  33.3 1.6 %shard_map.91 = bf16[16,12,16,128]{3,2,1,0:T(8,128)(2,1)} custom-call(s32[1]{0:T(128)} %bitcast.core_ref, bf16[256,1152]{1,0:T(8,128)(2,1)S(1)} %copy-done.4, bf16[256,1920]{1,0:T(8,128)(2,1)S(1)} %shard_map.90.mine_ref, bf16[256,1920]{1,0:T(8,128)(2,1)S(1)} %collective-permute-done.4.theirs_ref.packed_ref), custom_call_target="tpu_custom_call" | custom-call | flops 377487360 | bytes 3342340 | tf_op jit(solution)/shard_map/pallas_call | solution.py:55
  34.9 4.5 %all-to-all-start = ((bf16[16,12,16,128]{3,2,1,0:T(8,128)(2,1)}), bf16[16,12,16,128]{3,2,1,0:T(8,128)(2,1)S(1)}, u32[]{:S(2)}, u32[]{:S(2)}) async-start(bf16[16,12,16,128]{3,2,1,0:T(8,128)(2,1)} %shard_map.91), calls=%async_computation | async-start | bytes 1572864 | tf_op jit(solution)/shard_map/all_to_all | solution.py:36
  39.4 4.1 %collective-permute-start.5 = (bf16[256,640]{1,0:T(8,128)(2,1)S(1)}, bf16[256,640]{1,0:T(8,128)(2,1)}, u32[]{:S(2)}, u32[]{:S(2)}) collective-permute-start(bf16[256,640]{1,0:T(8,128)(2,1)S(1)} %get-tuple-element.27.rows_ref), channel_id=1, source_target_pairs={{0,3},{1,2},{2,1},{3,0},{4,7},{5,6},{6,5},{7,4},{8,11},{9,10},{10,... | collective-permute-start | bytes 983048 | tf_op jit(solution)/shard_map/ppermute | solution.py:32
  43.5 3.2 %collective-permute-start.6 = (bf16[256,640]{1,0:T(8,128)(2,1)S(1)}, bf16[256,640]{1,0:T(8,128)(2,1)}, u32[]{:S(2)}, u32[]{:S(2)}) collective-permute-start(bf16[256,640]{1,0:T(8,128)(2,1)S(1)} %get-tuple-element.27.rows_ref), channel_id=1, source_target_pairs={{0,7},{1,6},{2,5},{3,4},{4,3},{5,2},{6,1},{7,0},{8,15},{9,14},{10,... | collective-permute-start | bytes 983048 | tf_op jit(solution)/shard_map/ppermute | solution.py:32
  46.7 3.7 %collective-permute-start.7 = (bf16[256,640]{1,0:T(8,128)(2,1)S(1)}, bf16[256,640]{1,0:T(8,128)(2,1)S(1)}, u32[]{:S(2)}, u32[]{:S(2)}) collective-permute-start(bf16[256,640]{1,0:T(8,128)(2,1)S(1)} %get-tuple-element.27.rows_ref), channel_id=1, source_target_pairs={{0,15},{1,14},{2,13},{3,12},{4,11},{5,10},{6,9},{7,8},{8,7},{9,6},... | collective-permute-start | bytes 983048 | tf_op jit(solution)/shard_map/ppermute | solution.py:32
  50.4 1.1 copy-done.3
  53.1 9.1 %all_to_all.25.parts_ref = bf16[4,3,16,128]{3,2,1,0:T(8,128)(2,1)S(1)} all-to-all(bf16[4,3,16,128]{3,2,1,0:T(8,128)(2,1)S(1)} %bitcast.5), channel_id=1, replica_groups={{0,8,16,24},{1,9,17,25},{2,10,18,26},{3,11,19,27},{4,12,20,28},{5,13,21..., dimensions={0} | all-to-all | bytes 98304 | tf_op jit(solution)/shard_map/all_to_all | solution.py:36
  62.8 12.3 %all-to-all-start.2 = ((bf16[4,3,16,128]{3,2,1,0:T(8,128)(2,1)}), bf16[4,3,16,128]{3,2,1,0:T(8,128)(2,1)S(1)}, u32[]{:S(2)}, u32[]{:S(2)}) async-start(bf16[4,3,16,128]{3,2,1,0:T(8,128)(2,1)} %shard_map.94), calls=%async_computation.2 | async-start | bytes 98304 | tf_op jit(solution)/shard_map/all_to_all | solution.py:36
  75.2 2.1 %shard_map.95.total_ref = f32[256,640]{1,0:T(8,128)S(1)} custom-call(f32[1]{0:T(128)S(6)} %exp.3.scale_ref, f32[1]{0:T(128)S(6)} %copy.10.bias_ref, f32[256,640]{1,0:T(8,128)S(1)} %shard_map.92.total_ref, bf16[256,640]{1,0:T(8,128)(2,1)S(1)} %shard_map.85.txt_ref.rows_ref, bf16[256,640]{1,0:T(8,128)(2,1)} %collective-permute-done.5.a_ref, ...), custom_call_target="tpu_custom_call" | custom-call | flops 335544320 | bytes 2293768 | tf_op jit(solution)/shard_map/pallas_call | solution.py:55
  77.3 9.6 %all-to-all-done.2.parts_ref = bf16[4,3,16,128]{3,2,1,0:T(8,128)(2,1)S(1)} async-done(((bf16[4,3,16,128]{3,2,1,0:T(8,128)(2,1)}), bf16[4,3,16,128]{3,2,1,0:T(8,128)(2,1)S(1)}, u32[]{:S(2)}, u32[]{:S(2)}) %all-to-all-start.2) | async-done | bytes 49184 | tf_op jit(solution)/shard_map/all_to_all | solution.py:36
  86.9 7.3 %all_to_all.26 = bf16[4,3,16,128]{3,2,1,0:T(8,128)(2,1)S(1)} all-to-all(bf16[4,3,16,128]{3,2,1,0:T(8,128)(2,1)S(1)} %shard_map.97), channel_id=1, replica_groups={{0,8,16,24},{1,9,17,25},{2,10,18,26},{3,11,19,27},{4,12,20,28},{5,13,21..., dimensions={0} | all-to-all | bytes 98304 | tf_op jit(solution)/shard_map/all_to_all | solution.py:36
  94.4 17.0 %all_to_all.27.mine_ref = bf16[16,12,16,128]{3,2,1,0:T(8,128)(2,1)S(1)} all-to-all(bf16[16,12,16,128]{3,2,1,0:T(8,128)(2,1)S(1)} %broadcast_in_dim.16), channel_id=1, replica_groups={{0,2,4,6,128,130,132,134,256,258,260,262,384,386,388,390},{1,3,5,7,129,..., dimensions={0} | all-to-all | bytes 1572864 | tf_op jit(solution)/shard_map/all_to_all | solution.py:36
  111.4 6.1 %collective-permute-start.8 = (bf16[16,12,16,128]{3,2,1,0:T(8,128)(2,1)S(1)}, bf16[16,12,16,128]{3,2,1,0:T(8,128)(2,1)S(1)}, u32[]{:S(2)}, u32[]{:S(2)}) collective-permute-start(bf16[16,12,16,128]{3,2,1,0:T(8,128)(2,1)S(1)} %all_to_all.27.mine_ref), channel_id=1, source_target_pairs={{0,1},{1,0},{2,3},{3,2},{4,5},{5,4},{6,7},{7,6},{8,9},{9,8},{10,11... | collective-permute-start | bytes 2359304 | tf_op jit(solution)/shard_map/ppermute | solution.py:32
  117.4 1.5 %shard_map.96 = bf16[256,640]{1,0:T(8,128)(2,1)} custom-call(f32[1]{0:T(128)S(6)} %exp.3.scale_ref, f32[1]{0:T(128)S(6)} %copy.10.bias_ref, f32[256,640]{1,0:T(8,128)S(1)} %shard_map.95.total_ref, bf16[256,640]{1,0:T(8,128)(2,1)S(1)} %shard_map.85.txt_ref.rows_ref, bf16[256,640]{1,0:T(8,128)(2,1)S(1)} %collective-permute-done.7.other_ref, ...), custom_call_target="tpu_custom_call" | custom-call | flops 167772160 | bytes 1966088 | tf_op jit(solution)/shard_map/pallas_call | solution.py:55
  119.3 1.2 %shard_map.98 = bf16[1152,640]{1,0:T(8,128)(2,1)} custom-call(s32[1]{0:T(128)} %bitcast.core_ref, bf16[16,12,16,128]{3,2,1,0:T(8,128)(2,1)S(1)} %all_to_all.27.mine_ref, bf16[16,12,16,128]{3,2,1,0:T(8,128)(2,1)S(1)} %collective-permute-done.8.theirs_ref), custom_call_target="tpu_custom_call" | custom-call | bytes 3047428 | tf_op jit(solution)/shard_map/pallas_call | solution.py:55
  (33 shorter events, 7.4 us)
Async XLA Ops:
  0.6 9.9 %copy-start = (bf16[1152,640]{1,0:T(8,128)(2,1)S(1)}, bf16[1152,640]{1,0:T(8,128)(2,1)}, u32[]{:S(2)}) copy-start(bf16[1152,640]{1,0:T(8,128)(2,1)} %head_ref.1) | copy-start | bytes 4423684
  0.6 1.1 copy-start.5
  1.7 8.8 %copy-start.4 = (bf16[256,1152]{1,0:T(8,128)(2,1)S(1)}, bf16[256,1152]{1,0:T(8,128)(2,1)}, u32[]{:S(2)}) copy-start(bf16[256,1152]{1,0:T(8,128)(2,1)} %feat_ref.3) | copy-start | bytes 1769476
  1.7 8.8 %copy-start.7 = (s32[256]{0:T(256)S(1)}, s32[256]{0:T(256)}, u32[]{:S(2)}) copy-start(s32[256]{0:T(256)} %param.9) | copy-start | bytes 3076
  1.9 17.6 %collective-permute-start = (bf16[256,640]{1,0:T(8,128)(2,1)S(1)}, bf16[256,640]{1,0:T(8,128)(2,1)S(1)}, u32[]{:S(2)}, u32[]{:S(2)}) collective-permute-start(bf16[256,640]{1,0:T(8,128)(2,1)S(1)} %shard_map.85.txt_ref.rows_ref), channel_id=1, source_target_pairs={{0,15},{1,14},{2,13},{3,12},{4,11},{5,10},{6,9},{7,8},{8,7},{9,6},... | collective-permute-start | bytes 983048 | tf_op jit(solution)/shard_map/ppermute | solution.py:32
  12.0 11.9 %copy-start.2 = (f32[256,640]{1,0:T(8,128)}, f32[256,640]{1,0:T(8,128)S(1)}, u32[]{:S(2)}) copy-start(f32[256,640]{1,0:T(8,128)S(1)} %get-tuple-element.24.total_ref) | copy-start | bytes 1966084
  12.0 11.2 %collective-permute-start.1 = (bf16[256,640]{1,0:T(8,128)(2,1)S(1)}, bf16[256,640]{1,0:T(8,128)(2,1)S(1)}, u32[]{:S(2)}, u32[]{:S(2)}) collective-permute-start(bf16[256,640]{1,0:T(8,128)(2,1)S(1)} %shard_map.85.txt_ref.rows_ref), channel_id=1, source_target_pairs={{0,3},{1,2},{2,1},{3,0},{4,7},{5,6},{6,5},{7,4},{8,11},{9,10},{10,... | collective-permute-start | bytes 983048 | tf_op jit(solution)/shard_map/ppermute | solution.py:32
  13.9 12.4 %collective-permute-start.2 = (bf16[256,640]{1,0:T(8,128)(2,1)S(1)}, bf16[256,640]{1,0:T(8,128)(2,1)S(1)}, u32[]{:S(2)}, u32[]{:S(2)}) collective-permute-start(bf16[256,640]{1,0:T(8,128)(2,1)S(1)} %shard_map.85.txt_ref.rows_ref), channel_id=1, source_target_pairs={{0,7},{1,6},{2,5},{3,4},{4,3},{5,2},{6,1},{7,0},{8,15},{9,14},{10,... | collective-permute-start | bytes 983048 | tf_op jit(solution)/shard_map/ppermute | solution.py:32
  16.9 10.1 %collective-permute-start.3 = (bf16[256,640]{1,0:T(8,128)(2,1)S(1)}, bf16[256,640]{1,0:T(8,128)(2,1)S(1)}, u32[]{:S(2)}, u32[]{:S(2)}) collective-permute-start(bf16[256,640]{1,0:T(8,128)(2,1)S(1)} %shard_map.85.txt_ref.rows_ref), channel_id=1, source_target_pairs={{0,1},{1,0},{2,3},{3,2},{4,5},{5,4},{6,7},{7,6},{8,9},{9,8},{10,11... | collective-permute-start | bytes 983048 | tf_op jit(solution)/shard_map/ppermute | solution.py:32
  27.0 4.1 %copy-start.1 = (bf16[1152,640]{1,0:T(8,128)(2,1)S(1)}, bf16[1152,640]{1,0:T(8,128)(2,1)}, u32[]{:S(2)}) copy-start(bf16[1152,640]{1,0:T(8,128)(2,1)} %head_ref.1) | copy-start | bytes 4423684
  27.8 5.5 %collective-permute-start.4 = (bf16[256,1920]{1,0:T(8,128)(2,1)S(1)}, bf16[256,1920]{1,0:T(8,128)(2,1)S(1)}, u32[]{:S(2)}, u32[]{:S(2)}) collective-permute-start(bf16[256,1920]{1,0:T(8,128)(2,1)S(1)} %shard_map.90.mine_ref), channel_id=1, source_target_pairs={{0,1},{1,0},{2,3},{3,2},{4,5},{5,4},{6,7},{7,6},{8,9},{9,8},{10,11... | collective-permute-start | bytes 2949128 | tf_op jit(solution)/shard_map/ppermute | solution.py:32
  34.9 18.0 %all-to-all-start = ((bf16[16,12,16,128]{3,2,1,0:T(8,128)(2,1)}), bf16[16,12,16,128]{3,2,1,0:T(8,128)(2,1)S(1)}, u32[]{:S(2)}, u32[]{:S(2)}) async-start(bf16[16,12,16,128]{3,2,1,0:T(8,128)(2,1)} %shard_map.91), calls=%async_computation | async-start | bytes 1572864 | tf_op jit(solution)/shard_map/all_to_all | solution.py:36
  39.4 35.7 %collective-permute-start.5 = (bf16[256,640]{1,0:T(8,128)(2,1)S(1)}, bf16[256,640]{1,0:T(8,128)(2,1)}, u32[]{:S(2)}, u32[]{:S(2)}) collective-permute-start(bf16[256,640]{1,0:T(8,128)(2,1)S(1)} %get-tuple-element.27.rows_ref), channel_id=1, source_target_pairs={{0,3},{1,2},{2,1},{3,0},{4,7},{5,6},{6,5},{7,4},{8,11},{9,10},{10,... | collective-permute-start | bytes 983048 | tf_op jit(solution)/shard_map/ppermute | solution.py:32
  43.5 31.6 %collective-permute-start.6 = (bf16[256,640]{1,0:T(8,128)(2,1)S(1)}, bf16[256,640]{1,0:T(8,128)(2,1)}, u32[]{:S(2)}, u32[]{:S(2)}) collective-permute-start(bf16[256,640]{1,0:T(8,128)(2,1)S(1)} %get-tuple-element.27.rows_ref), channel_id=1, source_target_pairs={{0,7},{1,6},{2,5},{3,4},{4,3},{5,2},{6,1},{7,0},{8,15},{9,14},{10,... | collective-permute-start | bytes 983048 | tf_op jit(solution)/shard_map/ppermute | solution.py:32
  46.7 30.6 %collective-permute-start.7 = (bf16[256,640]{1,0:T(8,128)(2,1)S(1)}, bf16[256,640]{1,0:T(8,128)(2,1)S(1)}, u32[]{:S(2)}, u32[]{:S(2)}) collective-permute-start(bf16[256,640]{1,0:T(8,128)(2,1)S(1)} %get-tuple-element.27.rows_ref), channel_id=1, source_target_pairs={{0,15},{1,14},{2,13},{3,12},{4,11},{5,10},{6,9},{7,8},{8,7},{9,6},... | collective-permute-start | bytes 983048 | tf_op jit(solution)/shard_map/ppermute | solution.py:32
  50.4 1.1 copy-start.3
  62.8 24.1 %all-to-all-start.2 = ((bf16[4,3,16,128]{3,2,1,0:T(8,128)(2,1)}), bf16[4,3,16,128]{3,2,1,0:T(8,128)(2,1)S(1)}, u32[]{:S(2)}, u32[]{:S(2)}) async-start(bf16[4,3,16,128]{3,2,1,0:T(8,128)(2,1)} %shard_map.94), calls=%async_computation.2 | async-start | bytes 98304 | tf_op jit(solution)/shard_map/all_to_all | solution.py:36
  77.2 40.2 %copy-start.6 = (bf16[256,640]{1,0:T(8,128)(2,1)S(1)}, bf16[256,640]{1,0:T(8,128)(2,1)}, u32[]{:S(2)}) copy-start(bf16[256,640]{1,0:T(8,128)(2,1)} %txt_ref.3) | copy-start | bytes 983044
  111.4 8.0 %collective-permute-start.8 = (bf16[16,12,16,128]{3,2,1,0:T(8,128)(2,1)S(1)}, bf16[16,12,16,128]{3,2,1,0:T(8,128)(2,1)S(1)}, u32[]{:S(2)}, u32[]{:S(2)}) collective-permute-start(bf16[16,12,16,128]{3,2,1,0:T(8,128)(2,1)S(1)} %all_to_all.27.mine_ref), channel_id=1, source_target_pairs={{0,1},{1,0},{2,3},{3,2},{4,5},{5,4},{6,7},{7,6},{8,9},{9,8},{10,11... | collective-permute-start | bytes 2359304 | tf_op jit(solution)/shard_map/ppermute | solution.py:32

commit v8 on v7

--- a/solution.py
+++ b/solution.py
@@ -24,7 +24,7 @@
 
 
 PLANE = group((1, 2, 7, 8))
-NEAR, FAR = group((3, 4)), group((5, 6))
+LINE = group((3, 4, 5, 6))
 
 
 def swap(value, mask):
@@ -107,23 +107,20 @@
 
 
 def image_end_kernel(
-    scale_ref, bias_ref, total_ref, rows_ref, other_ref, unit_ref, inverse_ref, feat_ref, packed_ref
+    scale_ref, bias_ref, total_ref, rows_ref, a_ref, b_ref, unit_ref, inverse_ref, feat_ref, packed_ref
 ):
     rows = rows_ref[...]
-    total = total_ref[...] + pair_term(scale_ref, bias_ref, rows, other_ref[...])
+    total = total_ref[...] + pair_term(scale_ref, bias_ref, rows, a_ref[...])
+    total = total + pair_term(scale_ref, bias_ref, rows, b_ref[...])
     packed_ref[:, :E] = tangent(scale_ref[0] * total, unit_ref[...], inverse_ref[...])
     packed_ref[:, E : 2 * E] = rows
     packed_ref[:, 2 * E :] = feat_ref[...]
 
 
-def text_first_kernel(scale_ref, bias_ref, total_ref, rows_ref, packed_ref, out_ref):
-    term = pair_term(scale_ref, bias_ref, rows_ref[...], packed_ref[:, E : 2 * E])
-    out_ref[...] = total_ref[...] + term
-
-
-def text_pairs_kernel(scale_ref, bias_ref, total_ref, rows_ref, a_ref, b_ref, out_ref):
+def text_pairs_kernel(scale_ref, bias_ref, total_ref, rows_ref, packed_ref, a_ref, b_ref, out_ref):
     rows = rows_ref[...]
-    total = total_ref[...] + pair_term(scale_ref, bias_ref, rows, a_ref[...])
+    total = total_ref[...] + pair_term(scale_ref, bias_ref, rows, packed_ref[:, E : 2 * E])
+    total = total + pair_term(scale_ref, bias_ref, rows, a_ref[...])
     out_ref[...] = total + pair_term(scale_ref, bias_ref, rows, b_ref[...])
 
 
@@ -134,11 +131,12 @@
     out_ref[...] = tangent(scale_ref[0] * total, value * inverse, inverse)
 
 
-def sum_kernel(parts_ref, out_ref):
+def plane_sum_kernel(parts_ref, out_ref):
     total = parts_ref[0].astype(F32)
     for k in range(1, parts_ref.shape[0]):
         total = total + parts_ref[k].astype(F32)
-    out_ref[...] = total.astype(BF16)
+    out_ref[:SLABS] = total.astype(BF16)
+    out_ref[SLABS:] = jnp.zeros((OWNERS - SLABS, 16, 128), BF16)
 
 
 def spread_sum_kernel(parts_ref, out_ref):
@@ -202,8 +200,8 @@
     block16 = shape(ROWS, E, dtype=BF16)
 
     packed = shape(ROWS, 3 * E, dtype=BF16)
-    txt_rows = call(text_kernel, block16, [VMEM], 40 * pair, txt_emb)
-    txt_15 = swap(txt_rows, 15)
+    txt_rows = call(text_kernel, block16, [VMEM], little, txt_emb)
+    txt_15, txt_3, txt_7, txt_1 = [swap(txt_rows, c) for c in (15, 3, 7, 1)]
     unit, inverse, img_rows, d_img, d_txt, other_feat = call(
         image_kernel,
         (block, shape(ROWS, 1), block16, block, block, block16),
@@ -212,13 +210,11 @@
         core, scale, bias, labels[None, :], img_feat, head_weight, txt_rows,
     )
     pair_specs = [SMEM, SMEM, VMEM, VMEM, VMEM]
-    late = after(txt_rows, img_rows)
-    txt_3, txt_7, txt_1 = swap(late, 3), swap(late, 7), swap(late, 1)
-    for other in (txt_15, txt_3, txt_7):
+    for other in (txt_15, txt_3):
         d_img = call(pair_kernel, block, pair_specs, little, scale, bias, d_img, img_rows, other)
     packed_img = call(
-        image_end_kernel, packed, pair_specs + [VMEM] * 3, little,
-        scale, bias, d_img, img_rows, txt_1, unit, inverse, other_feat,
+        image_end_kernel, packed, pair_specs + [VMEM] * 4, little,
+        scale, bias, d_img, img_rows, txt_7, txt_1, unit, inverse, other_feat,
     )
     other_img = swap(packed_img, 1)
     d_img_feat = dot(packed_img[:, :E], head_weight, 1, 1).astype(BF16)
@@ -230,24 +226,17 @@
     parts = after(parts, d_img_feat)
     late = after(img_rows, parts)
     img_7, img_15, img_3 = swap(late, 7), swap(late, 15), swap(late, 3)
-    d_txt = call(
-        text_first_kernel, block, pair_specs, pair,
-        scale, bias, after(d_txt, parts), txt_rows, other_img,
-    )
     parts = exchange(parts, PLANE)
     slab = (16, 128)
-    part = call(sum_kernel, shape(SLABS, *slab, dtype=BF16), [VMEM], little, parts)
-    part = after(part, d_txt)
-    quarters = shape(4, SLABS // 4, *slab, dtype=BF16)
-    parts = exchange(part.reshape(quarters.shape), NEAR)
-    parts = call(spread_sum_kernel, quarters, [VMEM], little, parts)
+    line = shape(OWNERS, *slab, dtype=BF16)
+    parts = call(plane_sum_kernel, line, [VMEM], little, parts)
     d_txt = call(
-        text_pairs_kernel, block, pair_specs + [VMEM], 2 * pair,
-        scale, bias, after(d_txt, parts), txt_rows, img_3, img_7,
-    )
-    parts = after(exchange(parts, FAR), d_txt, img_15)
-    parts = call(spread_sum_kernel, quarters, [VMEM], little, parts)
-    parts = exchange(parts, NEAR)
+        text_pairs_kernel, block, pair_specs + [VMEM] * 2, 3 * pair,
+        scale, bias, after(d_txt, parts), txt_rows, other_img, img_3, img_7,
+    )
+    parts = after(exchange(parts, LINE), d_txt, img_15)
+    parts = call(spread_sum_kernel, line, [VMEM], little, parts)
+    parts = exchange(parts, LINE)[:SLABS]
     d_txt_emb = call(
         text_end_kernel, block16, pair_specs + [VMEM], pair,
         scale, bias, d_txt, txt_rows, img_15, txt_emb,

time: 121 us -> 119 us (0.983)
  waiting for transfers between devices: 17.1 us -> 13.5 us
  starting transfers between devices: 51.8 us -> 55 us
  blocking collectives: 33.4 us -> 30.2 us
  local copies, waits for them, and re-layouts: 2.33 us -> 4.24 us
    ppermute x9, waiting for transfers between devices: 6.67 us -> 3.16 us  [swap(): return lax.ppermute(value, 'dp', pairs)]
    all_to_all x3 -> x2, blocking collectives: 33.4 us -> 30.2 us  [exchange(): lax.all_to_all(value, 'dp', 0, 0, axis_index_groups=members, tiled=True)]
    all_to_all x2, starting transfers between devices: 16.8 us -> 19.5 us  [exchange(): lax.all_to_all(value, 'dp', 0, 0, axis_index_groups=members, tiled=True)]
    unnamed x16 -> x14, local copies, waits for them, and re-layouts: 2.19 us -> 4.09 us
    pallas_call x14 -> x11, Pallas kernels: 12.2 us -> 11.6 us  [call(): pl.pallas_call(kernel, out_shape=out_shape, in_specs=specs, out_specs=out...]
  transfers between devices with their start and end apart: 11 -> 11, of which waited for: 6 -> 5; matrix products, arithmetic and copies ran while one was open for 1% -> 1% of each run, Pallas kernels for 7% -> 6%
where the time goes in v8:
time: 119 us; the launch traced here: 118 us
  starting transfers between devices  55 us (46%)
  blocking collectives  30.2 us (25%)
  waiting for transfers between devices  13.5 us (11%)
  Pallas kernels  11.6 us (10%)
  local copies, waits for them, and re-layouts  4.24 us (4%)
  between operations  2.19 us (2%)
  matrix products  1.48 us (1%)
    ppermute x9, starting transfers between devices, swap(): return lax.ppermute(value, 'dp', pairs)  35.4 us
    all_to_all x2, blocking collectives, exchange(): lax.all_to_all(value, 'dp', 0, 0, axis_index_groups=members, tiled=True)  30.2 us
    all_to_all x2, starting transfers between devices, exchange(): lax.all_to_all(value, 'dp', 0, 0, axis_index_groups=members, tiled=True)  19.5 us
    pallas_call x11, Pallas kernels, call(): pl.pallas_call(kernel, out_shape=out_shape, in_specs=specs, out_specs=out...  11.6 us
    all_to_all x2, waiting for transfers between devices, exchange(): lax.all_to_all(value, 'dp', 0, 0, axis_index_groups=members, tiled=True)  10.4 us
    unnamed x14, local copies, waits for them, and re-layouts  4.09 us
    ppermute x9, waiting for transfers between devices, swap(): return lax.ppermute(value, 'dp', pairs)  3.16 us
  transfers between devices with their start and end apart: 11, of which 5 were waited for; matrix products, arithmetic and copies ran while one was open for 1% of the time, Pallas kernels for 6%

profile of v8, /device:TPU:1, one launch (start us, length us, event | category | flops | bytes accessed | tf_op | source)
XLA Modules:
  0.0 118.2 jit_solution(5576544078132167883)
XLA Ops:
  1.8 7.1 %collective-permute-start = (bf16[256,640]{1,0:T(8,128)(2,1)S(1)}, bf16[256,640]{1,0:T(8,128)(2,1)S(1)}, u32[]{:S(2)}, u32[]{:S(2)}) collective-permute-start(bf16[256,640]{1,0:T(8,128)(2,1)S(1)} %shard_map.85.txt_ref.rows_ref), channel_id=1, source_target_pairs={{0,15},{1,14},{2,13},{3,12},{4,11},{5,10},{6,9},{7,8},{8,7},{9,6},... | collective-permute-start | bytes 983048 | tf_op jit(solution)/shard_map/ppermute | solution.py:32
  8.9 1.9 %collective-permute-start.1 = (bf16[256,640]{1,0:T(8,128)(2,1)S(1)}, bf16[256,640]{1,0:T(8,128)(2,1)S(1)}, u32[]{:S(2)}, u32[]{:S(2)}) collective-permute-start(bf16[256,640]{1,0:T(8,128)(2,1)S(1)} %shard_map.85.txt_ref.rows_ref), channel_id=1, source_target_pairs={{0,3},{1,2},{2,1},{3,0},{4,7},{5,6},{6,5},{7,4},{8,11},{9,10},{10,... | collective-permute-start | bytes 983048 | tf_op jit(solution)/shard_map/ppermute | solution.py:32
  10.8 3.0 %collective-permute-start.2 = (bf16[256,640]{1,0:T(8,128)(2,1)S(1)}, bf16[256,640]{1,0:T(8,128)(2,1)S(1)}, u32[]{:S(2)}, u32[]{:S(2)}) collective-permute-start(bf16[256,640]{1,0:T(8,128)(2,1)S(1)} %shard_map.85.txt_ref.rows_ref), channel_id=1, source_target_pairs={{0,7},{1,6},{2,5},{3,4},{4,3},{5,2},{6,1},{7,0},{8,15},{9,14},{10,... | collective-permute-start | bytes 983048 | tf_op jit(solution)/shard_map/ppermute | solution.py:32
  13.8 2.5 %collective-permute-start.3 = (bf16[256,640]{1,0:T(8,128)(2,1)S(1)}, bf16[256,640]{1,0:T(8,128)(2,1)S(1)}, u32[]{:S(2)}, u32[]{:S(2)}) collective-permute-start(bf16[256,640]{1,0:T(8,128)(2,1)S(1)} %shard_map.85.txt_ref.rows_ref), channel_id=1, source_target_pairs={{0,1},{1,0},{2,3},{3,2},{4,5},{5,4},{6,7},{7,6},{8,9},{9,8},{10,11... | collective-permute-start | bytes 983048 | tf_op jit(solution)/shard_map/ppermute | solution.py:32
  17.7 1.4 %copy-done = bf16[1152,640]{1,0:T(8,128)(2,1)S(1)} copy-done((bf16[1152,640]{1,0:T(8,128)(2,1)S(1)}, bf16[1152,640]{1,0:T(8,128)(2,1)}, u32[]{:S(2)}) %copy-start) | copy-done | bytes 1474584
  20.8 1.5 %shard_map.86 = (f32[256,640]{1,0:T(8,128)S(1)}, f32[256,1]{1,0:T(8,128)S(1)}, bf16[256,640]{1,0:T(8,128)(2,1)S(1)}, f32[256,640]{1,0:T(8,128)S(1)}, f32[256,640...) custom-call(s32[1]{0:T(128)} %bitcast.core_ref, f32[1]{0:T(128)S(6)} %exp.3.scale_ref, f32[1]{0:T(128)S(6)} %copy.10.bias_ref, ...), custom_call_target="tpu_custom_call" | custom-call | flops 2013265920 | bytes 5015564 | tf_op jit(solution)/shard_map/pallas_call | solution.py:55
  23.6 2.1 %collective-permute-done.2.a_ref = bf16[256,640]{1,0:T(8,128)(2,1)S(1)} collective-permute-done((bf16[256,640]{1,0:T(8,128)(2,1)S(1)}, bf16[256,640]{1,0:T(8,128)(2,1)S(1)}, u32[]{:S(2)}, u32[]{:S(2)}) %collective-permute-start.2) | collective-permute-done | bytes 327712 | tf_op jit(solution)/shard_map/ppermute | solution.py:32
  25.7 1.2 shard_map.89.mine_ref
  26.9 2.5 %collective-permute-start.4 = (bf16[256,1920]{1,0:T(8,128)(2,1)S(1)}, bf16[256,1920]{1,0:T(8,128)(2,1)S(1)}, u32[]{:S(2)}, u32[]{:S(2)}) collective-permute-start(bf16[256,1920]{1,0:T(8,128)(2,1)S(1)} %shard_map.89.mine_ref), channel_id=1, source_target_pairs={{0,1},{1,0},{2,3},{3,2},{4,5},{5,4},{6,7},{7,6},{8,9},{9,8},{10,11... | collective-permute-start | bytes 2949128 | tf_op jit(solution)/shard_map/ppermute | solution.py:32
  29.4 1.5 %convolution_convert_fusion = bf16[256,1152]{1,0:T(8,128)(2,1)} fusion(bf16[1152,640]{1,0:T(8,128)(2,1)S(1)} %copy-done.1, bf16[256,1920]{1,0:T(8,128)(2,1)S(1)} %shard_map.89.mine_ref), kind=kOutput, calls=%fused_computation | convolution fusion | flops 377782272 | bytes 2392064 | tf_op jit(solution)/shard_map/dot_general | solution.py:48
  31.6 1.6 %shard_map.90 = bf16[16,12,16,128]{3,2,1,0:T(8,128)(2,1)} custom-call(s32[1]{0:T(128)} %bitcast.core_ref, bf16[256,1152]{1,0:T(8,128)(2,1)S(1)} %copy-done.5, bf16[256,1920]{1,0:T(8,128)(2,1)S(1)} %shard_map.89.mine_ref, bf16[256,1920]{1,0:T(8,128)(2,1)S(1)} %collective-permute-done.4.theirs_ref.packed_ref), custom_call_target="tpu_custom_call" | custom-call | flops 377487360 | bytes 3342340 | tf_op jit(solution)/shard_map/pallas_call | solution.py:55
  33.2 4.6 %all-to-all-start = ((bf16[16,12,16,128]{3,2,1,0:T(8,128)(2,1)}), bf16[16,12,16,128]{3,2,1,0:T(8,128)(2,1)S(1)}, u32[]{:S(2)}, u32[]{:S(2)}) async-start(bf16[16,12,16,128]{3,2,1,0:T(8,128)(2,1)} %shard_map.90), calls=%async_computation | async-start | bytes 1572864 | tf_op jit(solution)/shard_map/all_to_all | solution.py:36
  37.8 4.1 %collective-permute-start.5 = (bf16[256,640]{1,0:T(8,128)(2,1)S(1)}, bf16[256,640]{1,0:T(8,128)(2,1)}, u32[]{:S(2)}, u32[]{:S(2)}) collective-permute-start(bf16[256,640]{1,0:T(8,128)(2,1)S(1)} %get-tuple-element.21.rows_ref), channel_id=1, source_target_pairs={{0,3},{1,2},{2,1},{3,0},{4,7},{5,6},{6,5},{7,4},{8,11},{9,10},{10,... | collective-permute-start | bytes 983048 | tf_op jit(solution)/shard_map/ppermute | solution.py:32
  41.9 3.2 %collective-permute-start.6 = (bf16[256,640]{1,0:T(8,128)(2,1)S(1)}, bf16[256,640]{1,0:T(8,128)(2,1)}, u32[]{:S(2)}, u32[]{:S(2)}) collective-permute-start(bf16[256,640]{1,0:T(8,128)(2,1)S(1)} %get-tuple-element.21.rows_ref), channel_id=1, source_target_pairs={{0,7},{1,6},{2,5},{3,4},{4,3},{5,2},{6,1},{7,0},{8,15},{9,14},{10,... | collective-permute-start | bytes 983048 | tf_op jit(solution)/shard_map/ppermute | solution.py:32
  45.1 4.9 %collective-permute-start.7 = (bf16[256,640]{1,0:T(8,128)(2,1)S(1)}, bf16[256,640]{1,0:T(8,128)(2,1)S(1)}, u32[]{:S(2)}, u32[]{:S(2)}) collective-permute-start(bf16[256,640]{1,0:T(8,128)(2,1)S(1)} %get-tuple-element.21.rows_ref), channel_id=1, source_target_pairs={{0,15},{1,14},{2,13},{3,12},{4,11},{5,10},{6,9},{7,8},{8,7},{9,6},... | collective-permute-start | bytes 983048 | tf_op jit(solution)/shard_map/ppermute | solution.py:32
  50.0 1.3 %all-to-all-done.parts_ref = bf16[16,12,16,128]{3,2,1,0:T(8,128)(2,1)S(1)} async-done(((bf16[16,12,16,128]{3,2,1,0:T(8,128)(2,1)}), bf16[16,12,16,128]{3,2,1,0:T(8,128)(2,1)S(1)}, u32[]{:S(2)}, u32[]{:S(2)}) %all-to-all-start) | async-done | bytes 786464 | tf_op jit(solution)/shard_map/all_to_all | solution.py:36
  52.1 14.9 %all-to-all-start.1 = ((bf16[16,16,128]{2,1,0:T(8,128)(2,1)}), bf16[16,16,128]{2,1,0:T(8,128)(2,1)S(1)}, u32[]{:S(2)}, u32[]{:S(2)}) async-start(bf16[16,16,128]{2,1,0:T(8,128)(2,1)} %shard_map.91), calls=%async_computation.1 | async-start | bytes 131072 | tf_op jit(solution)/shard_map/all_to_all | solution.py:36
  67.0 2.5 %shard_map.92.total_ref = f32[256,640]{1,0:T(8,128)S(1)} custom-call(f32[1]{0:T(128)S(6)} %exp.3.scale_ref, f32[1]{0:T(128)S(6)} %copy.10.bias_ref, f32[256,640]{1,0:T(8,128)S(1)} %get-tuple-element.20.total_ref, bf16[256,640]{1,0:T(8,128)(2,1)S(1)} %shard_map.85.txt_ref.rows_ref, bf16[256,1920]{1,0:T(8,128)(2,1)S(1)} %collective-permute-done.4.theirs_ref.packed_ref, ...), custom_call_target="tpu_custom_call" | custom-call | flops 503316480 | bytes 3276808 | tf_op jit(solution)/shard_map/pallas_call | solution.py:55
  69.5 9.0 %all-to-all-done.1.parts_ref = bf16[16,16,128]{2,1,0:T(8,128)(2,1)S(1)} async-done(((bf16[16,16,128]{2,1,0:T(8,128)(2,1)}), bf16[16,16,128]{2,1,0:T(8,128)(2,1)S(1)}, u32[]{:S(2)}, u32[]{:S(2)}) %all-to-all-start.1) | async-done | bytes 65568 | tf_op jit(solution)/shard_map/all_to_all | solution.py:36
  78.6 14.4 %all_to_all.20 = bf16[16,16,128]{2,1,0:T(8,128)(2,1)S(1)} all-to-all(bf16[16,16,128]{2,1,0:T(8,128)(2,1)S(1)} %shard_map.94), channel_id=1, replica_groups={{0,8,16,24,32,40,48,56,64,72,80,88,96,104,112,120},{1,9,17,25,33,41,49,..., dimensions={0} | all-to-all | bytes 131072 | tf_op jit(solution)/shard_map/all_to_all | solution.py:36
  93.2 15.8 %all_to_all.21.mine_ref = bf16[16,12,16,128]{3,2,1,0:T(8,128)(2,1)S(1)} all-to-all(bf16[16,12,16,128]{3,2,1,0:T(8,128)(2,1)S(1)} %broadcast_in_dim.14), channel_id=1, replica_groups={{0,2,4,6,128,130,132,134,256,258,260,262,384,386,388,390},{1,3,5,7,129,..., dimensions={0} | all-to-all | bytes 1572864 | tf_op jit(solution)/shard_map/all_to_all | solution.py:36
  108.9 6.2 %collective-permute-start.8 = (bf16[16,12,16,128]{3,2,1,0:T(8,128)(2,1)S(1)}, bf16[16,12,16,128]{3,2,1,0:T(8,128)(2,1)S(1)}, u32[]{:S(2)}, u32[]{:S(2)}) collective-permute-start(bf16[16,12,16,128]{3,2,1,0:T(8,128)(2,1)S(1)} %all_to_all.21.mine_ref), channel_id=1, source_target_pairs={{0,1},{1,0},{2,3},{3,2},{4,5},{5,4},{6,7},{7,6},{8,9},{9,8},{10,11... | collective-permute-start | bytes 2359304 | tf_op jit(solution)/shard_map/ppermute | solution.py:32
  115.1 1.5 %shard_map.93 = bf16[256,640]{1,0:T(8,128)(2,1)} custom-call(f32[1]{0:T(128)S(6)} %exp.3.scale_ref, f32[1]{0:T(128)S(6)} %copy.10.bias_ref, f32[256,640]{1,0:T(8,128)S(1)} %shard_map.92.total_ref, bf16[256,640]{1,0:T(8,128)(2,1)S(1)} %shard_map.85.txt_ref.rows_ref, bf16[256,640]{1,0:T(8,128)(2,1)S(1)} %collective-permute-done.7.other_ref, ...), custom_call_target="tpu_custom_call" | custom-call | flops 167772160 | bytes 1966088 | tf_op jit(solution)/shard_map/pallas_call | solution.py:55
  117.0 1.2 %shard_map.95 = bf16[1152,640]{1,0:T(8,128)(2,1)} custom-call(s32[1]{0:T(128)} %bitcast.core_ref, bf16[16,12,16,128]{3,2,1,0:T(8,128)(2,1)S(1)} %all_to_all.21.mine_ref, bf16[16,12,16,128]{3,2,1,0:T(8,128)(2,1)S(1)} %collective-permute-done.8.theirs_ref), custom_call_target="tpu_custom_call" | custom-call | bytes 3047428 | tf_op jit(solution)/shard_map/pallas_call | solution.py:55
  (28 shorter events, 6.2 us)
Async XLA Ops:
  0.6 1.0 copy-start.2
  1.8 20.5 %collective-permute-start = (bf16[256,640]{1,0:T(8,128)(2,1)S(1)}, bf16[256,640]{1,0:T(8,128)(2,1)S(1)}, u32[]{:S(2)}, u32[]{:S(2)}) collective-permute-start(bf16[256,640]{1,0:T(8,128)(2,1)S(1)} %shard_map.85.txt_ref.rows_ref), channel_id=1, source_target_pairs={{0,15},{1,14},{2,13},{3,12},{4,11},{5,10},{6,9},{7,8},{8,7},{9,6},... | collective-permute-start | bytes 983048 | tf_op jit(solution)/shard_map/ppermute | solution.py:32
  8.9 14.0 %collective-permute-start.1 = (bf16[256,640]{1,0:T(8,128)(2,1)S(1)}, bf16[256,640]{1,0:T(8,128)(2,1)S(1)}, u32[]{:S(2)}, u32[]{:S(2)}) collective-permute-start(bf16[256,640]{1,0:T(8,128)(2,1)S(1)} %shard_map.85.txt_ref.rows_ref), channel_id=1, source_target_pairs={{0,3},{1,2},{2,1},{3,0},{4,7},{5,6},{6,5},{7,4},{8,11},{9,10},{10,... | collective-permute-start | bytes 983048 | tf_op jit(solution)/shard_map/ppermute | solution.py:32
  10.8 14.8 %collective-permute-start.2 = (bf16[256,640]{1,0:T(8,128)(2,1)S(1)}, bf16[256,640]{1,0:T(8,128)(2,1)S(1)}, u32[]{:S(2)}, u32[]{:S(2)}) collective-permute-start(bf16[256,640]{1,0:T(8,128)(2,1)S(1)} %shard_map.85.txt_ref.rows_ref), channel_id=1, source_target_pairs={{0,7},{1,6},{2,5},{3,4},{4,3},{5,2},{6,1},{7,0},{8,15},{9,14},{10,... | collective-permute-start | bytes 983048 | tf_op jit(solution)/shard_map/ppermute | solution.py:32
  13.8 11.9 %collective-permute-start.3 = (bf16[256,640]{1,0:T(8,128)(2,1)S(1)}, bf16[256,640]{1,0:T(8,128)(2,1)S(1)}, u32[]{:S(2)}, u32[]{:S(2)}) collective-permute-start(bf16[256,640]{1,0:T(8,128)(2,1)S(1)} %shard_map.85.txt_ref.rows_ref), channel_id=1, source_target_pairs={{0,1},{1,0},{2,3},{3,2},{4,5},{5,4},{6,7},{7,6},{8,9},{9,8},{10,11... | collective-permute-start | bytes 983048 | tf_op jit(solution)/shard_map/ppermute | solution.py:32
  17.7 1.4 %copy-start = (bf16[1152,640]{1,0:T(8,128)(2,1)S(1)}, bf16[1152,640]{1,0:T(8,128)(2,1)}, u32[]{:S(2)}) copy-start(bf16[1152,640]{1,0:T(8,128)(2,1)} %head_ref.1) | copy-start | bytes 4423684
  19.1 1.1 copy-start.4
  20.1 0.7 copy-start.6
  25.7 3.7 %copy-start.1 = (bf16[1152,640]{1,0:T(8,128)(2,1)S(1)}, bf16[1152,640]{1,0:T(8,128)(2,1)}, u32[]{:S(2)}) copy-start(bf16[1152,640]{1,0:T(8,128)(2,1)} %head_ref.1) | copy-start | bytes 4423684
  26.9 4.7 %copy-start.5 = (bf16[256,1152]{1,0:T(8,128)(2,1)S(1)}, bf16[256,1152]{1,0:T(8,128)(2,1)}, u32[]{:S(2)}) copy-start(bf16[256,1152]{1,0:T(8,128)(2,1)} %feat_ref.3) | copy-start | bytes 1769476
  26.9 4.7 %collective-permute-start.4 = (bf16[256,1920]{1,0:T(8,128)(2,1)S(1)}, bf16[256,1920]{1,0:T(8,128)(2,1)S(1)}, u32[]{:S(2)}, u32[]{:S(2)}) collective-permute-start(bf16[256,1920]{1,0:T(8,128)(2,1)S(1)} %shard_map.89.mine_ref), channel_id=1, source_target_pairs={{0,1},{1,0},{2,3},{3,2},{4,5},{5,4},{6,7},{7,6},{8,9},{9,8},{10,11... | collective-permute-start | bytes 2949128 | tf_op jit(solution)/shard_map/ppermute | solution.py:32
  33.2 18.2 %all-to-all-start = ((bf16[16,12,16,128]{3,2,1,0:T(8,128)(2,1)}), bf16[16,12,16,128]{3,2,1,0:T(8,128)(2,1)S(1)}, u32[]{:S(2)}, u32[]{:S(2)}) async-start(bf16[16,12,16,128]{3,2,1,0:T(8,128)(2,1)} %shard_map.90), calls=%async_computation | async-start | bytes 1572864 | tf_op jit(solution)/shard_map/all_to_all | solution.py:36
  37.8 29.2 %collective-permute-start.5 = (bf16[256,640]{1,0:T(8,128)(2,1)S(1)}, bf16[256,640]{1,0:T(8,128)(2,1)}, u32[]{:S(2)}, u32[]{:S(2)}) collective-permute-start(bf16[256,640]{1,0:T(8,128)(2,1)S(1)} %get-tuple-element.21.rows_ref), channel_id=1, source_target_pairs={{0,3},{1,2},{2,1},{3,0},{4,7},{5,6},{6,5},{7,4},{8,11},{9,10},{10,... | collective-permute-start | bytes 983048 | tf_op jit(solution)/shard_map/ppermute | solution.py:32
  41.9 25.1 %collective-permute-start.6 = (bf16[256,640]{1,0:T(8,128)(2,1)S(1)}, bf16[256,640]{1,0:T(8,128)(2,1)}, u32[]{:S(2)}, u32[]{:S(2)}) collective-permute-start(bf16[256,640]{1,0:T(8,128)(2,1)S(1)} %get-tuple-element.21.rows_ref), channel_id=1, source_target_pairs={{0,7},{1,6},{2,5},{3,4},{4,3},{5,2},{6,1},{7,0},{8,15},{9,14},{10,... | collective-permute-start | bytes 983048 | tf_op jit(solution)/shard_map/ppermute | solution.py:32
  45.1 24.4 %collective-permute-start.7 = (bf16[256,640]{1,0:T(8,128)(2,1)S(1)}, bf16[256,640]{1,0:T(8,128)(2,1)S(1)}, u32[]{:S(2)}, u32[]{:S(2)}) collective-permute-start(bf16[256,640]{1,0:T(8,128)(2,1)S(1)} %get-tuple-element.21.rows_ref), channel_id=1, source_target_pairs={{0,15},{1,14},{2,13},{3,12},{4,11},{5,10},{6,9},{7,8},{8,7},{9,6},... | collective-permute-start | bytes 983048 | tf_op jit(solution)/shard_map/ppermute | solution.py:32
  52.1 26.5 %all-to-all-start.1 = ((bf16[16,16,128]{2,1,0:T(8,128)(2,1)}), bf16[16,16,128]{2,1,0:T(8,128)(2,1)S(1)}, u32[]{:S(2)}, u32[]{:S(2)}) async-start(bf16[16,16,128]{2,1,0:T(8,128)(2,1)} %shard_map.91), calls=%async_computation.1 | async-start | bytes 131072 | tf_op jit(solution)/shard_map/all_to_all | solution.py:36
  69.5 45.6 %copy-start.3 = (bf16[256,640]{1,0:T(8,128)(2,1)S(1)}, bf16[256,640]{1,0:T(8,128)(2,1)}, u32[]{:S(2)}) copy-start(bf16[256,640]{1,0:T(8,128)(2,1)} %txt_ref.3) | copy-start | bytes 983044
  108.9 8.1 %collective-permute-start.8 = (bf16[16,12,16,128]{3,2,1,0:T(8,128)(2,1)S(1)}, bf16[16,12,16,128]{3,2,1,0:T(8,128)(2,1)S(1)}, u32[]{:S(2)}, u32[]{:S(2)}) collective-permute-start(bf16[16,12,16,128]{3,2,1,0:T(8,128)(2,1)S(1)} %all_to_all.21.mine_ref), channel_id=1, source_target_pairs={{0,1},{1,0},{2,3},{3,2},{4,5},{5,4},{6,7},{7,6},{8,9},{9,8},{10,11... | collective-permute-start | bytes 2359304 | tf_op jit(solution)/shard_map/ppermute | solution.py:32

commit v9 on v8

--- a/solution.py
+++ b/solution.py
@@ -71,9 +71,13 @@
     return ((d_unit - unit * jnp.sum(unit * d_unit, axis=-1, keepdims=True)) * inverse).astype(BF16)
 
 
+def unit_rows(ref):
+    value = ref[...].astype(F32)
+    return (value * inverse_norm(value)).astype(BF16)
+
+
 def text_kernel(txt_ref, rows_ref):
-    value = txt_ref[...].astype(F32)
-    rows_ref[...] = (value * inverse_norm(value)).astype(BF16)
+    rows_ref[...] = unit_rows(txt_ref)
 
 
 def image_kernel(
@@ -102,30 +106,44 @@
     return dot(jax.nn.sigmoid(logits).astype(BF16), others)
 
 
-def pair_kernel(scale_ref, bias_ref, total_ref, rows_ref, other_ref, out_ref):
-    out_ref[...] = total_ref[...] + pair_term(scale_ref, bias_ref, rows_ref[...], other_ref[...])
+def three_pairs_kernel(
+    scale_ref, bias_ref, total_ref, rows_ref, a_ref, b_ref, c_ref, out_ref, held, sems
+):
+    copies = [
+        pltpu.make_async_copy(ref, held.at[k], sems.at[k])
+        for k, ref in enumerate((a_ref, b_ref, c_ref))
+    ]
+    for copy in copies:
+        copy.start()
+    rows, total = rows_ref[...], total_ref[...]
+    for k, copy in enumerate(copies):
+        copy.wait()
+        total = total + pair_term(scale_ref, bias_ref, rows, unit_rows(held.at[k]))
+    out_ref[...] = total
 
 
 def image_end_kernel(
-    scale_ref, bias_ref, total_ref, rows_ref, a_ref, b_ref, unit_ref, inverse_ref, feat_ref, packed_ref
+    scale_ref, bias_ref, total_ref, rows_ref, other_ref, unit_ref, inverse_ref, feat_ref, packed_ref
 ):
     rows = rows_ref[...]
-    total = total_ref[...] + pair_term(scale_ref, bias_ref, rows, a_ref[...])
-    total = total + pair_term(scale_ref, bias_ref, rows, b_ref[...])
+    total = total_ref[...] + pair_term(scale_ref, bias_ref, rows, unit_rows(other_ref))
     packed_ref[:, :E] = tangent(scale_ref[0] * total, unit_ref[...], inverse_ref[...])
     packed_ref[:, E : 2 * E] = rows
     packed_ref[:, 2 * E :] = feat_ref[...]
 
 
-def text_pairs_kernel(scale_ref, bias_ref, total_ref, rows_ref, packed_ref, a_ref, b_ref, out_ref):
+def text_pairs_kernel(scale_ref, bias_ref, total_ref, rows_ref, a_ref, b_ref, out_ref):
+    rows = rows_ref[...]
+    total = total_ref[...] + pair_term(scale_ref, bias_ref, rows, a_ref[...])
+    out_ref[...] = total + pair_term(scale_ref, bias_ref, rows, b_ref[...])
+
+
+def text_end_kernel(
+    scale_ref, bias_ref, total_ref, rows_ref, packed_ref, other_ref, txt_ref, out_ref
+):
     rows = rows_ref[...]
     total = total_ref[...] + pair_term(scale_ref, bias_ref, rows, packed_ref[:, E : 2 * E])
-    total = total + pair_term(scale_ref, bias_ref, rows, a_ref[...])
-    out_ref[...] = total + pair_term(scale_ref, bias_ref, rows, b_ref[...])
-
-
-def text_end_kernel(scale_ref, bias_ref, total_ref, rows_ref, other_ref, txt_ref, out_ref):
-    total = total_ref[...] + pair_term(scale_ref, bias_ref, rows_ref[...], other_ref[...])
+    total = total + pair_term(scale_ref, bias_ref, rows, other_ref[...])
     value = txt_ref[...].astype(F32)
     inverse = inverse_norm(value)
     out_ref[...] = tangent(scale_ref[0] * total, value * inverse, inverse)
@@ -200,8 +218,8 @@
     block16 = shape(ROWS, E, dtype=BF16)
 
     packed = shape(ROWS, 3 * E, dtype=BF16)
-    txt_rows = call(text_kernel, block16, [VMEM], little, txt_emb)
-    txt_15, txt_3, txt_7, txt_1 = [swap(txt_rows, c) for c in (15, 3, 7, 1)]
+    txt_15, txt_3, txt_1, txt_7 = [swap(txt_emb, c) for c in (15, 3, 1, 7)]
+    txt_rows = call(text_kernel, block16, [VMEM], 12 * pair, txt_emb)
     unit, inverse, img_rows, d_img, d_txt, other_feat = call(
         image_kernel,
         (block, shape(ROWS, 1), block16, block, block, block16),
@@ -210,11 +228,14 @@
         core, scale, bias, labels[None, :], img_feat, head_weight, txt_rows,
     )
     pair_specs = [SMEM, SMEM, VMEM, VMEM, VMEM]
-    for other in (txt_15, txt_3):
-        d_img = call(pair_kernel, block, pair_specs, little, scale, bias, d_img, img_rows, other)
+    d_img = call(
+        three_pairs_kernel, block, pair_specs[:4] + [pl.BlockSpec(memory_space=pl.ANY)] * 3, little,
+        scale, bias, d_img, img_rows, txt_15, txt_3, txt_1,
+        scratch=[pltpu.VMEM((3, ROWS, E), BF16), pltpu.SemaphoreType.DMA((3,))],
+    )
     packed_img = call(
-        image_end_kernel, packed, pair_specs + [VMEM] * 4, little,
-        scale, bias, d_img, img_rows, txt_7, txt_1, unit, inverse, other_feat,
+        image_end_kernel, packed, pair_specs + [VMEM] * 3, little,
+        scale, bias, d_img, img_rows, txt_7, unit, inverse, other_feat,
     )
     other_img = swap(packed_img, 1)
     d_img_feat = dot(packed_img[:, :E], head_weight, 1, 1).astype(BF16)
@@ -231,15 +252,15 @@
     line = shape(OWNERS, *slab, dtype=BF16)
     parts = call(plane_sum_kernel, line, [VMEM], little, parts)
     d_txt = call(
-        text_pairs_kernel, block, pair_specs + [VMEM] * 2, 3 * pair,
-        scale, bias, after(d_txt, parts), txt_rows, other_img, img_3, img_7,
+        text_pairs_kernel, block, pair_specs + [VMEM], 2 * pair,
+        scale, bias, after(d_txt, parts), txt_rows, img_3, img_7,
     )
     parts = after(exchange(parts, LINE), d_txt, img_15)
     parts = call(spread_sum_kernel, line, [VMEM], little, parts)
     parts = exchange(parts, LINE)[:SLABS]
     d_txt_emb = call(
-        text_end_kernel, block16, pair_specs + [VMEM], pair,
-        scale, bias, d_txt, txt_rows, img_15, txt_emb,
+        text_end_kernel, block16, pair_specs + [VMEM] * 2, 2 * pair,
+        scale, bias, d_txt, txt_rows, other_img, img_15, txt_emb,
     )
     part = parts.reshape(SLABS, *slab)
     parts = exchange(after(jnp.broadcast_to(part[None], (OWNERS, SLABS, 16, 128))), PLANE)

time: 119 us -> 117 us (0.983)
  local copies, waits for them, and re-layouts: 4.24 us -> 2.48 us
    unnamed x14 -> x10, local copies, waits for them, and re-layouts: 4.09 us -> 2.33 us
    pallas_call x11 -> x10, Pallas kernels: 11.6 us -> 12.5 us  [call(): pl.pallas_call(kernel, out_shape=out_shape, in_specs=specs, out_specs=out...]
  transfers between devices with their start and end apart: 11 -> 11, of which waited for: 5 -> 4; matrix products, arithmetic and copies ran while one was open for 1% -> 1% of each run, Pallas kernels for 6% -> 8%
where the time goes in v9:
time: 117 us
  starting transfers between devices  54 us (46%)
  blocking collectives  29.6 us (25%)
  waiting for transfers between devices  14.2 us (12%)
  Pallas kernels  12.5 us (11%)
  local copies, waits for them, and re-layouts  2.48 us (2%)
  between operations  2.17 us (2%)
  matrix products  1.5 us (1%)
    ppermute x9, starting transfers between devices, swap(): return lax.ppermute(value, 'dp', pairs)  35.6 us
    all_to_all x2, blocking collectives, exchange(): lax.all_to_all(value, 'dp', 0, 0, axis_index_groups=members, tiled=True)  29.6 us
    all_to_all x2, starting transfers between devices, exchange(): lax.all_to_all(value, 'dp', 0, 0, axis_index_groups=members, tiled=True)  18.4 us
    pallas_call x10, Pallas kernels, call(): pl.pallas_call(kernel, out_shape=out_shape, in_specs=specs, out_specs=out...  12.5 us
    all_to_all x2, waiting for transfers between devices, exchange(): lax.all_to_all(value, 'dp', 0, 0, axis_index_groups=members, tiled=True)  10.3 us
    ppermute x9, waiting for transfers between devices, swap(): return lax.ppermute(value, 'dp', pairs)  3.96 us
  transfers between devices with their start and end apart: 11, of which 4 were waited for; matrix products, arithmetic and copies ran while one was open for 1% of the time, Pallas kernels for 8%

profile of v9, /device:TPU:1, one launch (start us, length us, event | category | flops | bytes accessed | tf_op | source)
XLA Modules:
  0.0 116.5 jit_solution(11826647925412247190)
XLA Ops:
  0.6 7.1 %collective-permute-start = (bf16[256,640]{1,0:T(8,128)(2,1)}, bf16[256,640]{1,0:T(8,128)(2,1)S(1)}, u32[]{:S(2)}, u32[]{:S(2)}) collective-permute-start(bf16[256,640]{1,0:T(8,128)(2,1)} %txt_ref.3), channel_id=1, source_target_pairs={{0,15},{1,14},{2,13},{3,12},{4,11},{5,10},{6,9},{7,8},{8,7},{9,6},... | collective-permute-start | bytes 983048 | tf_op jit(solution)/shard_map/ppermute | solution.py:32
  7.8 1.9 %collective-permute-start.1 = (bf16[256,640]{1,0:T(8,128)(2,1)}, bf16[256,640]{1,0:T(8,128)(2,1)S(1)}, u32[]{:S(2)}, u32[]{:S(2)}) collective-permute-start(bf16[256,640]{1,0:T(8,128)(2,1)} %txt_ref.3), channel_id=1, source_target_pairs={{0,3},{1,2},{2,1},{3,0},{4,7},{5,6},{6,5},{7,4},{8,11},{9,10},{10,... | collective-permute-start | bytes 983048 | tf_op jit(solution)/shard_map/ppermute | solution.py:32
  9.7 3.6 %collective-permute-start.2 = (bf16[256,640]{1,0:T(8,128)(2,1)}, bf16[256,640]{1,0:T(8,128)(2,1)S(1)}, u32[]{:S(2)}, u32[]{:S(2)}) collective-permute-start(bf16[256,640]{1,0:T(8,128)(2,1)} %txt_ref.3), channel_id=1, source_target_pairs={{0,1},{1,0},{2,3},{3,2},{4,5},{5,4},{6,7},{7,6},{8,9},{9,8},{10,11... | collective-permute-start | bytes 983048 | tf_op jit(solution)/shard_map/ppermute | solution.py:32
  13.3 1.9 %collective-permute-start.3 = (bf16[256,640]{1,0:T(8,128)(2,1)}, bf16[256,640]{1,0:T(8,128)(2,1)S(1)}, u32[]{:S(2)}, u32[]{:S(2)}) collective-permute-start(bf16[256,640]{1,0:T(8,128)(2,1)} %txt_ref.3), channel_id=1, source_target_pairs={{0,7},{1,6},{2,5},{3,4},{4,3},{5,2},{6,1},{7,0},{8,15},{9,14},{10,... | collective-permute-start | bytes 983048 | tf_op jit(solution)/shard_map/ppermute | solution.py:32
  17.7 1.2 %copy-done = bf16[1152,640]{1,0:T(8,128)(2,1)S(1)} copy-done((bf16[1152,640]{1,0:T(8,128)(2,1)S(1)}, bf16[1152,640]{1,0:T(8,128)(2,1)}, u32[]{:S(2)}) %copy-start) | copy-done | bytes 1474584
  19.0 1.5 %shard_map.86 = (f32[256,640]{1,0:T(8,128)S(1)}, f32[256,1]{1,0:T(8,128)S(1)}, bf16[256,640]{1,0:T(8,128)(2,1)S(1)}, f32[256,640]{1,0:T(8,128)S(1)}, f32[256,640...) custom-call(s32[1]{0:T(128)} %bitcast.core_ref, f32[1]{0:T(128)S(6)} %exp.3.scale_ref, f32[1]{0:T(128)S(6)} %copy.10.bias_ref, ...), custom_call_target="tpu_custom_call" | custom-call | flops 2013265920 | bytes 5015564 | tf_op jit(solution)/shard_map/pallas_call | solution.py:55
  20.5 2.5 %shard_map.87.total_ref = f32[256,640]{1,0:T(8,128)S(1)} custom-call(f32[1]{0:T(128)S(6)} %exp.3.scale_ref, f32[1]{0:T(128)S(6)} %copy.10.bias_ref, f32[256,640]{1,0:T(8,128)S(1)} %get-tuple-element.13.total_ref, bf16[256,640]{1,0:T(8,128)(2,1)S(1)} %get-tuple-element.21.rows_ref, bf16[256,640]{1,0:T(8,128)(2,1)S(1)} %collective-permute-done.a_ref, ...), custom_call_target="tpu_custom_call" | custom-call | flops 1677721 | bytes 2621448 | tf_op jit(solution)/shard_map/pallas_call | solution.py:55
  23.0 3.0 %collective-permute-done.3.other_ref = bf16[256,640]{1,0:T(8,128)(2,1)S(1)} collective-permute-done((bf16[256,640]{1,0:T(8,128)(2,1)}, bf16[256,640]{1,0:T(8,128)(2,1)S(1)}, u32[]{:S(2)}, u32[]{:S(2)}) %collective-permute-start.3) | collective-permute-done | bytes 327712 | tf_op jit(solution)/shard_map/ppermute | solution.py:32
  26.9 2.0 %collective-permute-start.4 = (bf16[256,1920]{1,0:T(8,128)(2,1)S(1)}, bf16[256,1920]{1,0:T(8,128)(2,1)S(1)}, u32[]{:S(2)}, u32[]{:S(2)}) collective-permute-start(bf16[256,1920]{1,0:T(8,128)(2,1)S(1)} %shard_map.88.mine_ref), channel_id=1, source_target_pairs={{0,1},{1,0},{2,3},{3,2},{4,5},{5,4},{6,7},{7,6},{8,9},{9,8},{10,11... | collective-permute-start | bytes 2949128 | tf_op jit(solution)/shard_map/ppermute | solution.py:32
  28.8 1.5 %convolution_convert_fusion = bf16[256,1152]{1,0:T(8,128)(2,1)} fusion(bf16[1152,640]{1,0:T(8,128)(2,1)S(1)} %copy-done, bf16[256,1920]{1,0:T(8,128)(2,1)S(1)} %shard_map.88.mine_ref), kind=kOutput, calls=%fused_computation | convolution fusion | flops 377782272 | bytes 2392064 | tf_op jit(solution)/shard_map/dot_general | solution.py:48
  30.3 1.0 collective-permute-done.4.theirs_ref.packed_ref
  31.3 1.6 %shard_map.89 = bf16[16,12,16,128]{3,2,1,0:T(8,128)(2,1)} custom-call(s32[1]{0:T(128)} %bitcast.core_ref, bf16[256,1152]{1,0:T(8,128)(2,1)S(1)} %copy-done.1, bf16[256,1920]{1,0:T(8,128)(2,1)S(1)} %shard_map.88.mine_ref, bf16[256,1920]{1,0:T(8,128)(2,1)S(1)} %collective-permute-done.4.theirs_ref.packed_ref), custom_call_target="tpu_custom_call" | custom-call | flops 377487360 | bytes 3342340 | tf_op jit(solution)/shard_map/pallas_call | solution.py:55
  32.9 3.6 %all-to-all-start = ((bf16[16,12,16,128]{3,2,1,0:T(8,128)(2,1)}), bf16[16,12,16,128]{3,2,1,0:T(8,128)(2,1)S(1)}, u32[]{:S(2)}, u32[]{:S(2)}) async-start(bf16[16,12,16,128]{3,2,1,0:T(8,128)(2,1)} %shard_map.89), calls=%async_computation | async-start | bytes 1572864 | tf_op jit(solution)/shard_map/all_to_all | solution.py:36
  36.6 4.0 %collective-permute-start.5 = (bf16[256,640]{1,0:T(8,128)(2,1)S(1)}, bf16[256,640]{1,0:T(8,128)(2,1)}, u32[]{:S(2)}, u32[]{:S(2)}) collective-permute-start(bf16[256,640]{1,0:T(8,128)(2,1)S(1)} %get-tuple-element.21.rows_ref), channel_id=1, source_target_pairs={{0,3},{1,2},{2,1},{3,0},{4,7},{5,6},{6,5},{7,4},{8,11},{9,10},{10,... | collective-permute-start | bytes 983048 | tf_op jit(solution)/shard_map/ppermute | solution.py:32
  40.6 3.2 %collective-permute-start.6 = (bf16[256,640]{1,0:T(8,128)(2,1)S(1)}, bf16[256,640]{1,0:T(8,128)(2,1)}, u32[]{:S(2)}, u32[]{:S(2)}) collective-permute-start(bf16[256,640]{1,0:T(8,128)(2,1)S(1)} %get-tuple-element.21.rows_ref), channel_id=1, source_target_pairs={{0,7},{1,6},{2,5},{3,4},{4,3},{5,2},{6,1},{7,0},{8,15},{9,14},{10,... | collective-permute-start | bytes 983048 | tf_op jit(solution)/shard_map/ppermute | solution.py:32
  43.7 5.5 %collective-permute-start.7 = (bf16[256,640]{1,0:T(8,128)(2,1)S(1)}, bf16[256,640]{1,0:T(8,128)(2,1)S(1)}, u32[]{:S(2)}, u32[]{:S(2)}) collective-permute-start(bf16[256,640]{1,0:T(8,128)(2,1)S(1)} %get-tuple-element.21.rows_ref), channel_id=1, source_target_pairs={{0,15},{1,14},{2,13},{3,12},{4,11},{5,10},{6,9},{7,8},{8,7},{9,6},... | collective-permute-start | bytes 983048 | tf_op jit(solution)/shard_map/ppermute | solution.py:32
  50.8 14.8 %all-to-all-start.1 = ((bf16[16,16,128]{2,1,0:T(8,128)(2,1)}), bf16[16,16,128]{2,1,0:T(8,128)(2,1)S(1)}, u32[]{:S(2)}, u32[]{:S(2)}) async-start(bf16[16,16,128]{2,1,0:T(8,128)(2,1)} %shard_map.90), calls=%async_computation.1 | async-start | bytes 131072 | tf_op jit(solution)/shard_map/all_to_all | solution.py:36
  65.7 2.1 %shard_map.91.total_ref = f32[256,640]{1,0:T(8,128)S(1)} custom-call(f32[1]{0:T(128)S(6)} %exp.3.scale_ref, f32[1]{0:T(128)S(6)} %copy.10.bias_ref, f32[256,640]{1,0:T(8,128)S(1)} %get-tuple-element.20.total_ref, bf16[256,640]{1,0:T(8,128)(2,1)S(1)} %shard_map.85.txt_ref.rows_ref, bf16[256,640]{1,0:T(8,128)(2,1)} %collective-permute-done.5.a_ref, ...), custom_call_target="tpu_custom_call" | custom-call | flops 335544320 | bytes 2293768 | tf_op jit(solution)/shard_map/pallas_call | solution.py:55
  67.8 9.4 %all-to-all-done.1.parts_ref = bf16[16,16,128]{2,1,0:T(8,128)(2,1)S(1)} async-done(((bf16[16,16,128]{2,1,0:T(8,128)(2,1)}), bf16[16,16,128]{2,1,0:T(8,128)(2,1)S(1)}, u32[]{:S(2)}, u32[]{:S(2)}) %all-to-all-start.1) | async-done | bytes 65568 | tf_op jit(solution)/shard_map/all_to_all | solution.py:36
  77.2 14.4 %all_to_all.20 = bf16[16,16,128]{2,1,0:T(8,128)(2,1)S(1)} all-to-all(bf16[16,16,128]{2,1,0:T(8,128)(2,1)S(1)} %shard_map.93), channel_id=1, replica_groups={{0,8,16,24,32,40,48,56,64,72,80,88,96,104,112,120},{1,9,17,25,33,41,49,..., dimensions={0} | all-to-all | bytes 131072 | tf_op jit(solution)/shard_map/all_to_all | solution.py:36
  91.8 15.2 %all_to_all.21.mine_ref = bf16[16,12,16,128]{3,2,1,0:T(8,128)(2,1)S(1)} all-to-all(bf16[16,12,16,128]{3,2,1,0:T(8,128)(2,1)S(1)} %broadcast_in_dim.14), channel_id=1, replica_groups={{0,2,4,6,128,130,132,134,256,258,260,262,384,386,388,390},{1,3,5,7,129,..., dimensions={0} | all-to-all | bytes 1572864 | tf_op jit(solution)/shard_map/all_to_all | solution.py:36
  107.0 6.4 %collective-permute-start.8 = (bf16[16,12,16,128]{3,2,1,0:T(8,128)(2,1)S(1)}, bf16[16,12,16,128]{3,2,1,0:T(8,128)(2,1)S(1)}, u32[]{:S(2)}, u32[]{:S(2)}) collective-permute-start(bf16[16,12,16,128]{3,2,1,0:T(8,128)(2,1)S(1)} %all_to_all.21.mine_ref), channel_id=1, source_target_pairs={{0,1},{1,0},{2,3},{3,2},{4,5},{5,4},{6,7},{7,6},{8,9},{9,8},{10,11... | collective-permute-start | bytes 2359304 | tf_op jit(solution)/shard_map/ppermute | solution.py:32
  113.4 1.9 %shard_map.92 = bf16[256,640]{1,0:T(8,128)(2,1)} custom-call(f32[1]{0:T(128)S(6)} %exp.3.scale_ref, f32[1]{0:T(128)S(6)} %copy.10.bias_ref, f32[256,640]{1,0:T(8,128)S(1)} %shard_map.91.total_ref, bf16[256,640]{1,0:T(8,128)(2,1)S(1)} %shard_map.85.txt_ref.rows_ref, bf16[256,1920]{1,0:T(8,128)(2,1)S(1)} %collective-permute-done.4.theirs_ref.packed_ref, ...), custom_call_target="tpu_custom_call" | custom-call | flops 335544320 | bytes 2949128 | tf_op jit(solution)/shard_map/pallas_call | solution.py:55
  115.3 1.2 %shard_map.94 = bf16[1152,640]{1,0:T(8,128)(2,1)} custom-call(s32[1]{0:T(128)} %bitcast.core_ref, bf16[16,12,16,128]{3,2,1,0:T(8,128)(2,1)S(1)} %all_to_all.21.mine_ref, bf16[16,12,16,128]{3,2,1,0:T(8,128)(2,1)S(1)} %collective-permute-done.8.theirs_ref), custom_call_target="tpu_custom_call" | custom-call | bytes 3047428 | tf_op jit(solution)/shard_map/pallas_call | solution.py:55
  (23 shorter events, 3.9 us)
Async XLA Ops:
  0.6 19.9 %collective-permute-start = (bf16[256,640]{1,0:T(8,128)(2,1)}, bf16[256,640]{1,0:T(8,128)(2,1)S(1)}, u32[]{:S(2)}, u32[]{:S(2)}) collective-permute-start(bf16[256,640]{1,0:T(8,128)(2,1)} %txt_ref.3), channel_id=1, source_target_pairs={{0,15},{1,14},{2,13},{3,12},{4,11},{5,10},{6,9},{7,8},{8,7},{9,6},... | collective-permute-start | bytes 983048 | tf_op jit(solution)/shard_map/ppermute | solution.py:32
  7.8 12.7 %collective-permute-start.1 = (bf16[256,640]{1,0:T(8,128)(2,1)}, bf16[256,640]{1,0:T(8,128)(2,1)S(1)}, u32[]{:S(2)}, u32[]{:S(2)}) collective-permute-start(bf16[256,640]{1,0:T(8,128)(2,1)} %txt_ref.3), channel_id=1, source_target_pairs={{0,3},{1,2},{2,1},{3,0},{4,7},{5,6},{6,5},{7,4},{8,11},{9,10},{10,... | collective-permute-start | bytes 983048 | tf_op jit(solution)/shard_map/ppermute | solution.py:32
  9.7 10.8 %collective-permute-start.2 = (bf16[256,640]{1,0:T(8,128)(2,1)}, bf16[256,640]{1,0:T(8,128)(2,1)S(1)}, u32[]{:S(2)}, u32[]{:S(2)}) collective-permute-start(bf16[256,640]{1,0:T(8,128)(2,1)} %txt_ref.3), channel_id=1, source_target_pairs={{0,1},{1,0},{2,3},{3,2},{4,5},{5,4},{6,7},{7,6},{8,9},{9,8},{10,11... | collective-permute-start | bytes 983048 | tf_op jit(solution)/shard_map/ppermute | solution.py:32
  13.3 12.7 %collective-permute-start.3 = (bf16[256,640]{1,0:T(8,128)(2,1)}, bf16[256,640]{1,0:T(8,128)(2,1)S(1)}, u32[]{:S(2)}, u32[]{:S(2)}) collective-permute-start(bf16[256,640]{1,0:T(8,128)(2,1)} %txt_ref.3), channel_id=1, source_target_pairs={{0,7},{1,6},{2,5},{3,4},{4,3},{5,2},{6,1},{7,0},{8,15},{9,14},{10,... | collective-permute-start | bytes 983048 | tf_op jit(solution)/shard_map/ppermute | solution.py:32
  16.6 1.0 copy-start.2
  17.5 1.4 %copy-start = (bf16[1152,640]{1,0:T(8,128)(2,1)S(1)}, bf16[1152,640]{1,0:T(8,128)(2,1)}, u32[]{:S(2)}) copy-start(bf16[1152,640]{1,0:T(8,128)(2,1)} %head_ref.1) | copy-start | bytes 4423684
  17.5 1.5 %copy-start.1 = (bf16[256,1152]{1,0:T(8,128)(2,1)S(1)}, bf16[256,1152]{1,0:T(8,128)(2,1)}, u32[]{:S(2)}) copy-start(bf16[256,1152]{1,0:T(8,128)(2,1)} %feat_ref.3) | copy-start | bytes 1769476
  17.5 1.5 %copy-start.4 = (s32[256]{0:T(256)S(1)}, s32[256]{0:T(256)}, u32[]{:S(2)}) copy-start(s32[256]{0:T(256)} %param.9) | copy-start | bytes 3076
  26.9 4.5 %collective-permute-start.4 = (bf16[256,1920]{1,0:T(8,128)(2,1)S(1)}, bf16[256,1920]{1,0:T(8,128)(2,1)S(1)}, u32[]{:S(2)}, u32[]{:S(2)}) collective-permute-start(bf16[256,1920]{1,0:T(8,128)(2,1)S(1)} %shard_map.88.mine_ref), channel_id=1, source_target_pairs={{0,1},{1,0},{2,3},{3,2},{4,5},{5,4},{6,7},{7,6},{8,9},{9,8},{10,11... | collective-permute-start | bytes 2949128 | tf_op jit(solution)/shard_map/ppermute | solution.py:32
  32.9 17.2 %all-to-all-start = ((bf16[16,12,16,128]{3,2,1,0:T(8,128)(2,1)}), bf16[16,12,16,128]{3,2,1,0:T(8,128)(2,1)S(1)}, u32[]{:S(2)}, u32[]{:S(2)}) async-start(bf16[16,12,16,128]{3,2,1,0:T(8,128)(2,1)} %shard_map.89), calls=%async_computation | async-start | bytes 1572864 | tf_op jit(solution)/shard_map/all_to_all | solution.py:36
  36.6 29.1 %collective-permute-start.5 = (bf16[256,640]{1,0:T(8,128)(2,1)S(1)}, bf16[256,640]{1,0:T(8,128)(2,1)}, u32[]{:S(2)}, u32[]{:S(2)}) collective-permute-start(bf16[256,640]{1,0:T(8,128)(2,1)S(1)} %get-tuple-element.21.rows_ref), channel_id=1, source_target_pairs={{0,3},{1,2},{2,1},{3,0},{4,7},{5,6},{6,5},{7,4},{8,11},{9,10},{10,... | collective-permute-start | bytes 983048 | tf_op jit(solution)/shard_map/ppermute | solution.py:32
  40.6 25.1 %collective-permute-start.6 = (bf16[256,640]{1,0:T(8,128)(2,1)S(1)}, bf16[256,640]{1,0:T(8,128)(2,1)}, u32[]{:S(2)}, u32[]{:S(2)}) collective-permute-start(bf16[256,640]{1,0:T(8,128)(2,1)S(1)} %get-tuple-element.21.rows_ref), channel_id=1, source_target_pairs={{0,7},{1,6},{2,5},{3,4},{4,3},{5,2},{6,1},{7,0},{8,15},{9,14},{10,... | collective-permute-start | bytes 983048 | tf_op jit(solution)/shard_map/ppermute | solution.py:32
  43.7 24.0 %collective-permute-start.7 = (bf16[256,640]{1,0:T(8,128)(2,1)S(1)}, bf16[256,640]{1,0:T(8,128)(2,1)S(1)}, u32[]{:S(2)}, u32[]{:S(2)}) collective-permute-start(bf16[256,640]{1,0:T(8,128)(2,1)S(1)} %get-tuple-element.21.rows_ref), channel_id=1, source_target_pairs={{0,15},{1,14},{2,13},{3,12},{4,11},{5,10},{6,9},{7,8},{8,7},{9,6},... | collective-permute-start | bytes 983048 | tf_op jit(solution)/shard_map/ppermute | solution.py:32
  50.8 26.4 %all-to-all-start.1 = ((bf16[16,16,128]{2,1,0:T(8,128)(2,1)}), bf16[16,16,128]{2,1,0:T(8,128)(2,1)S(1)}, u32[]{:S(2)}, u32[]{:S(2)}) async-start(bf16[16,16,128]{2,1,0:T(8,128)(2,1)} %shard_map.90), calls=%async_computation.1 | async-start | bytes 131072 | tf_op jit(solution)/shard_map/all_to_all | solution.py:36
  67.7 45.7 %copy-start.3 = (bf16[256,640]{1,0:T(8,128)(2,1)S(1)}, bf16[256,640]{1,0:T(8,128)(2,1)}, u32[]{:S(2)}) copy-start(bf16[256,640]{1,0:T(8,128)(2,1)} %txt_ref.3) | copy-start | bytes 983044
  107.0 8.3 %collective-permute-start.8 = (bf16[16,12,16,128]{3,2,1,0:T(8,128)(2,1)S(1)}, bf16[16,12,16,128]{3,2,1,0:T(8,128)(2,1)S(1)}, u32[]{:S(2)}, u32[]{:S(2)}) collective-permute-start(bf16[16,12,16,128]{3,2,1,0:T(8,128)(2,1)S(1)} %all_to_all.21.mine_ref), channel_id=1, source_target_pairs={{0,1},{1,0},{2,3},{3,2},{4,5},{5,4},{6,7},{7,6},{8,9},{9,8},{10,11... | collective-permute-start | bytes 2359304 | tf_op jit(solution)/shard_map/ppermute | solution.py:32
